TPU v7x, 768 devices: a whole 4x8x12 slice. The times are simulated.
768 devices in a mesh: dp: 96 (over z, y), mp: 8 (over x, core).
Axes of the slice: x: 4, y: 8, z: 12, core: 2. Of those that a mesh axis runs over, the one named last changes fastest.
Arguments:
- grad_proj: bfloat16 [12288, 12800], P(('dp', 'mp')), may hold values from -6 to 6
- tile_counts: int32 [96, 1], P('dp'), may hold values from 1 to 8, as said below
- tile_home: int32 [96, 8], P('dp'), may hold values from 0 to 7, each once within a row
- saved_feat: bfloat16 [12288, 12800], P(('dp', 'mp')), may hold values from -6 to 6
- ln_gain: float32 [12800], replicated, may hold values from 0.1 to 1.9
- layer_scale: float32 [3200], replicated, may hold values from 0.2 to 2
- attn_saved: bfloat16 [49152, 1664], P('dp', 'mp'), may hold values from -6 to 6
- proj_weight: bfloat16 [3200, 1664], P(None, 'mp'), may hold values from -0.109375 to 0.109375
Outputs:
- residual_grad: bfloat16 [49152, 3200], P(('dp', 'mp'))
- attn_grad: bfloat16 [49152, 1664], P('dp', 'mp')
- proj_grad: float32 [3264, 1664], P('dp', 'mp')
- gain_grad: float32 [12800], replicated
Inputs may be any that keep to these rules, and one draw needn't show every extreme that they name: `tile_counts`: tiles of each sample; in every draw some vision group has its sample at 8 tiles. `tile_home`: each row names every vision slot of its group once.
All inputs are finite; a program needn't handle non-finite values.
Results may differ from a plain program's by a relative error of at most 0.0049.
Values may be sent and summed in bfloat16 or wider, within the bound.
No kernel may reach another device: no remote copies, remote signals or barrier semaphores. Data moves between devices by JAX's collectives and lax.ppermute only.
A program may use at most 32 MiB of HBM per device.

v0:
```python
import jax
import jax.numpy as jnp
from jax import lax
from jax.sharding import PartitionSpec as P

VW = 3200
TILE_SIDE = 8


EPSILON = 1e-05


def layer_norm_back(upstream, features, ln_gain):
    values = features.astype(jnp.float32)
    centered = values - jnp.mean(values, axis=-1, keepdims=True)
    inverse_std = lax.rsqrt(jnp.mean(centered * centered, axis=-1, keepdims=True) + EPSILON)
    normed = centered * inverse_std
    scaled = upstream * ln_gain
    first_mean = jnp.mean(scaled, axis=-1, keepdims=True)
    second_mean = jnp.mean(scaled * normed, axis=-1, keepdims=True)
    return (inverse_std * (scaled - first_mean - normed * second_mean), normed)


def unshuffle(rows, tiles, tile_side):
    half_side = tile_side // 2
    blocks = rows.reshape(tiles, half_side, half_side, 2, 2, VW)
    blocks = jnp.transpose(blocks, (0, 1, 3, 2, 4, 5))
    return blocks.reshape(tiles * tile_side * tile_side, VW)


def body(
    grad_proj, tile_counts, tile_home, saved_feat, ln_gain, layer_scale, attn_saved, proj_weight
):
    mp_count = lax.axis_size("mp")
    dp_count = lax.axis_size("dp")
    mp_index = lax.axis_index("mp")
    capacity = tile_home.shape[1]
    rows_dev = grad_proj.shape[0]
    tiles_dev = capacity // mp_count
    tile_rows = rows_dev // tiles_dev
    live_total = jnp.sum(tile_counts)
    slot_ids = mp_index * tiles_dev + jnp.arange(tiles_dev, dtype=jnp.int32)
    matches = tile_home[0][None, :] == slot_ids[:, None]
    packed_ids = jnp.arange(capacity, dtype=jnp.int32)[None, :]
    source_tile = jnp.sum(jnp.where(matches, packed_ids, jnp.zeros_like(packed_ids)), axis=1)
    row_tile = jnp.repeat(source_tile, tile_rows)
    wanted = row_tile * tile_rows + jnp.tile(jnp.arange(tile_rows, dtype=jnp.int32), tiles_dev)
    row_live = row_tile < live_total
    pieces = lax.all_gather(grad_proj, "mp", axis=0, tiled=True)
    columns = jnp.arange(pieces.shape[0], dtype=jnp.int32)
    select = ((wanted[:, None] == columns[None, :]) & row_live[:, None]).astype(jnp.bfloat16)
    upstream = jnp.dot(select, pieces, preferred_element_type=jnp.float32)
    grad_input, normed = layer_norm_back(upstream, saved_feat, ln_gain)
    gain_local = jnp.sum(upstream * normed, axis=0)
    vit_grad = unshuffle(grad_input, tiles_dev, TILE_SIDE)
    residual_grad = vit_grad.astype(jnp.bfloat16)
    branch = (vit_grad * layer_scale).astype(jnp.bfloat16)
    padded_rows = -(-VW // dp_count) * dp_count
    pieces = lax.all_gather(branch, "mp", axis=0, tiled=True)
    local_grad = jnp.dot(pieces, proj_weight, preferred_element_type=jnp.float32)
    weight_part = lax.dot_general(
        pieces, attn_saved, (((0,), (0,)), ((), ())), preferred_element_type=jnp.float32
    )
    padded = jnp.pad(weight_part, ((0, padded_rows - VW), (0, 0)))
    proj_grad = lax.psum_scatter(padded, "dp", scatter_dimension=0, tiled=True)
    gain_grad = lax.psum(gain_local, ("dp", "mp"))
    return (residual_grad, local_grad.astype(jnp.bfloat16), proj_grad, gain_grad)


def solution(mesh):
    in_specs = (
        P(("dp", "mp"), None),
        P("dp", None),
        P("dp", None),
        P(("dp", "mp"), None),
        P(),
        P(),
        P("dp", "mp"),
        P(None, "mp"),
    )
    out_specs = (P(("dp", "mp"), None), P("dp", "mp"), P("dp", "mp"), P())
    return jax.shard_map(body, mesh=mesh, in_specs=in_specs, out_specs=out_specs, check_vma=False)
```

profile of v0, /device:TPU:6, one launch (start us, length us, event | category | flops | bytes accessed | tf_op | source)
XLA Modules:
  0.0 353.6 jit_solution(15570724324542115122)
XLA Ops:
  7.2 0.0 copy-start
  7.2 0.0 copy-start.1
  7.2 0.0 copy-start.2
  7.2 0.0 all-gather.3.cloned.1.call-start
  7.2 0.7 all-gather.3.cloned.1.call-update
  7.9 0.0 all-gather.5.cloned.1.call-start
  8.6 1.3 fusion.15
  11.2 1.2 convert_reduce_fusion
  12.5 1.3 fusion.9
  13.8 38.5 %all-gather.3.cloned.1.call-done = bf16[128,12800]{1,0:T(8,128)(2,1)} async-done(((bf16[16,12800]{1,0:T(8,128)(2,1)}), bf16[128,12800]{1,0:T(8,128)(2,1)}) %all-gather.3.cloned.1.call-update) | async-done | bytes 3276816 | tf_op jit(solution)/shard_map/all_gather | solution.py:49
  52.3 2.8 fusion.8
  55.1 0.0 copy-done.1
  55.1 0.0 copy-done.2
  55.1 0.0 copy-start.4
  55.1 0.3 fusion.7
  55.4 0.0 copy-start.3
  55.4 0.6 reshape.48
  56.0 0.1 copy.14
  56.0 0.6 reshape.49
  56.6 0.0 copy-done.4
  56.6 1.0 multiply_convert_fusion
  57.6 0.0 all-gather.5.cloned.1.call-update
  57.6 0.0 all-reduce.4.cloned.1.call-start
  57.6 36.4 %all-gather.5.cloned.1.call-done = bf16[512,3200]{1,0:T(8,128)(2,1)} async-done(((bf16[64,3200]{1,0:T(8,128)(2,1)}), bf16[512,3200]{1,0:T(8,128)(2,1)}) %all-gather.5.cloned.1.call-update) | async-done | bytes 3276816 | tf_op jit(solution)/shard_map/all_gather | solution.py:59
  94.1 0.0 copy-done.3
  94.1 2.8 fusion.16
  96.9 1.8 pad.4
  98.7 0.0 all-reduce.4.cloned.1.call-update
  98.7 1.3 dynamic-slice
  100.6 112.0 %psum.7 = f32[12800]{0:T(1024)} all-reduce(f32[12800]{0:T(1024)S(1)} %get-tuple-element.12), channel_id=1, replica_groups=mesh['dp'=96,'mp'=8] {'dp','mp'}, use_global_device_ids=true, to_apply=%region_7.8 | all-reduce | flops 12800 | bytes 102400 | tf_op jit(solution)/shard_map/psum | solution.py:66
  212.6 0.0 copy-done
  212.6 3.8 %convolution_convert_fusion = bf16[512,208]{0,1:T(8,128)(2,1)} fusion(bf16[512,3200]{1,0:T(8,128)(2,1)} %all-gather.5.cloned.1.call-done, bf16[3200,208]{0,1:T(8,128)(2,1)S(1)} %copy-done), kind=kOutput, calls=%fused_computation | convolution fusion | flops 681680896 | bytes 4820992 | tf_op jit(solution)/shard_map/dot_general | solution.py:60
  216.4 128.9 %all-reduce.4.cloned.1.call-done = f32[3264,208]{0,1:T(8,128)} async-done(((f32[3264,208]{0,1:T(8,128)}), f32[3264,208]{0,1:T(8,128)}) %all-reduce.4.cloned.1.call-update) | async-done | bytes 2715664
  345.3 1.0 constant_dynamic-slice_fusion
  346.3 0.7 copy.15
  (4 shorter events, 0.0 us)
Async XLA Ops:
  7.2 205.4 %copy-start = (bf16[3200,208]{0,1:T(8,128)(2,1)S(1)}, bf16[3200,208]{0,1:T(8,128)(2,1)}, u32[]{:S(2)}) copy-start(bf16[3200,208]{0,1:T(8,128)(2,1)} %param.15) | copy-start | bytes 3993604
  7.2 47.9 %copy-start.1 = (bf16[16,12800]{1,0:T(8,128)(2,1)S(1)}, bf16[16,12800]{1,0:T(8,128)(2,1)}, u32[]{:S(2)}) copy-start(bf16[16,12800]{1,0:T(8,128)(2,1)} %param.11) | copy-start | bytes 1228804
  7.2 47.9 %copy-start.2 = (f32[12800]{0:T(1024)S(1)}, f32[12800]{0:T(1024)}, u32[]{:S(2)}) copy-start(f32[12800]{0:T(1024)} %param.12) | copy-start | bytes 153604
  7.2 45.0 %all-gather.3.cloned.1.call-start = ((), (), s32[]{:S(2)}) async-start(), calls=%async_computation | async-start | bytes 3686400 | tf_op jit(solution)/shard_map/all_gather | solution.py:49
  7.9 86.1 %all-gather.5.cloned.1.call-start = ((), (), s32[]{:S(2)}) async-start(), calls=%async_computation.1 | async-start | bytes 3686400 | tf_op jit(solution)/shard_map/all_gather | solution.py:59
  55.1 1.5 copy-start.4
  55.4 38.7 %copy-start.3 = (bf16[512,208]{0,1:T(8,128)(2,1)S(1)}, bf16[512,208]{0,1:T(8,128)(2,1)}, u32[]{:S(2)}) copy-start(bf16[512,208]{0,1:T(8,128)(2,1)} %param.14) | copy-start | bytes 638980
  57.6 287.7 %all-reduce.4.cloned.1.call-start = ((), (), s32[]{:S(2)}) async-start(), calls=%async_computation.2 | async-start | bytes 5537792
Sparse Core Ops, SparseCore 0:
  10.5 41.7 all-gather.2
  57.7 36.3 all-gather.4
  98.8 246.4 all-reduce.3
where the time goes:
time: 354 us
  waiting for transfers between devices  205 us (58%)
  blocking collectives  112 us (32%)
  between operations  16.5 us (5%)
  matrix products  9.39 us (3%)
  local copies, waits for them, and re-layouts  5.98 us (2%)
  other arithmetic  5.07 us (1%)
    unnamed x4, waiting for transfers between devices  130 us
    psum x1, blocking collectives, body(): gain_grad = lax.psum(gain_local, ('dp', 'mp'))  112 us
    all_gather x1, waiting for transfers between devices, body(): pieces = lax.all_gather(grad_proj, 'mp', axis=0, tiled=True)  38.5 us
    all_gather x1, waiting for transfers between devices, body(): pieces = lax.all_gather(branch, 'mp', axis=0, tiled=True)  36.4 us
  transfers between devices with their start and end apart: 3, of which 3 were waited for; matrix products, arithmetic and copies ran while one was open for 3% of the time, Pallas kernels for 0%

commit v1 on v0

--- a/solution.py
+++ b/solution.py
@@ -1,13 +1,14 @@
 import jax
 import jax.numpy as jnp
 from jax import lax
+from jax.sharding import Mesh
 from jax.sharding import PartitionSpec as P
 
 VW = 3200
 TILE_SIDE = 8
-
-
 EPSILON = 1e-05
+DP = ("z", "y")
+MP = ("x", "c")
 
 
 def layer_norm_back(upstream, features, ln_gain):
@@ -28,12 +29,20 @@
     return blocks.reshape(tiles * tile_side * tile_side, VW)
 
 
+def sum_everywhere(part, axis):
+    count = lax.axis_size(axis)
+    terms = jnp.broadcast_to(part[None], (count,) + part.shape)
+    return jnp.sum(lax.all_to_all(terms, axis, 0, 0), axis=0)
+
+
 def body(
     grad_proj, tile_counts, tile_home, saved_feat, ln_gain, layer_scale, attn_saved, proj_weight
 ):
-    mp_count = lax.axis_size("mp")
-    dp_count = lax.axis_size("dp")
-    mp_index = lax.axis_index("mp")
+    mp_count = lax.axis_size("x") * lax.axis_size("c")
+    z_count = lax.axis_size("z")
+    y_count = lax.axis_size("y")
+    dp_count = z_count * y_count
+    mp_index = lax.axis_index(MP)
     capacity = tile_home.shape[1]
     rows_dev = grad_proj.shape[0]
     tiles_dev = capacity // mp_count
@@ -46,7 +55,7 @@
     row_tile = jnp.repeat(source_tile, tile_rows)
     wanted = row_tile * tile_rows + jnp.tile(jnp.arange(tile_rows, dtype=jnp.int32), tiles_dev)
     row_live = row_tile < live_total
-    pieces = lax.all_gather(grad_proj, "mp", axis=0, tiled=True)
+    pieces = lax.all_gather(grad_proj, MP, axis=0, tiled=True)
     columns = jnp.arange(pieces.shape[0], dtype=jnp.int32)
     select = ((wanted[:, None] == columns[None, :]) & row_live[:, None]).astype(jnp.bfloat16)
     upstream = jnp.dot(select, pieces, preferred_element_type=jnp.float32)
@@ -55,28 +64,42 @@
     vit_grad = unshuffle(grad_input, tiles_dev, TILE_SIDE)
     residual_grad = vit_grad.astype(jnp.bfloat16)
     branch = (vit_grad * layer_scale).astype(jnp.bfloat16)
-    padded_rows = -(-VW // dp_count) * dp_count
-    pieces = lax.all_gather(branch, "mp", axis=0, tiled=True)
+    pieces = lax.all_gather(branch, MP, axis=0, tiled=True)
+
+    gain_part = gain_local.reshape(mp_count, -1)
+    gain_part = jnp.sum(lax.all_to_all(gain_part, MP, 0, 0), axis=0)
+    gain_part = sum_everywhere(gain_part, "y")
+    gain_part = sum_everywhere(gain_part, "z")
+    terms = jnp.broadcast_to(gain_part[None], (mp_count,) + gain_part.shape)
+    gain_grad = lax.all_to_all(terms, MP, 0, 0).reshape(-1)
+
     local_grad = jnp.dot(pieces, proj_weight, preferred_element_type=jnp.float32)
     weight_part = lax.dot_general(
         pieces, attn_saved, (((0,), (0,)), ((), ())), preferred_element_type=jnp.float32
     )
-    padded = jnp.pad(weight_part, ((0, padded_rows - VW), (0, 0)))
-    proj_grad = lax.psum_scatter(padded, "dp", scatter_dimension=0, tiled=True)
-    gain_grad = lax.psum(gain_local, ("dp", "mp"))
+    block = -(-VW // dp_count)
+    cols = weight_part.shape[1]
+    padded = jnp.pad(weight_part, ((0, block * dp_count - VW), (0, 0))).astype(jnp.bfloat16)
+    terms = padded.reshape(z_count, y_count, block, cols).transpose(1, 0, 2, 3)
+    terms = lax.all_to_all(terms.reshape(y_count, z_count * block, cols), "y", 0, 0)
+    part = jnp.sum(terms.astype(jnp.float32), axis=0).astype(jnp.bfloat16)
+    terms = lax.all_to_all(part.reshape(z_count, block, cols), "z", 0, 0)
+    proj_grad = jnp.sum(terms.astype(jnp.float32), axis=0)
     return (residual_grad, local_grad.astype(jnp.bfloat16), proj_grad, gain_grad)
 
 
 def solution(mesh):
+    shape = (12, 8, 4, 2)
+    fine = Mesh(mesh.devices.reshape(shape), DP + MP)
     in_specs = (
-        P(("dp", "mp"), None),
-        P("dp", None),
-        P("dp", None),
-        P(("dp", "mp"), None),
+        P(DP + MP, None),
+        P(DP, None),
+        P(DP, None),
+        P(DP + MP, None),
         P(),
         P(),
-        P("dp", "mp"),
-        P(None, "mp"),
+        P(DP, MP),
+        P(None, MP),
     )
-    out_specs = (P(("dp", "mp"), None), P("dp", "mp"), P("dp", "mp"), P())
-    return jax.shard_map(body, mesh=mesh, in_specs=in_specs, out_specs=out_specs, check_vma=False)
+    out_specs = (P(DP + MP, None), P(DP, MP), P(DP, MP), P())
+    return jax.shard_map(body, mesh=fine, in_specs=in_specs, out_specs=out_specs, check_vma=False)

time: 354 us -> 201 us (0.57)
  the two profiles are of different devices: /device:TPU:6 before, /device:TPU:65 now
where the time goes in v1:
time: 201 us
  waiting for transfers between devices  99.6 us (50%)
  starting transfers between devices  32.6 us (16%)
  blocking collectives  21.1 us (10%)
  between operations  16.1 us (8%)
  local copies, waits for them, and re-layouts  15.4 us (8%)
  matrix products  9.39 us (5%)
  other arithmetic  6.39 us (3%)
    all_to_all x1, waiting for transfers between devices, body(): lax.all_to_all(terms.reshape(y_count, z_count * block, cols), 'y', 0, 0)  40 us
    all_gather x1, waiting for transfers between devices, body(): pieces = lax.all_gather(grad_proj, MP, axis=0, tiled=True)  39.4 us
    all_to_all x1, blocking collectives, sum_everywhere(): return jnp.sum(lax.all_to_all(terms, axis, 0, 0), axis=0)  13.4 us
    all_to_all x1, waiting for transfers between devices, body(): terms = lax.all_to_all(part.reshape(z_count, block, cols), 'z', 0, 0)  11.2 us
    all_to_all x1, starting transfers between devices, body(): terms = lax.all_to_all(part.reshape(z_count, block, cols), 'z', 0, 0)  9.97 us
    all_to_all x1, starting transfers between devices, sum_everywhere(): return jnp.sum(lax.all_to_all(terms, axis, 0, 0), axis=0)  9.97 us
    all_to_all x1, blocking collectives, body(): gain_part = jnp.sum(lax.all_to_all(gain_part, MP, 0, 0), axis=0)  7.74 us
    all_to_all x1, starting transfers between devices, body(): lax.all_to_all(terms.reshape(y_count, z_count * block, cols), 'y', 0, 0)  6.45 us
  transfers between devices with their start and end apart: 6, of which 5 were waited for; matrix products, arithmetic and copies ran while one was open for 11% of the time, Pallas kernels for 0%

profile of v1, /device:TPU:65, one launch (start us, length us, event | category | flops | bytes accessed | tf_op | source)
XLA Modules:
  0.0 200.7 jit_solution(14274430995775996128)
XLA Ops:
  7.2 0.0 copy-start
  7.2 0.0 all-gather.3.cloned.1.call-start
  7.2 0.7 all-gather.3.cloned.1.call-update
  7.9 0.0 all-gather.5.cloned.1.call-start
  8.6 1.3 fusion.15
  11.2 0.0 copy-start.1
  11.2 0.0 copy-start.3
  11.2 1.3 convert_reduce_fusion
  12.5 1.3 fusion.9
  13.8 39.4 %all-gather.3.cloned.1.call-done = bf16[128,12800]{1,0:T(8,128)(2,1)} async-done(((bf16[16,12800]{1,0:T(8,128)(2,1)}), bf16[128,12800]{1,0:T(8,128)(2,1)}) %all-gather.3.cloned.1.call-update) | async-done | bytes 3276816 | tf_op jit(solution)/shard_map/all_gather | solution.py:58
  53.2 2.8 %fusion.8 = (f32[12800]{0:T(1024)S(1)}, f32[16]{0:T(128)S(1)}, f32[16]{0:T(128)S(1)}, f32[16,12800]{1,0:T(8,128)S(1)}) fusion(bf16[16,12800]{1,0:T(8,128)(2,1)} %param.11, f32[16]{0:T(128)S(1)} %add_rsqrt_fusion, f32[16]{0:T(128)S(1)} %broadcast_multiply_fusion.2, f32[12800]{0:T(1024)} %param.12, bf16[128,12800]{1,0:T(8,128)(2,1)} %all-gather.3.cloned.1.call-done, ...), kind=kOutput, calls=%fused_computation.12 | convolution fusion | flops 54263264 | bytes 4608321 | tf_op jit(solution)/shard_map/dot_general | solution.py:61
  56.1 0.0 copy-done.1
  56.1 0.0 copy-done.3
  56.1 0.3 fusion.7
  56.4 0.0 copy-start.4
  56.4 0.5 reshape.83
  56.9 1.0 copy.24
  57.9 1.7 reshape.84
  59.6 0.0 copy-done.4
  59.6 1.0 multiply_convert_fusion
  60.6 0.0 all-gather.5.cloned.1.call-update
  60.6 0.1 all_to_all.26
  60.7 7.7 %all_to_all.37 = f32[8,1,1600]{2,1,0:T(1,128)S(1)} all-to-all(f32[8,1,1600]{2,1,0:T(1,128)S(1)} %all_to_all.26), channel_id=1, replica_groups=mesh['z'=12,'y'=8,'x'=4,'c'=2] {'x','c'}, dimensions={0} | all-to-all | bytes 102400 | tf_op jit(solution)/shard_map/all_to_all | solution.py:70
  68.6 13.4 %all_to_all.38 = f32[8,1,1600]{2,1,0:T(1,128)S(1)} all-to-all(f32[8,1,1600]{2,1,0:T(1,128)S(1)} %broadcast_in_dim.6), channel_id=1, replica_groups=mesh['z'=12,'y'=8,'x'=4,'c'=2] {'y'}, dimensions={0} | all-to-all | bytes 102400 | tf_op jit(solution)/shard_map/all_to_all | solution.py:35
  82.0 0.7 broadcast_in_dim.7
  82.6 10.0 %all-to-all-start.4 = ((f32[12,1,1600]{2,1,0:T(1,128)}), f32[12,1,1600]{2,1,0:T(1,128)S(1)}, u32[]{:S(2)}, u32[]{:S(2)}) async-start(f32[12,1,1600]{2,1,0:T(1,128)} %broadcast_in_dim.7), calls=%async_computation.4 | async-start | bytes 159744 | tf_op jit(solution)/shard_map/all_to_all | solution.py:35
  92.6 4.5 %all-gather.5.cloned.1.call-done = bf16[512,3200]{1,0:T(8,128)(2,1)} async-done(((bf16[64,3200]{1,0:T(8,128)(2,1)}), bf16[512,3200]{1,0:T(8,128)(2,1)}) %all-gather.5.cloned.1.call-update) | async-done | bytes 3276816 | tf_op jit(solution)/shard_map/all_gather | solution.py:67
  97.1 2.8 %convolution_convert_fusion = bf16[3200,208]{0,1:T(8,128)(2,1)S(1)} fusion(bf16[512,208]{0,1:T(8,128)(2,1)S(1)} %copy-done.2, bf16[512,3200]{1,0:T(8,128)(2,1)} %all-gather.5.cloned.1.call-done), kind=kOutput, calls=%fused_computation | convolution fusion | flops 682240000 | bytes 4820992 | tf_op jit(solution)/shard_map/dot_general | solution.py:77
  100.0 1.7 copy.32
  101.7 2.9 %pad.5.clone = bf16[3264,208]{1,0:T(8,128)(2,1)} pad(bf16[3200,208]{1,0:T(8,128)(2,1)} %copy.32, bf16[]{:T(256)} %constant.28.clone.1), padding=0_64x0_0 | pad | bytes 2689026 | tf_op jit(solution)/shard_map/jit(_pad)/pad | solution.py:82
  104.5 2.7 %reshape.85 = bf16[12,8,34,208]{3,2,1,0:T(8,128)(2,1)S(1)} reshape(bf16[3264,208]{1,0:T(8,128)(2,1)} %pad.5.clone) | data formatting | bytes 2715648 | tf_op jit(solution)/shard_map/reshape | solution.py:83
  107.3 0.4 copy.26
  107.7 1.5 copy.27
  109.2 0.0 all-to-all-done.4
  109.2 6.5 %all-to-all-start = ((bf16[8,408,208]{2,1,0:T(8,128)(2,1)}), bf16[8,408,208]{2,1,0:T(8,128)(2,1)S(1)}, u32[]{:S(2)}, u32[]{:S(2)}) async-start(bf16[8,408,208]{2,1,0:T(8,128)(2,1)} %copy.27), calls=%async_computation | async-start | bytes 3342336 | tf_op jit(solution)/shard_map/all_to_all | solution.py:84
  115.6 0.1 reduce_sum.119
  115.7 40.0 %all-to-all-done = bf16[8,408,208]{2,1,0:T(8,128)(2,1)S(1)} async-done(((bf16[8,408,208]{2,1,0:T(8,128)(2,1)}), bf16[8,408,208]{2,1,0:T(8,128)(2,1)S(1)}, u32[]{:S(2)}, u32[]{:S(2)}) %all-to-all-start) | async-done | bytes 1357856 | tf_op jit(solution)/shard_map/all_to_all | solution.py:84
  155.7 0.6 broadcast_in_dim.8
  156.4 6.2 %all-to-all-start.5 = ((f32[8,1,1600]{2,1,0:T(1,128)}), f32[8,1,1600]{2,1,0:T(1,128)S(1)}, u32[]{:S(2)}, u32[]{:S(2)}) async-start(f32[8,1,1600]{2,1,0:T(1,128)} %broadcast_in_dim.8), calls=%async_computation.5 | async-start | bytes 106496 | tf_op jit(solution)/shard_map/all_to_all | solution.py:74
  162.6 0.3 reduce_sum.114
  162.9 0.8 reshape.87
  163.7 3.7 %all-to-all-done.5 = f32[8,1,1600]{2,1,0:T(1,128)S(1)} async-done(((f32[8,1,1600]{2,1,0:T(1,128)}), f32[8,1,1600]{2,1,0:T(1,128)S(1)}, u32[]{:S(2)}, u32[]{:S(2)}) %all-to-all-start.5) | async-done | bytes 51232 | tf_op jit(solution)/shard_map/all_to_all | solution.py:74
  167.4 10.0 %all-to-all-start.1 = ((bf16[12,34,208]{2,1,0:T(8,128)(2,1)}), bf16[12,34,208]{2,1,0:T(8,128)(2,1)S(1)}, u32[]{:S(2)}, u32[]{:S(2)}) async-start(bf16[12,34,208]{2,1,0:T(8,128)(2,1)} %reshape.87), calls=%async_computation.1 | async-start | bytes 491520 | tf_op jit(solution)/shard_map/all_to_all | solution.py:86
  177.4 0.1 reduce.5
  177.5 0.7 reshape.88
  178.2 3.8 %convolution_convert_fusion.1 = bf16[512,208]{0,1:T(8,128)(2,1)} fusion(bf16[512,3200]{1,0:T(8,128)(2,1)} %all-gather.5.cloned.1.call-done, bf16[3200,208]{0,1:T(8,128)(2,1)S(1)} %copy-done), kind=kOutput, calls=%fused_computation.1 | convolution fusion | flops 681680896 | bytes 4820992 | tf_op jit(solution)/shard_map/dot_general | solution.py:76
  182.0 11.2 %all-to-all-done.1 = bf16[12,34,208]{2,1,0:T(8,128)(2,1)S(1)} async-done(((bf16[12,34,208]{2,1,0:T(8,128)(2,1)}), bf16[12,34,208]{2,1,0:T(8,128)(2,1)S(1)}, u32[]{:S(2)}, u32[]{:S(2)}) %all-to-all-start.1) | async-done | bytes 169760 | tf_op jit(solution)/shard_map/all_to_all | solution.py:86
  193.2 0.7 convert_reduce_fusion.1
  (10 shorter events, 0.2 us)
Async XLA Ops:
  7.2 171.0 %copy-start = (bf16[3200,208]{0,1:T(8,128)(2,1)S(1)}, bf16[3200,208]{0,1:T(8,128)(2,1)}, u32[]{:S(2)}) copy-start(bf16[3200,208]{0,1:T(8,128)(2,1)} %param.15) | copy-start | bytes 3993604
  7.2 46.1 %all-gather.3.cloned.1.call-start = ((), (), s32[]{:S(2)}) async-start(), calls=%async_computation.6 | async-start | bytes 3686400 | tf_op jit(solution)/shard_map/all_gather | solution.py:58
  7.9 89.2 %all-gather.5.cloned.1.call-start = ((), (), s32[]{:S(2)}) async-start(), calls=%async_computation.7 | async-start | bytes 3686400 | tf_op jit(solution)/shard_map/all_gather | solution.py:67
  11.2 44.8 %copy-start.1 = (bf16[16,12800]{1,0:T(8,128)(2,1)S(1)}, bf16[16,12800]{1,0:T(8,128)(2,1)}, u32[]{:S(2)}) copy-start(bf16[16,12800]{1,0:T(8,128)(2,1)} %param.11) | copy-start | bytes 1228804
  11.2 44.8 %copy-start.3 = (f32[12800]{0:T(1024)S(1)}, f32[12800]{0:T(1024)}, u32[]{:S(2)}) copy-start(f32[12800]{0:T(1024)} %param.12) | copy-start | bytes 153604
  56.4 3.3 %copy-start.4 = (f32[3200]{0:T(1024)S(1)}, f32[3200]{0:T(1024)}, u32[]{:S(2)}) copy-start(f32[3200]{0:T(1024)} %param.13) | copy-start | bytes 38404
  57.9 39.2 %copy-start.2 = (bf16[512,208]{0,1:T(8,128)(2,1)S(1)}, bf16[512,208]{0,1:T(8,128)(2,1)}, u32[]{:S(2)}) copy-start(bf16[512,208]{0,1:T(8,128)(2,1)} %param.14) | copy-start | bytes 638980
  82.6 26.5 %all-to-all-start.4 = ((f32[12,1,1600]{2,1,0:T(1,128)}), f32[12,1,1600]{2,1,0:T(1,128)S(1)}, u32[]{:S(2)}, u32[]{:S(2)}) async-start(f32[12,1,1600]{2,1,0:T(1,128)} %broadcast_in_dim.7), calls=%async_computation.4 | async-start | bytes 159744 | tf_op jit(solution)/shard_map/all_to_all | solution.py:35
  109.2 46.6 %all-to-all-start = ((bf16[8,408,208]{2,1,0:T(8,128)(2,1)}), bf16[8,408,208]{2,1,0:T(8,128)(2,1)S(1)}, u32[]{:S(2)}, u32[]{:S(2)}) async-start(bf16[8,408,208]{2,1,0:T(8,128)(2,1)} %copy.27), calls=%async_computation | async-start | bytes 3342336 | tf_op jit(solution)/shard_map/all_to_all | solution.py:84
  156.4 11.0 %all-to-all-start.5 = ((f32[8,1,1600]{2,1,0:T(1,128)}), f32[8,1,1600]{2,1,0:T(1,128)S(1)}, u32[]{:S(2)}, u32[]{:S(2)}) async-start(f32[8,1,1600]{2,1,0:T(1,128)} %broadcast_in_dim.8), calls=%async_computation.5 | async-start | bytes 106496 | tf_op jit(solution)/shard_map/all_to_all | solution.py:74
  167.4 25.8 %all-to-all-start.1 = ((bf16[12,34,208]{2,1,0:T(8,128)(2,1)}), bf16[12,34,208]{2,1,0:T(8,128)(2,1)S(1)}, u32[]{:S(2)}, u32[]{:S(2)}) async-start(bf16[12,34,208]{2,1,0:T(8,128)(2,1)} %reshape.87), calls=%async_computation.1 | async-start | bytes 491520 | tf_op jit(solution)/shard_map/all_to_all | solution.py:86
Sparse Core Ops, SparseCore 0:
  10.4 42.7 all-gather.2
  60.8 36.3 all-gather.4

commit v2 on v1

v2 whole, which is shorter than its diff:
```python
import jax
import jax.numpy as jnp
from jax import lax
from jax.experimental import pallas as pl
from jax.experimental.pallas import tpu as pltpu
from jax.sharding import Mesh
from jax.sharding import PartitionSpec as P

VW = 3200
PW = 12800
EPSILON = 1e-05
DP = ("z", "y")
MP = ("x", "c")
NZ, NY, NMP = 12, 8, 8
BLOCK = 34
FEAT = NZ * BLOCK
WIDE = 512
TILES, PR, SUB, VT = 8, 16, 4, 64
VMEM = pltpu.CompilerParams(vmem_limit_bytes=48 * 1024 * 1024)
F32, BF16 = jnp.float32, jnp.bfloat16


def split3(value):
    high = value.astype(BF16).astype(F32)
    middle = (value - high).astype(BF16).astype(F32)
    low = (value - high - middle).astype(BF16).astype(F32)
    return high, middle, low


def cut_kernel(grad_ref, feat_ref, out_ref):
    values = feat_ref[...].astype(F32)
    mean = jnp.mean(values, axis=-1, keepdims=True)
    centered = values - mean
    inverse_std = lax.rsqrt(jnp.mean(centered * centered, axis=-1, keepdims=True) + EPSILON)
    marks = split3(mean) + split3(inverse_std)
    lane = lax.broadcasted_iota(jnp.int32, (PR, WIDE), 1)
    for sub in range(SUB):
        for part in range(NMP):
            low = sub * VW + part * FEAT
            start = low // 128 * 128
            width = min(640, PW - start)
            live = lane < min(FEAT, VW - part * FEAT)
            for which, ref in enumerate((grad_ref, feat_ref)):
                window = ref[:, start : start + width].astype(F32)
                if width < 640:
                    window = jnp.concatenate([window, jnp.zeros((PR, 640 - width), F32)], axis=1)
                if low > start:
                    window = pltpu.roll(window, 640 - (low - start), 1)
                chunk = jnp.where(live, window[:, :WIDE], 0.0)
                if which == 1:
                    for at, mark in enumerate(marks):
                        chunk = jnp.where(lane == FEAT + at, mark, chunk)
                row = which * VT + sub * PR
                out_ref[part, row : row + PR, :] = chunk.astype(BF16)


def slot_values(tile, source_ref, live_ref, recv_ref):
    grads = recv_ref[source_ref[tile], 0:VT, :].astype(F32)
    grads = jnp.where(live_ref[tile] > 0, grads, 0.0)
    feats = recv_ref[tile, VT : 2 * VT, :].astype(F32)
    marks = feats[0:PR, 384:512]
    lane = lax.broadcasted_iota(jnp.int32, (PR, 128), 1) + 384
    in_mean = (lane >= FEAT) & (lane < FEAT + 3)
    in_std = (lane >= FEAT + 3) & (lane < FEAT + 6)
    mean = jnp.sum(jnp.where(in_mean, marks, 0.0), axis=-1, keepdims=True)
    inverse_std = jnp.sum(jnp.where(in_std, marks, 0.0), axis=-1, keepdims=True)
    upstream = [grads[s * PR : (s + 1) * PR] for s in range(SUB)]
    normed = [(feats[s * PR : (s + 1) * PR] - mean) * inverse_std for s in range(SUB)]
    return upstream, normed, inverse_std


def sums_kernel(source_ref, live_ref, recv_ref, gain_ref, out_ref):
    lane = lax.broadcasted_iota(jnp.int32, (PR, 128), 1)
    rows = []
    for tile in range(TILES):
        upstream, normed, _ = slot_values(tile, source_ref, live_ref, recv_ref)
        first = jnp.zeros((PR, WIDE), F32)
        second = jnp.zeros((PR, WIDE), F32)
        for s in range(SUB):
            scaled = upstream[s] * gain_ref[s : s + 1, :]
            first = first + scaled
            second = second + scaled * normed[s]
        first = jnp.sum(first, axis=-1, keepdims=True)
        second = jnp.sum(second, axis=-1, keepdims=True)
        rows.append(jnp.where(lane == 0, first, jnp.where(lane == 1, second, 0.0)))
    turned = jnp.concatenate(rows, axis=0).T[0:8, :]
    for part in range(NMP):
        out_ref[part] = turned


def branch_kernel(
    source_ref, live_ref, recv_ref, gain_ref, scale_ref, sums_ref, attn_ref,
    branch_ref, residual_ref, gain_out_ref, terms_ref,
):
    total = sums_ref[0]
    for part in range(1, NMP):
        total = total + sums_ref[part]
    means = jnp.concatenate([total, jnp.zeros((120, 128), F32)], axis=0).T * (1.0 / PW)
    lane = lax.broadcasted_iota(jnp.int32, (PR, 128), 1)
    token = lax.broadcasted_iota(jnp.int32, (VT, VT), 0)
    place = lax.broadcasted_iota(jnp.int32, (VT, VT), 1)
    sub_of = ((token >> 3) & 1) * 2 + (token & 1)
    row_of = (token >> 4) * 4 + ((token >> 1) & 3)
    order = (place == sub_of * PR + row_of).astype(BF16)
    gains = [jnp.zeros((PR, WIDE), F32) for _ in range(SUB)]
    for tile in range(TILES):
        upstream, normed, inverse_std = slot_values(tile, source_ref, live_ref, recv_ref)
        own = means[tile * PR : (tile + 1) * PR]
        first = jnp.sum(jnp.where(lane == 0, own, 0.0), axis=-1, keepdims=True)
        second = jnp.sum(jnp.where(lane == 1, own, 0.0), axis=-1, keepdims=True)
        residual, branch = [], []
        for s in range(SUB):
            scaled = upstream[s] * gain_ref[s : s + 1, :]
            grad = inverse_std * (scaled - first - normed[s] * second)
            residual.append(grad.astype(BF16))
            branch.append((grad * scale_ref[...]).astype(BF16))
            gains[s] = gains[s] + upstream[s] * normed[s]
        residual = jnp.concatenate(residual, axis=0)
        branch = jnp.concatenate(branch, axis=0)
        residual = jnp.dot(order, residual, preferred_element_type=F32)
        branch = jnp.dot(order, branch, preferred_element_type=F32)
        residual_ref[tile] = residual.astype(BF16)
        branch_ref[tile * VT : (tile + 1) * VT, :] = branch.astype(BF16)
    gain_out_ref[...] = jnp.concatenate(
        [jnp.sum(g, axis=0, keepdims=True) for g in gains] + [jnp.zeros((4, WIDE), F32)], axis=0
    )
    turned = branch_ref[...].T
    for part in range(NMP):
        term = jnp.dot(turned, attn_ref[part], preferred_element_type=F32)
        terms_ref[part] = term[:FEAT].astype(BF16)


def whole(count):
    return [pl.BlockSpec(memory_space=pltpu.VMEM)] * count


def scalars(count):
    return [pl.BlockSpec(memory_space=pltpu.SMEM)] * count


def sum_everywhere(part, axis):
    count = lax.axis_size(axis)
    terms = jnp.broadcast_to(part[None], (count,) + part.shape)
    return jnp.sum(lax.all_to_all(terms, axis, 0, 0), axis=0)


def last_places():
    pairs = []
    for z in range(NZ):
        for y in range(NY):
            for part in range(NMP):
                pairs.append(((z * NY + y) * NMP + part, (NZ * part + z) * NMP + y))
    return pairs


def body(
    grad_proj, tile_counts, tile_home, saved_feat, ln_gain, layer_scale, attn_saved, proj_weight
):
    mp_index = lax.axis_index(MP)
    cols = attn_saved.shape[1]
    attn = lax.all_gather(attn_saved, MP, axis=0)

    send = pl.pallas_call(
        cut_kernel,
        out_shape=jax.ShapeDtypeStruct((NMP, 2 * VT, WIDE), BF16),
        in_specs=whole(2),
        out_specs=whole(1)[0],
        compiler_params=VMEM,
        name="cut",
    )(grad_proj, saved_feat)
    recv = lax.all_to_all(send, MP, 0, 0)

    slot_ids = jnp.arange(TILES, dtype=jnp.int32)
    matches = tile_home[0][None, :] == slot_ids[:, None]
    source = jnp.sum(jnp.where(matches, slot_ids[None, :], 0), axis=1).astype(jnp.int32)
    live = (source < jnp.sum(tile_counts)).astype(jnp.int32)
    pad = NMP * FEAT - VW
    gain = jnp.pad(ln_gain.reshape(SUB, VW), ((0, 0), (0, pad + WIDE - FEAT)))
    gain = lax.dynamic_slice_in_dim(gain, mp_index * FEAT, WIDE, axis=1)
    scale = jnp.pad(layer_scale, (0, pad + WIDE - FEAT))
    scale = lax.dynamic_slice_in_dim(scale, mp_index * FEAT, WIDE, axis=0)[None]
    inside = (jnp.arange(WIDE) < FEAT)[None]
    gain = jnp.where(inside, gain, 0.0)
    scale = jnp.where(inside, scale, 0.0)

    sums = pl.pallas_call(
        sums_kernel,
        out_shape=jax.ShapeDtypeStruct((NMP, 8, 128), F32),
        in_specs=scalars(2) + whole(2),
        out_specs=whole(1)[0],
        compiler_params=VMEM,
        name="sums",
    )(source, live, recv, gain)
    sums = lax.all_to_all(sums, MP, 0, 0)

    branch, residual, gain_part, terms = pl.pallas_call(
        branch_kernel,
        out_shape=(
            jax.ShapeDtypeStruct((TILES * VT, WIDE), BF16),
            jax.ShapeDtypeStruct((TILES, VT, WIDE), BF16),
            jax.ShapeDtypeStruct((8, WIDE), F32),
            jax.ShapeDtypeStruct((NMP, FEAT, cols), BF16),
        ),
        in_specs=scalars(2) + whole(5),
        out_specs=tuple(whole(4)),
        compiler_params=VMEM,
        name="branch",
    )(source, live, recv, gain, scale, sums, attn)

    terms = lax.all_to_all(terms, "y", 0, 0)
    part = jnp.sum(terms.astype(F32), axis=0).astype(BF16)
    terms = lax.all_to_all(part.reshape(NZ, BLOCK, cols), "z", 0, 0)
    part = jnp.sum(terms.astype(F32), axis=0)
    proj_grad = lax.ppermute(part, DP + MP, last_places())

    pieces = lax.all_gather(branch, MP, axis=0)
    pieces = jnp.transpose(pieces[:, :, :FEAT], (1, 0, 2)).reshape(TILES * VT, NMP * FEAT)
    attn_grad = jnp.dot(pieces[:, :VW], proj_weight, preferred_element_type=F32).astype(BF16)

    residual = lax.all_to_all(residual, MP, 0, 0)
    residual = jnp.transpose(residual[:, :, :FEAT], (1, 0, 2)).reshape(VT, NMP * FEAT)
    residual_grad = residual[:, :VW]

    gain_part = sum_everywhere(gain_part, "y")
    gain_part = sum_everywhere(gain_part, "z")
    gains = jnp.broadcast_to(gain_part[None], (NMP,) + gain_part.shape)
    gains = lax.all_to_all(gains, MP, 0, 0)[:, :SUB, :FEAT]
    gain_grad = jnp.transpose(gains, (1, 0, 2)).reshape(SUB, NMP * FEAT)[:, :VW].reshape(-1)
    return (residual_grad, attn_grad, proj_grad, gain_grad)


def solution(mesh):
    fine = Mesh(mesh.devices.reshape(NZ, NY, 4, 2), DP + MP)
    in_specs = (
        P(DP + MP, None),
        P(DP, None),
        P(DP, None),
        P(DP + MP, None),
        P(),
        P(),
        P(DP, MP),
        P(None, MP),
    )
    out_specs = (P(DP + MP, None), P(DP, MP), P(DP, MP), P())
    return jax.shard_map(body, mesh=fine, in_specs=in_specs, out_specs=out_specs, check_vma=False)
```

time: 201 us -> 221 us (1.100)
  the two profiles are of different devices: /device:TPU:65 before, /device:TPU:68 now
where the time goes in v2:
time: 221 us; the launch traced here: 220 us
  waiting for transfers between devices  101 us (46%)
  starting transfers between devices  38.6 us (17%)
  blocking collectives  33.4 us (15%)
  local copies, waits for them, and re-layouts  20.4 us (9%)
  between operations  14.8 us (7%)
  Pallas kernels  5.88 us (3%)
  matrix products  3.5 us (2%)
    all_to_all x1, waiting for transfers between devices, body(): terms = lax.all_to_all(terms, 'y', 0, 0)  42.5 us
    all_to_all x1, blocking collectives, body(): residual = lax.all_to_all(residual, MP, 0, 0)  17.2 us
    all_to_all x1, blocking collectives, sum_everywhere(): return jnp.sum(lax.all_to_all(terms, axis, 0, 0), axis=0)  16.2 us
    ppermute x1, waiting for transfers between devices, body(): proj_grad = lax.ppermute(part, DP + MP, last_places())  13.7 us
    all_to_all x1, waiting for transfers between devices, body(): recv = lax.all_to_all(send, MP, 0, 0)  11.9 us
    unnamed x18, local copies, waits for them, and re-layouts  11.8 us
    all_to_all x1, waiting for transfers between devices, body(): terms = lax.all_to_all(part.reshape(NZ, BLOCK, cols), 'z', 0, 0)  10.8 us
    all_gather x1, waiting for transfers between devices, body(): attn = lax.all_gather(attn_saved, MP, axis=0)  10.6 us
  transfers between devices with their start and end apart: 9, of which 7 were waited for; matrix products, arithmetic and copies ran while one was open for 5% of the time, Pallas kernels for 1%

profile of v2, /device:TPU:68, one launch (start us, length us, event | category | flops | bytes accessed | tf_op | source)
XLA Modules:
  0.0 219.6 jit_solution(16301465976565478199)
XLA Ops:
  7.2 0.0 copy-start
  7.2 0.0 all-gather.5.cloned.1.call-start
  7.2 0.7 all-gather.5.cloned.1.call-update
  7.9 1.0 copy-done.3
  8.9 1.0 copy-done.4
  9.9 1.7 cut.1
  11.6 4.9 %all-to-all-start = ((bf16[8,128,512]{2,1,0:T(8,128)(2,1)}), bf16[8,128,512]{2,1,0:T(8,128)(2,1)S(1)}, u32[]{:S(2)}, u32[]{:S(2)}) async-start(bf16[8,128,512]{2,1,0:T(8,128)(2,1)} %cut.1), calls=%async_computation | async-start | bytes 2097152 | tf_op jit(solution)/shard_map/all_to_all | solution.py:171
  17.2 0.0 copy-done.5
  17.2 0.0 copy-done.7
  17.2 0.1 select_reduce_fusion.source_ref
  17.4 0.1 fusion.5.gain_ref
  17.4 11.9 %all-to-all-done.recv_ref = bf16[8,128,512]{2,1,0:T(8,128)(2,1)S(1)} async-done(((bf16[8,128,512]{2,1,0:T(8,128)(2,1)}), bf16[8,128,512]{2,1,0:T(8,128)(2,1)S(1)}, u32[]{:S(2)}, u32[]{:S(2)}) %all-to-all-start) | async-done | bytes 1048608 | tf_op jit(solution)/shard_map/all_to_all | solution.py:171
  29.3 1.6 sums.1
  30.9 6.4 %all-to-all-start.1 = ((f32[8,8,128]{2,1,0:T(8,128)}), f32[8,8,128]{2,1,0:T(8,128)S(1)}, u32[]{:S(2)}, u32[]{:S(2)}) async-start(f32[8,8,128]{2,1,0:T(8,128)} %sums.1), calls=%async_computation.1 | async-start | bytes 65536 | tf_op jit(solution)/shard_map/all_to_all | solution.py:194
  37.4 0.0 copy-done.6
  37.4 0.1 fusion.6
  37.4 10.6 %all-gather.5.cloned.1.call-done = bf16[4096,208]{0,1:T(8,128)(2,1)} async-done(((bf16[512,208]{0,1:T(8,128)(2,1)}), bf16[4096,208]{0,1:T(8,128)(2,1)}) %all-gather.5.cloned.1.call-update) | async-done | bytes 1703952 | tf_op jit(solution)/shard_map/all_gather | solution.py:161
  48.1 3.9 %copy.20 = bf16[4096,208]{1,0:T(8,128)(2,1)} copy(bf16[4096,208]{0,1:T(8,128)(2,1)} %all-gather.5.cloned.1.call-done) | data formatting | bytes 3407872 | tf_op jit(solution)/shard_map/all_gather | solution.py:161
  51.9 0.0 all-to-all-done.1.sums_ref
  52.0 1.6 copy-done.1
  53.5 2.6 %branch.1 = (bf16[512,512]{1,0:T(8,128)(2,1)}, bf16[8,64,512]{2,1,0:T(8,128)(2,1)S(1)}, f32[8,512]{1,0:T(8,128)S(1)}, bf16[8,408,208]{2,1,0:T(8,128)(2,1)S(1)}) custom-call(s32[8]{0:T(128)S(1)} %select_reduce_fusion.source_ref, s32[8]{0:T(128)S(1)} %compare_convert_fusion.live_ref, bf16[8,128,512]{2,1,0:T(8,128)(2,1)S(1)} %all-to-all-done.recv_ref, ...), custom_call_target="tpu_custom_call" | custom-call | tf_op jit(solution)/shard_map/branch/pallas_call | solution.py:196
  56.2 0.0 copy-start.2
  56.2 1.2 copy-done.2
  57.4 0.0 all-gather.7.cloned.1.call-update
  57.5 16.2 %all_to_all.40 = f32[8,8,512]{2,1,0:T(8,128)S(1)} all-to-all(f32[8,8,512]{2,1,0:T(8,128)S(1)} %broadcast_in_dim.55), channel_id=1, replica_groups=mesh['z'=12,'y'=8,'x'=4,'c'=2] {'y'}, dimensions={0} | all-to-all | bytes 262144 | tf_op jit(solution)/shard_map/all_to_all | solution.py:144
  73.6 17.2 %all_to_all.41 = bf16[8,64,512]{2,1,0:T(8,128)(2,1)S(1)} all-to-all(bf16[8,64,512]{2,1,0:T(8,128)(2,1)S(1)} %get-tuple-element.8), channel_id=1, replica_groups=mesh['z'=12,'y'=8,'x'=4,'c'=2] {'x','c'}, dimensions={0} | all-to-all | bytes 1048576 | tf_op jit(solution)/shard_map/all_to_all | solution.py:220
  90.9 4.3 %all-to-all-start.3 = ((bf16[8,408,208]{2,1,0:T(8,128)(2,1)}), bf16[8,408,208]{2,1,0:T(8,128)(2,1)}, u32[]{:S(2)}, u32[]{:S(2)}) async-start(bf16[8,408,208]{2,1,0:T(8,128)(2,1)} %copy-done.2), calls=%async_computation.3 | async-start | bytes 3342336 | tf_op jit(solution)/shard_map/all_to_all | solution.py:210
  95.2 42.5 %all-to-all-done.3 = bf16[8,408,208]{2,1,0:T(8,128)(2,1)} async-done(((bf16[8,408,208]{2,1,0:T(8,128)(2,1)}), bf16[8,408,208]{2,1,0:T(8,128)(2,1)}, u32[]{:S(2)}, u32[]{:S(2)}) %all-to-all-start.3) | async-done | bytes 1357856 | tf_op jit(solution)/shard_map/all_to_all | solution.py:210
  137.7 0.7 broadcast_in_dim.56
  138.4 10.5 %all-to-all-start.6 = ((f32[12,8,512]{2,1,0:T(8,128)}), f32[12,8,512]{2,1,0:T(8,128)S(1)}, u32[]{:S(2)}, u32[]{:S(2)}) async-start(f32[12,8,512]{2,1,0:T(8,128)} %broadcast_in_dim.56), calls=%async_computation.6 | async-start | bytes 393216 | tf_op jit(solution)/shard_map/all_to_all | solution.py:144
  148.8 1.8 reduce_sum.56
  150.6 0.8 reshape.38
  151.4 9.2 %all-to-all-done.6 = f32[12,8,512]{2,1,0:T(8,128)S(1)} async-done(((f32[12,8,512]{2,1,0:T(8,128)}), f32[12,8,512]{2,1,0:T(8,128)S(1)}, u32[]{:S(2)}, u32[]{:S(2)}) %all-to-all-start.6) | async-done | bytes 196640 | tf_op jit(solution)/shard_map/all_to_all | solution.py:144
  160.6 4.1 %all-to-all-start.4 = ((bf16[12,34,208]{2,1,0:T(8,128)(2,1)}), bf16[12,34,208]{2,1,0:T(8,128)(2,1)S(1)}, u32[]{:S(2)}, u32[]{:S(2)}) async-start(bf16[12,34,208]{2,1,0:T(8,128)(2,1)} %reshape.38), calls=%async_computation.4 | async-start | bytes 491520 | tf_op jit(solution)/shard_map/all_to_all | solution.py:212
  164.8 0.3 copy.21
  165.1 0.7 reshape.36
  165.8 0.8 slice.25
  166.6 10.8 %all-to-all-done.4 = bf16[12,34,208]{2,1,0:T(8,128)(2,1)S(1)} async-done(((bf16[12,34,208]{2,1,0:T(8,128)(2,1)}), bf16[12,34,208]{2,1,0:T(8,128)(2,1)S(1)}, u32[]{:S(2)}, u32[]{:S(2)}) %all-to-all-start.4) | async-done | bytes 169760 | tf_op jit(solution)/shard_map/all_to_all | solution.py:212
  177.4 0.7 broadcast_in_dim.57
  178.0 6.3 %all-to-all-start.7 = ((f32[8,8,512]{2,1,0:T(8,128)}), f32[8,8,512]{2,1,0:T(8,128)S(1)}, u32[]{:S(2)}, u32[]{:S(2)}) async-start(f32[8,8,512]{2,1,0:T(8,128)} %broadcast_in_dim.57), calls=%async_computation.7 | async-start | bytes 262144 | tf_op jit(solution)/shard_map/all_to_all | solution.py:227
  184.4 2.0 collective-permute-start
  186.4 1.4 all-to-all-done.7
  187.9 0.1 reshape.39
  188.0 0.6 reshape.40
  188.6 13.7 %collective-permute-done = f32[34,208]{1,0:T(8,128)S(1)} collective-permute-done((f32[34,208]{1,0:T(8,128)S(1)}, f32[34,208]{1,0:T(8,128)S(1)}, u32[]{:S(2)}, u32[]{:S(2)}) %collective-permute-start) | collective-permute-done | bytes 28320 | tf_op jit(solution)/shard_map/ppermute | solution.py:214
  202.3 6.3 %copy.24 = bf16[8,512,408]{1,2,0:T(8,128)(2,1)} copy(bf16[8,512,408]{2,1,0:T(8,128)(2,1)} %bitcast.17) | data formatting | bytes 6684672
  208.7 3.5 %fusion.2 = bf16[512,208]{0,1:T(8,128)(2,1)} fusion(bf16[3200,208]{0,1:T(8,128)(2,1)S(1)} %copy-done, bf16[512,3264]{0,1:T(8,128)(2,1)} %bitcast.18), kind=kOutput, calls=%fused_computation.2 | convolution fusion | flops 681680896 | bytes 4820992 | tf_op jit(solution)/shard_map/dot_general | solution.py:218
  212.2 0.6 copy.27
  (20 shorter events, 0.2 us)
Async XLA Ops:
  7.2 201.5 %copy-start = (bf16[3200,208]{0,1:T(8,128)(2,1)S(1)}, bf16[3200,208]{0,1:T(8,128)(2,1)}, u32[]{:S(2)}) copy-start(bf16[3200,208]{0,1:T(8,128)(2,1)} %param.15) | copy-start | bytes 3993604
  7.2 10.0 %copy-start.5 = (f32[12800]{0:T(1024)S(1)}, f32[12800]{0:T(1024)}, u32[]{:S(2)}) copy-start(f32[12800]{0:T(1024)} %param.12) | copy-start | bytes 153604
  7.2 40.9 %all-gather.5.cloned.1.call-start = ((), (), s32[]{:S(2)}) async-start(), calls=%async_computation.8 | async-start | bytes 1916928 | tf_op jit(solution)/shard_map/all_gather | solution.py:161
  7.9 1.0 copy-start.3
  8.9 1.0 copy-start.4
  9.9 7.3 %copy-start.7 = (s32[1,8]{1,0:T(1,128)S(1)}, s32[1,8]{1,0:T(1,128)}, u32[]{:S(2)}) copy-start(s32[1,8]{1,0:T(1,128)} %param.10) | copy-start | bytes 100
  11.6 25.8 %copy-start.6 = (f32[3200]{0:T(1024)S(1)}, f32[3200]{0:T(1024)}, u32[]{:S(2)}) copy-start(f32[3200]{0:T(1024)} %param.13) | copy-start | bytes 38404
  11.6 17.7 %all-to-all-start = ((bf16[8,128,512]{2,1,0:T(8,128)(2,1)}), bf16[8,128,512]{2,1,0:T(8,128)(2,1)S(1)}, u32[]{:S(2)}, u32[]{:S(2)}) async-start(bf16[8,128,512]{2,1,0:T(8,128)(2,1)} %cut.1), calls=%async_computation | async-start | bytes 2097152 | tf_op jit(solution)/shard_map/all_to_all | solution.py:171
  30.9 21.0 %all-to-all-start.1 = ((f32[8,8,128]{2,1,0:T(8,128)}), f32[8,8,128]{2,1,0:T(8,128)S(1)}, u32[]{:S(2)}, u32[]{:S(2)}) async-start(f32[8,8,128]{2,1,0:T(8,128)} %sums.1), calls=%async_computation.1 | async-start | bytes 65536 | tf_op jit(solution)/shard_map/all_to_all | solution.py:194
  37.4 165.0 %all-gather.7.cloned.1.call-start = ((), (), s32[]{:S(2)}) async-start(), calls=%async_computation.9 | async-start | bytes 4718592 | tf_op jit(solution)/shard_map/all_gather | solution.py:216
  51.9 1.6 copy-start.1
  56.2 1.2 copy-start.2
  90.9 46.8 %all-to-all-start.3 = ((bf16[8,408,208]{2,1,0:T(8,128)(2,1)}), bf16[8,408,208]{2,1,0:T(8,128)(2,1)}, u32[]{:S(2)}, u32[]{:S(2)}) async-start(bf16[8,408,208]{2,1,0:T(8,128)(2,1)} %copy-done.2), calls=%async_computation.3 | async-start | bytes 3342336 | tf_op jit(solution)/shard_map/all_to_all | solution.py:210
  138.4 22.2 %all-to-all-start.6 = ((f32[12,8,512]{2,1,0:T(8,128)}), f32[12,8,512]{2,1,0:T(8,128)S(1)}, u32[]{:S(2)}, u32[]{:S(2)}) async-start(f32[12,8,512]{2,1,0:T(8,128)} %broadcast_in_dim.56), calls=%async_computation.6 | async-start | bytes 393216 | tf_op jit(solution)/shard_map/all_to_all | solution.py:144
  160.6 16.8 %all-to-all-start.4 = ((bf16[12,34,208]{2,1,0:T(8,128)(2,1)}), bf16[12,34,208]{2,1,0:T(8,128)(2,1)S(1)}, u32[]{:S(2)}, u32[]{:S(2)}) async-start(bf16[12,34,208]{2,1,0:T(8,128)(2,1)} %reshape.38), calls=%async_computation.4 | async-start | bytes 491520 | tf_op jit(solution)/shard_map/all_to_all | solution.py:212
  178.0 9.8 %all-to-all-start.7 = ((f32[8,8,512]{2,1,0:T(8,128)}), f32[8,8,512]{2,1,0:T(8,128)S(1)}, u32[]{:S(2)}, u32[]{:S(2)}) async-start(f32[8,8,512]{2,1,0:T(8,128)} %broadcast_in_dim.57), calls=%async_computation.7 | async-start | bytes 262144 | tf_op jit(solution)/shard_map/all_to_all | solution.py:227
  184.4 17.9 %collective-permute-start = (f32[34,208]{1,0:T(8,128)S(1)}, f32[34,208]{1,0:T(8,128)S(1)}, u32[]{:S(2)}, u32[]{:S(2)}) collective-permute-start(f32[34,208]{1,0:T(8,128)S(1)} %convert_reduce_fusion), channel_id=1, source_target_pairs={{0,0},{1,96},{2,192},{3,288},{4,384},{5,480},{6,576},{7,672},{8,1}... | collective-permute-start | bytes 84872 | tf_op jit(solution)/shard_map/ppermute | solution.py:214
Sparse Core Ops, SparseCore 0:
  10.4 37.5 all-gather.4
  57.6 45.9 all-gather.6

commit v3 on v2

--- a/solution.py
+++ b/solution.py
@@ -27,13 +27,19 @@
     return high, middle, low
 
 
-def cut_kernel(grad_ref, feat_ref, out_ref):
+def cut_kernel(grad_hbm, feat_hbm, out_ref, grad_ref, feat_ref, sems):
+    feat_copy = pltpu.make_async_copy(feat_hbm, feat_ref, sems.at[0])
+    grad_copy = pltpu.make_async_copy(grad_hbm, grad_ref, sems.at[1])
+    feat_copy.start()
+    grad_copy.start()
+    feat_copy.wait()
     values = feat_ref[...].astype(F32)
     mean = jnp.mean(values, axis=-1, keepdims=True)
     centered = values - mean
     inverse_std = lax.rsqrt(jnp.mean(centered * centered, axis=-1, keepdims=True) + EPSILON)
     marks = split3(mean) + split3(inverse_std)
     lane = lax.broadcasted_iota(jnp.int32, (PR, WIDE), 1)
+    grad_copy.wait()
     for sub in range(SUB):
         for part in range(NMP):
             low = sub * VW + part * FEAT
@@ -88,10 +94,21 @@
         out_ref[part] = turned
 
 
+def dot_nt(left, right):
+    return lax.dot_general(left, right, (((1,), (1,)), ((), ())), preferred_element_type=F32)
+
+
+ROWS1, ROWS2, ROWS3, GAIN = 416, 208, 64, 16
+AT2, AT3, AT4, AT5 = ROWS1, ROWS1 + ROWS2, ROWS1 + ROWS2 + ROWS3, ROWS1 + ROWS2 + ROWS3 + GAIN
+MESSAGE = AT5 + GAIN
+
+
 def branch_kernel(
-    source_ref, live_ref, recv_ref, gain_ref, scale_ref, sums_ref, attn_ref,
-    branch_ref, residual_ref, gain_out_ref, terms_ref,
+    source_ref, live_ref, recv_ref, gain_ref, scale_ref, sums_ref, attn_hbm,
+    turned_ref, terms_hbm, attn_ref, terms_ref, branch_ref, attn_sem, terms_sems,
 ):
+    attn_copy = pltpu.make_async_copy(attn_hbm, attn_ref, attn_sem)
+    attn_copy.start()
     total = sums_ref[0]
     for part in range(1, NMP):
         total = total + sums_ref[part]
@@ -108,26 +125,96 @@
         own = means[tile * PR : (tile + 1) * PR]
         first = jnp.sum(jnp.where(lane == 0, own, 0.0), axis=-1, keepdims=True)
         second = jnp.sum(jnp.where(lane == 1, own, 0.0), axis=-1, keepdims=True)
-        residual, branch = [], []
+        branch = []
         for s in range(SUB):
             scaled = upstream[s] * gain_ref[s : s + 1, :]
             grad = inverse_std * (scaled - first - normed[s] * second)
-            residual.append(grad.astype(BF16))
             branch.append((grad * scale_ref[...]).astype(BF16))
             gains[s] = gains[s] + upstream[s] * normed[s]
-        residual = jnp.concatenate(residual, axis=0)
-        branch = jnp.concatenate(branch, axis=0)
-        residual = jnp.dot(order, residual, preferred_element_type=F32)
-        branch = jnp.dot(order, branch, preferred_element_type=F32)
-        residual_ref[tile] = residual.astype(BF16)
+        branch = jnp.dot(order, jnp.concatenate(branch, axis=0), preferred_element_type=F32)
         branch_ref[tile * VT : (tile + 1) * VT, :] = branch.astype(BF16)
-    gain_out_ref[...] = jnp.concatenate(
-        [jnp.sum(g, axis=0, keepdims=True) for g in gains] + [jnp.zeros((4, WIDE), F32)], axis=0
-    )
+    gain = jnp.concatenate([jnp.sum(g, axis=0, keepdims=True) for g in gains], axis=0)
+    gain = jnp.concatenate([gain[:, q * 128 : (q + 1) * 128] for q in range(4)], axis=0)
+    gain_high = gain.astype(BF16)
+    gain_low = (gain - gain_high.astype(F32)).astype(BF16)
     turned = branch_ref[...].T
+    turned_ref[...] = turned[:FEAT]
+    attn_copy.wait()
+    half = lax.broadcasted_iota(jnp.int32, (ROWS2, 128), 1) < 64
+    group = lax.broadcasted_iota(jnp.int32, (ROWS3, 128), 1) >> 4
+    copies = []
     for part in range(NMP):
-        term = jnp.dot(turned, attn_ref[part], preferred_element_type=F32)
-        terms_ref[part] = term[:FEAT].astype(BF16)
+        attn = attn_ref[part]
+        terms_ref[part, 0:AT2, :] = dot_nt(turned[:ROWS1], attn[0:128]).astype(BF16)
+        second = dot_nt(turned[:ROWS1], jnp.concatenate([attn[128:192]] * 2, axis=0))
+        second = jnp.where(half, second[:ROWS2], second[ROWS2:])
+        terms_ref[part, AT2:AT3, :] = second.astype(BF16)
+        third = dot_nt(turned[: 7 * ROWS3], jnp.concatenate([attn[192:208]] * 8, axis=0))
+        packed = third[:ROWS3]
+        for g in range(1, 7):
+            packed = jnp.where(group == g, third[g * ROWS3 : (g + 1) * ROWS3], packed)
+        terms_ref[part, AT3:AT4, :] = packed.astype(BF16)
+        terms_ref[part, AT4:AT5, :] = gain_high
+        terms_ref[part, AT5:MESSAGE, :] = gain_low
+        copies.append(
+            pltpu.make_async_copy(terms_ref.at[part], terms_hbm.at[part], terms_sems.at[part])
+        )
+        copies[-1].start()
+    for copy in copies:
+        copy.wait()
+
+
+def fold_kernel(recv_ref, out_ref, wide_ref):
+    total = recv_ref[0].astype(F32)
+    for part in range(1, NY):
+        total = total + recv_ref[part].astype(F32)
+    second = total[AT2:AT3]
+    second = jnp.concatenate([second, pltpu.roll(second, 64, 1)], axis=0)
+    third = total[AT3:AT4]
+    third = [pltpu.roll(third, (64 - 16 * g) % 128, 1) if g != 4 else third for g in range(7)]
+    third = jnp.concatenate(third, axis=0)[:ROWS1]
+    lane = lax.broadcasted_iota(jnp.int32, (ROWS1, 128), 1)
+    wide_ref[:, 0:128] = total[0:ROWS1]
+    wide_ref[:, 128:256] = jnp.where(lane < 64, second, jnp.where(lane < 80, third, 0.0))
+    gain = total[AT4:AT5] + total[AT5:MESSAGE]
+    gain = jnp.concatenate([gain[0:8], gain[8:16]], axis=1)
+    for z in range(NZ):
+        rows = wide_ref[z * BLOCK : z * BLOCK + 40, :]
+        out_ref[z] = jnp.concatenate([rows, gain], axis=0).astype(BF16)
+
+
+def settle_kernel(recv_ref, block_ref, gain_ref):
+    total = recv_ref[0].astype(F32)
+    for part in range(1, NZ):
+        total = total + recv_ref[part].astype(F32)
+    block_ref[...] = total[0:BLOCK, 0 : block_ref.shape[1]]
+    gain = jnp.concatenate([total[40:48, 0:128], total[40:48, 128:256]], axis=0)
+    for part in range(NMP):
+        gain_ref[part] = gain
+
+
+def spread_kernel(gain_ref, out_ref, wide_ref):
+    wide_ref[...] = jnp.zeros_like(wide_ref)
+    for part in range(NMP):
+        gain = gain_ref[part]
+        pieces = [gain[q * SUB : (q + 1) * SUB] for q in range(4)] + [jnp.zeros((SUB, 128), F32)]
+        low = part * FEAT
+        start = low // 128 * 128
+        pieces = jnp.concatenate(pieces, axis=1)
+        if low > start:
+            pieces = pltpu.roll(pieces, low - start, 1)
+        wide_ref[:, start : start + 640] += pieces
+    out_ref[...] = wide_ref[:, 0:VW]
+
+
+def gathered_kernel(own_ref, turned_ref, weight_ref, scale_ref, attn_ref, residual_ref):
+    attn = jnp.dot(weight_ref[...], turned_ref[0:VW, :], preferred_element_type=F32)
+    attn_ref[...] = attn.astype(BF16)
+    own = own_ref[0]
+    at = pl.multiple_of((own >> 1) * 128, 128)
+    tokens = turned_ref[0:VW, pl.ds(at, 128)].astype(F32).T
+    tokens = jnp.where((own & 1) == 0, tokens[0:VT], tokens[VT : 2 * VT])
+    residual_ref[...] = (tokens / scale_ref[...]).astype(BF16)
 
 
 def whole(count):
@@ -136,12 +223,6 @@
 
 def scalars(count):
     return [pl.BlockSpec(memory_space=pltpu.SMEM)] * count
-
-
-def sum_everywhere(part, axis):
-    count = lax.axis_size(axis)
-    terms = jnp.broadcast_to(part[None], (count,) + part.shape)
-    return jnp.sum(lax.all_to_all(terms, axis, 0, 0), axis=0)
 
 
 def last_places():
@@ -153,18 +234,27 @@
     return pairs
 
 
+def in_hbm(count):
+    return [pl.BlockSpec(memory_space=pltpu.HBM)] * count
+
+
 def body(
     grad_proj, tile_counts, tile_home, saved_feat, ln_gain, layer_scale, attn_saved, proj_weight
 ):
     mp_index = lax.axis_index(MP)
     cols = attn_saved.shape[1]
-    attn = lax.all_gather(attn_saved, MP, axis=0)
+    attn = lax.all_gather(attn_saved.T, MP, axis=0)
 
     send = pl.pallas_call(
         cut_kernel,
         out_shape=jax.ShapeDtypeStruct((NMP, 2 * VT, WIDE), BF16),
-        in_specs=whole(2),
+        in_specs=in_hbm(2),
         out_specs=whole(1)[0],
+        scratch_shapes=[
+            pltpu.VMEM((PR, PW), BF16),
+            pltpu.VMEM((PR, PW), BF16),
+            pltpu.SemaphoreType.DMA((2,)),
+        ],
         compiler_params=VMEM,
         name="cut",
     )(grad_proj, saved_feat)
@@ -193,40 +283,75 @@
     )(source, live, recv, gain)
     sums = lax.all_to_all(sums, MP, 0, 0)
 
-    branch, residual, gain_part, terms = pl.pallas_call(
+    turned, terms = pl.pallas_call(
         branch_kernel,
         out_shape=(
-            jax.ShapeDtypeStruct((TILES * VT, WIDE), BF16),
-            jax.ShapeDtypeStruct((TILES, VT, WIDE), BF16),
-            jax.ShapeDtypeStruct((8, WIDE), F32),
-            jax.ShapeDtypeStruct((NMP, FEAT, cols), BF16),
+            jax.ShapeDtypeStruct((FEAT, TILES * VT), BF16),
+            jax.ShapeDtypeStruct((NMP, MESSAGE, 128), BF16),
         ),
-        in_specs=scalars(2) + whole(5),
-        out_specs=tuple(whole(4)),
+        in_specs=scalars(2) + whole(4) + in_hbm(1),
+        out_specs=(whole(1)[0], in_hbm(1)[0]),
+        scratch_shapes=[
+            pltpu.VMEM((NMP, cols, TILES * VT), BF16),
+            pltpu.VMEM((NMP, MESSAGE, 128), BF16),
+            pltpu.VMEM((TILES * VT, WIDE), BF16),
+            pltpu.SemaphoreType.DMA,
+            pltpu.SemaphoreType.DMA((NMP,)),
+        ],
         compiler_params=VMEM,
         name="branch",
     )(source, live, recv, gain, scale, sums, attn)
 
     terms = lax.all_to_all(terms, "y", 0, 0)
-    part = jnp.sum(terms.astype(F32), axis=0).astype(BF16)
-    terms = lax.all_to_all(part.reshape(NZ, BLOCK, cols), "z", 0, 0)
-    part = jnp.sum(terms.astype(F32), axis=0)
+    terms = pl.pallas_call(
+        fold_kernel,
+        out_shape=jax.ShapeDtypeStruct((NZ, 48, 256), BF16),
+        in_specs=whole(1),
+        out_specs=whole(1)[0],
+        scratch_shapes=[pltpu.VMEM((ROWS1, 256), F32)],
+        compiler_params=VMEM,
+        name="fold",
+    )(terms)
+    terms = lax.all_to_all(terms, "z", 0, 0)
+
+    turned = lax.all_gather(turned, MP, axis=0, tiled=True)
+    attn_grad, residual_grad = pl.pallas_call(
+        gathered_kernel,
+        out_shape=(
+            jax.ShapeDtypeStruct((cols, TILES * VT), BF16),
+            jax.ShapeDtypeStruct((VT, VW), BF16),
+        ),
+        in_specs=scalars(1) + whole(3),
+        out_specs=tuple(whole(2)),
+        compiler_params=VMEM,
+        name="gathered",
+    )(mp_index.astype(jnp.int32)[None], turned, proj_weight.T, layer_scale[None])
+
+    terms, attn_grad, residual_grad = lax.optimization_barrier((terms, attn_grad, residual_grad))
+    part, gains = pl.pallas_call(
+        settle_kernel,
+        out_shape=(
+            jax.ShapeDtypeStruct((BLOCK, cols), F32),
+            jax.ShapeDtypeStruct((NMP, GAIN, 128), F32),
+        ),
+        in_specs=whole(1),
+        out_specs=tuple(whole(2)),
+        compiler_params=VMEM,
+        name="settle",
+    )(terms)
+
     proj_grad = lax.ppermute(part, DP + MP, last_places())
-
-    pieces = lax.all_gather(branch, MP, axis=0)
-    pieces = jnp.transpose(pieces[:, :, :FEAT], (1, 0, 2)).reshape(TILES * VT, NMP * FEAT)
-    attn_grad = jnp.dot(pieces[:, :VW], proj_weight, preferred_element_type=F32).astype(BF16)
-
-    residual = lax.all_to_all(residual, MP, 0, 0)
-    residual = jnp.transpose(residual[:, :, :FEAT], (1, 0, 2)).reshape(VT, NMP * FEAT)
-    residual_grad = residual[:, :VW]
-
-    gain_part = sum_everywhere(gain_part, "y")
-    gain_part = sum_everywhere(gain_part, "z")
-    gains = jnp.broadcast_to(gain_part[None], (NMP,) + gain_part.shape)
-    gains = lax.all_to_all(gains, MP, 0, 0)[:, :SUB, :FEAT]
-    gain_grad = jnp.transpose(gains, (1, 0, 2)).reshape(SUB, NMP * FEAT)[:, :VW].reshape(-1)
-    return (residual_grad, attn_grad, proj_grad, gain_grad)
+    gains = lax.all_to_all(gains, MP, 0, 0)
+    gain_grad = pl.pallas_call(
+        spread_kernel,
+        out_shape=jax.ShapeDtypeStruct((SUB, VW), F32),
+        in_specs=whole(1),
+        out_specs=whole(1)[0],
+        scratch_shapes=[pltpu.VMEM((SUB, 3456), F32)],
+        compiler_params=VMEM,
+        name="spread",
+    )(gains)
+    return (residual_grad, attn_grad.T, proj_grad, gain_grad.reshape(-1))
 
 
 def solution(mesh):

time: 221 us -> 163 us (0.74)
  waiting for transfers between devices: 101 us -> 50.6 us
  local copies, waits for them, and re-layouts: 20.4 us -> 6.71 us
  blocking collectives: 33.4 us -> 45.1 us
  Pallas kernels: 5.88 us -> 16.5 us
  starting transfers between devices: 38.6 us -> 28.5 us
  matrix products: 3.5 us -> 0 us
    all_to_all x4 -> x2, waiting for transfers between devices: 63.9 us -> 12.1 us  [the longest x1 12.1 us: body(): terms = lax.all_to_all(terms, 'z', 0, 0)]
    all_to_all x2 -> x1, blocking collectives: 33.4 us -> 45.1 us  [body(): terms = lax.all_to_all(terms, 'y', 0, 0)]
    pallas_call x1 -> x5, Pallas kernels: 2.63 us -> 12.7 us  [the longest x1 9.3 us: body(): pl.pallas_call(branch_kernel, out_shape=(jax.ShapeDtypeStruct((FEAT, TILE...]
    all_to_all x4 -> x2, starting transfers between devices: 25.3 us -> 15.2 us  [the longest x1 10.2 us: body(): terms = lax.all_to_all(terms, 'z', 0, 0)]
    unnamed x18 -> x17, local copies, waits for them, and re-layouts: 11.8 us -> 6.03 us
    all_gather x1 -> x0, local copies, waits for them, and re-layouts: 3.89 us -> none  [body(): attn = lax.all_gather(attn_saved, MP, axis=0)]
    all_gather x2, waiting for transfers between devices: 10.6 us -> 7.02 us  [the longest x1 7 us: body(): attn = lax.all_gather(attn_saved.T, MP, axis=0)]
    dot_general x1 -> x0, matrix products: 3.5 us -> none  [body(): jnp.dot(pieces[:, :VW], proj_weight, preferred_element_type=F32)]
  transfers between devices with their start and end apart: 9 -> 7, of which waited for: 7 -> 5; matrix products, arithmetic and copies ran while one was open for 5% -> 0% of each run, Pallas kernels for 1% -> 4%
where the time goes in v3:
time: 163 us
  waiting for transfers between devices  50.6 us (31%)
  blocking collectives  45.1 us (28%)
  starting transfers between devices  28.5 us (17%)
  Pallas kernels  16.5 us (10%)
  between operations  14.8 us (9%)
  local copies, waits for them, and re-layouts  6.71 us (4%)
    all_to_all x1, blocking collectives, body(): terms = lax.all_to_all(terms, 'y', 0, 0)  45.1 us
    ppermute x1, waiting for transfers between devices, body(): proj_grad = lax.ppermute(part, DP + MP, last_places())  16 us
    all_to_all x1, waiting for transfers between devices, body(): terms = lax.all_to_all(terms, 'z', 0, 0)  12.1 us
    all_to_all x1, waiting for transfers between devices, body(): recv = lax.all_to_all(send, MP, 0, 0)  11.9 us
    all_to_all x1, starting transfers between devices, body(): terms = lax.all_to_all(terms, 'z', 0, 0)  10.2 us
    pallas_call x1, Pallas kernels, body(): pl.pallas_call(branch_kernel, out_shape=(jax.ShapeDtypeStruct((FEAT, TILE...  9.3 us
    all_gather x1, waiting for transfers between devices, body(): attn = lax.all_gather(attn_saved.T, MP, axis=0)  7 us
    all_to_all x1, starting transfers between devices, body(): sums = lax.all_to_all(sums, MP, 0, 0)  6.42 us
  transfers between devices with their start and end apart: 7, of which 5 were waited for; matrix products, arithmetic and copies ran while one was open for 0% of the time, Pallas kernels for 4%

profile of v3, /device:TPU:68, one launch (start us, length us, event | category | flops | bytes accessed | tf_op | source)
XLA Modules:
  0.0 162.6 jit_solution(6130272979649074985)
XLA Ops:
  7.2 0.0 all-gather.6.cloned.1.call-start
  7.2 0.7 all-gather.6.cloned.1.call-update
  7.9 0.0 copy-start.3
  7.9 1.0 copy-done.3
  8.9 0.0 copy-start.4
  8.9 1.0 copy-done.4
  9.9 2.2 %cut.1 = bf16[8,128,512]{2,1,0:T(8,128)(2,1)} custom-call(bf16[16,12800]{1,0:T(8,128)(2,1)S(1)} %copy-done.3, bf16[16,12800]{1,0:T(8,128)(2,1)S(1)} %copy-done.4), custom_call_target="tpu_custom_call" | custom-call | tf_op jit(solution)/shard_map/cut/pallas_call | solution.py:248
  12.1 0.0 copy-start.6
  12.1 0.0 copy-start.7
  12.1 0.0 copy-start.5
  12.1 4.9 %all-to-all-start = ((bf16[8,128,512]{2,1,0:T(8,128)(2,1)}), bf16[8,128,512]{2,1,0:T(8,128)(2,1)S(1)}, u32[]{:S(2)}, u32[]{:S(2)}) async-start(bf16[8,128,512]{2,1,0:T(8,128)(2,1)} %cut.1), calls=%async_computation | async-start | bytes 2097152 | tf_op jit(solution)/shard_map/all_to_all | solution.py:261
  17.7 0.0 copy-done.6
  17.8 0.0 copy-done.7
  17.8 0.1 select_reduce_fusion.source_ref
  17.9 0.1 fusion.gain_ref
  18.0 11.9 %all-to-all-done.recv_ref = bf16[8,128,512]{2,1,0:T(8,128)(2,1)S(1)} async-done(((bf16[8,128,512]{2,1,0:T(8,128)(2,1)}), bf16[8,128,512]{2,1,0:T(8,128)(2,1)S(1)}, u32[]{:S(2)}, u32[]{:S(2)}) %all-to-all-start) | async-done | bytes 1048608 | tf_op jit(solution)/shard_map/all_to_all | solution.py:261
  29.9 1.6 sums.1
  31.5 6.4 %all-to-all-start.1 = ((f32[8,8,128]{2,1,0:T(8,128)}), f32[8,8,128]{2,1,0:T(8,128)S(1)}, u32[]{:S(2)}, u32[]{:S(2)}) async-start(f32[8,8,128]{2,1,0:T(8,128)} %sums.1), calls=%async_computation.1 | async-start | bytes 65536 | tf_op jit(solution)/shard_map/all_to_all | solution.py:284
  37.9 0.0 all-gather.4.cloned.1.call-start
  37.9 0.0 copy-done.5
  37.9 0.1 fusion.1
  38.0 2.9 %all-to-all-done.1.sums_ref = f32[8,8,128]{2,1,0:T(8,128)S(1)} async-done(((f32[8,8,128]{2,1,0:T(8,128)}), f32[8,8,128]{2,1,0:T(8,128)S(1)}, u32[]{:S(2)}, u32[]{:S(2)}) %all-to-all-start.1) | async-done | bytes 32800 | tf_op jit(solution)/shard_map/all_to_all | solution.py:284
  40.9 7.0 %all-gather.6.cloned.1.call-done = bf16[1664,512]{1,0:T(8,128)(2,1)} async-done(((bf16[208,512]{1,0:T(8,128)(2,1)}), bf16[1664,512]{1,0:T(8,128)(2,1)}) %all-gather.6.cloned.1.call-update) | async-done | bytes 1703952 | tf_op jit(solution)/shard_map/all_gather | solution.py:246
  47.9 0.0 copy-start.1
  47.9 1.5 copy-done.1
  49.4 9.3 %branch.1 = (bf16[408,512]{1,0:T(8,128)(2,1)}, bf16[8,720,128]{2,1,0:T(8,128)(2,1)S(1)}) custom-call(s32[8]{0:T(128)S(1)} %select_reduce_fusion.source_ref, s32[8]{0:T(128)S(1)} %compare_convert_fusion.live_ref, bf16[8,128,512]{2,1,0:T(8,128)(2,1)S(1)} %all-to-all-done.recv_ref, f32[4,512]{1,0:T(4,128)S(1)} %fusion.gain_ref, f32[1,512]{1,0:T(1,128)S(1)} %bitcast.11, ...), custom_call_target="tpu_custom_call" | custom-call | tf_op jit(solution)/shard_map/branch/pallas_call | solution.py:286
  58.7 0.0 all-gather.4.cloned.1.call-update
  58.7 45.1 %all_to_all.25.recv_ref = bf16[8,720,128]{2,1,0:T(8,128)(2,1)S(1)} all-to-all(bf16[8,720,128]{2,1,0:T(8,128)(2,1)S(1)} %get-tuple-element.13), channel_id=1, replica_groups=mesh['z'=12,'y'=8,'x'=4,'c'=2] {'y'}, dimensions={0} | all-to-all | bytes 2949120 | tf_op jit(solution)/shard_map/all_to_all | solution.py:305
  103.8 0.0 copy-start.2
  103.8 1.0 fold.1
  104.8 10.2 %all-to-all-start.3 = ((bf16[12,48,256]{2,1,0:T(8,128)(2,1)}), bf16[12,48,256]{2,1,0:T(8,128)(2,1)S(1)}, u32[]{:S(2)}, u32[]{:S(2)}) async-start(bf16[12,48,256]{2,1,0:T(8,128)(2,1)} %fold.1), calls=%async_computation.3 | async-start | bytes 589824 | tf_op jit(solution)/shard_map/all_to_all | solution.py:315
  115.1 0.0 all-gather.4.cloned.1.call-done.turned_ref
  115.1 0.0 copy-done.2
  115.1 0.0 copy-start
  115.1 1.9 %copy-done = bf16[3264,512]{1,0:T(8,128)(2,1)S(1)} copy-done((bf16[3264,512]{1,0:T(8,128)(2,1)S(1)}, bf16[3264,512]{1,0:T(8,128)(2,1)}, u32[]{:S(2)}) %copy-start) | copy-done | bytes 3342360
  117.1 1.7 %gathered.1 = (bf16[208,512]{1,0:T(8,128)(2,1)}, bf16[64,3200]{1,0:T(8,128)(2,1)}) custom-call(s32[1]{0:T(128)} %bitcast.5.own_ref, bf16[3264,512]{1,0:T(8,128)(2,1)S(1)} %copy-done, bf16[208,3200]{1,0:T(8,128)(2,1)S(1)} %bitcast.10, f32[1,3200]{1,0:T(1,128)S(1)} %broadcast_in_dim.44.scale_ref), custom_call_target="tpu_custom_call" | custom-call | tf_op jit(solution)/shard_map/gathered/pallas_call | solution.py:318
  118.8 12.1 %all-to-all-done.3.recv_ref = bf16[12,48,256]{2,1,0:T(8,128)(2,1)S(1)} async-done(((bf16[12,48,256]{2,1,0:T(8,128)(2,1)}), bf16[12,48,256]{2,1,0:T(8,128)(2,1)S(1)}, u32[]{:S(2)}, u32[]{:S(2)}) %all-to-all-start.3) | async-done | bytes 294944 | tf_op jit(solution)/shard_map/all_to_all | solution.py:315
  130.9 0.6 settle.1
  131.5 5.0 %all-to-all-start.4 = ((f32[8,16,128]{2,1,0:T(8,128)}), f32[8,16,128]{2,1,0:T(8,128)S(1)}, u32[]{:S(2)}, u32[]{:S(2)}) async-start(f32[8,16,128]{2,1,0:T(8,128)} %get-tuple-element.21), calls=%async_computation.4 | async-start | bytes 131072 | tf_op jit(solution)/shard_map/all_to_all | solution.py:344
  136.5 1.9 %collective-permute-start = (f32[34,208]{1,0:T(8,128)S(1)}, f32[34,208]{1,0:T(8,128)S(1)}, u32[]{:S(2)}, u32[]{:S(2)}) collective-permute-start(f32[34,208]{1,0:T(8,128)S(1)} %get-tuple-element.20), channel_id=1, source_target_pairs={{0,0},{1,96},{2,192},{3,288},{4,384},{5,480},{6,576},{7,672},{8,1}... | collective-permute-start | bytes 84872 | tf_op jit(solution)/shard_map/ppermute | solution.py:343
  138.4 16.0 %collective-permute-done = f32[34,208]{1,0:T(8,128)S(1)} collective-permute-done((f32[34,208]{1,0:T(8,128)S(1)}, f32[34,208]{1,0:T(8,128)S(1)}, u32[]{:S(2)}, u32[]{:S(2)}) %collective-permute-start) | collective-permute-done | bytes 28320 | tf_op jit(solution)/shard_map/ppermute | solution.py:343
  154.4 0.0 all-to-all-done.4.gain_ref
  154.4 0.1 spread.1
  154.5 0.6 reshape.21
  155.2 0.6 copy.14
  (4 shorter events, 0.0 us)
Async XLA Ops:
  7.2 40.8 %all-gather.6.cloned.1.call-start = ((), (), s32[]{:S(2)}) async-start(), calls=%async_computation.6 | async-start | bytes 1916928 | tf_op jit(solution)/shard_map/all_gather | solution.py:246
  7.9 1.0 copy-start.3
  8.9 1.0 copy-start.4
  12.1 5.6 %copy-start.6 = (f32[12800]{0:T(1024)S(1)}, f32[12800]{0:T(1024)}, u32[]{:S(2)}) copy-start(f32[12800]{0:T(1024)} %param.12) | copy-start | bytes 153604
  12.1 5.7 %copy-start.7 = (s32[1,8]{1,0:T(1,128)S(1)}, s32[1,8]{1,0:T(1,128)}, u32[]{:S(2)}) copy-start(s32[1,8]{1,0:T(1,128)} %param.10) | copy-start | bytes 100
  12.1 25.8 %copy-start.5 = (f32[3200]{0:T(1024)S(1)}, f32[3200]{0:T(1024)}, u32[]{:S(2)}) copy-start(f32[3200]{0:T(1024)} %param.13) | copy-start | bytes 38404
  12.1 17.8 %all-to-all-start = ((bf16[8,128,512]{2,1,0:T(8,128)(2,1)}), bf16[8,128,512]{2,1,0:T(8,128)(2,1)S(1)}, u32[]{:S(2)}, u32[]{:S(2)}) async-start(bf16[8,128,512]{2,1,0:T(8,128)(2,1)} %cut.1), calls=%async_computation | async-start | bytes 2097152 | tf_op jit(solution)/shard_map/all_to_all | solution.py:261
  31.5 9.4 %all-to-all-start.1 = ((f32[8,8,128]{2,1,0:T(8,128)}), f32[8,8,128]{2,1,0:T(8,128)S(1)}, u32[]{:S(2)}, u32[]{:S(2)}) async-start(f32[8,8,128]{2,1,0:T(8,128)} %sums.1), calls=%async_computation.1 | async-start | bytes 65536 | tf_op jit(solution)/shard_map/all_to_all | solution.py:284
  37.9 77.2 %all-gather.4.cloned.1.call-start = ((), (), s32[]{:S(2)}) async-start(), calls=%async_computation.5 | async-start | bytes 3760128 | tf_op jit(solution)/shard_map/all_gather | solution.py:317
  47.9 1.5 copy-start.1
  103.8 11.3 %copy-start.2 = (bf16[3200,208]{0,1:T(8,128)(2,1)S(1)}, bf16[3200,208]{0,1:T(8,128)(2,1)}, u32[]{:S(2)}) copy-start(bf16[3200,208]{0,1:T(8,128)(2,1)} %param.15) | copy-start | bytes 3993604
  104.8 26.1 %all-to-all-start.3 = ((bf16[12,48,256]{2,1,0:T(8,128)(2,1)}), bf16[12,48,256]{2,1,0:T(8,128)(2,1)S(1)}, u32[]{:S(2)}, u32[]{:S(2)}) async-start(bf16[12,48,256]{2,1,0:T(8,128)(2,1)} %fold.1), calls=%async_computation.3 | async-start | bytes 589824 | tf_op jit(solution)/shard_map/all_to_all | solution.py:315
  115.1 1.9 %copy-start = (bf16[3264,512]{1,0:T(8,128)(2,1)S(1)}, bf16[3264,512]{1,0:T(8,128)(2,1)}, u32[]{:S(2)}) copy-start(bf16[3264,512]{1,0:T(8,128)(2,1)} %all-gather.4.cloned.1.call-done.turned_ref) | copy-start | bytes 10027012
  131.5 22.9 %all-to-all-start.4 = ((f32[8,16,128]{2,1,0:T(8,128)}), f32[8,16,128]{2,1,0:T(8,128)S(1)}, u32[]{:S(2)}, u32[]{:S(2)}) async-start(f32[8,16,128]{2,1,0:T(8,128)} %get-tuple-element.21), calls=%async_computation.4 | async-start | bytes 131072 | tf_op jit(solution)/shard_map/all_to_all | solution.py:344
  136.5 17.9 %collective-permute-start = (f32[34,208]{1,0:T(8,128)S(1)}, f32[34,208]{1,0:T(8,128)S(1)}, u32[]{:S(2)}, u32[]{:S(2)}) collective-permute-start(f32[34,208]{1,0:T(8,128)S(1)} %get-tuple-element.20), channel_id=1, source_target_pairs={{0,0},{1,96},{2,192},{3,288},{4,384},{5,480},{6,576},{7,672},{8,1}... | collective-permute-start | bytes 84872 | tf_op jit(solution)/shard_map/ppermute | solution.py:343
Sparse Core Ops, SparseCore 0:
  10.4 37.4 all-gather.5
  58.8 36.6 all-gather.3

commit v4 on v3

--- a/solution.py
+++ b/solution.py
@@ -15,6 +15,7 @@
 BLOCK = 34
 FEAT = NZ * BLOCK
 WIDE = 512
+REST = 384
 TILES, PR, SUB, VT = 8, 16, 4, 64
 VMEM = pltpu.CompilerParams(vmem_limit_bytes=48 * 1024 * 1024)
 F32, BF16 = jnp.float32, jnp.bfloat16
@@ -40,12 +41,13 @@
     marks = split3(mean) + split3(inverse_std)
     lane = lax.broadcasted_iota(jnp.int32, (PR, WIDE), 1)
     grad_copy.wait()
-    for sub in range(SUB):
-        for part in range(NMP):
+    for part in range(NMP):
+        rest = [jnp.zeros((PR, 128), F32), jnp.zeros((PR, 128), F32)]
+        live = lane < min(FEAT, VW - part * FEAT)
+        for sub in range(SUB):
             low = sub * VW + part * FEAT
             start = low // 128 * 128
             width = min(640, PW - start)
-            live = lane < min(FEAT, VW - part * FEAT)
             for which, ref in enumerate((grad_ref, feat_ref)):
                 window = ref[:, start : start + width].astype(F32)
                 if width < 640:
@@ -53,18 +55,39 @@
                 if low > start:
                     window = pltpu.roll(window, 640 - (low - start), 1)
                 chunk = jnp.where(live, window[:, :WIDE], 0.0)
-                if which == 1:
+                if which == 1 and sub == 0:
                     for at, mark in enumerate(marks):
                         chunk = jnp.where(lane == FEAT + at, mark, chunk)
                 row = which * VT + sub * PR
-                out_ref[part, row : row + PR, :] = chunk.astype(BF16)
+                for tile in range(3):
+                    at = tile * 2 * VT + row
+                    out_ref[part, at : at + PR, :] = chunk[:, tile * 128 : tile * 128 + 128].astype(BF16)
+                group = row // 32
+                last = chunk[:, 384:512]
+                rest[sub % 2] += pltpu.roll(last, 32 * group, 1) if group else last
+        out_ref[part, REST : REST + PR, :] = rest[0].astype(BF16)
+        out_ref[part, REST + PR : REST + 2 * PR, :] = rest[1].astype(BF16)
+
+
+def unpack(ref, tile, which):
+    at = [q * 2 * VT + which * VT for q in range(3)]
+    pieces = [ref[tile, r : r + VT, :].astype(F32) for r in at]
+    rest = ref[tile, REST : REST + 2 * PR, :].astype(F32)
+    turn = (128 - 64 * which) % 128
+    rest = jnp.concatenate(
+        [pltpu.roll(rest, turn, 1) if turn else rest, pltpu.roll(rest, (turn + 96) % 128, 1)], axis=0
+    )
+    return pieces, rest
 
 
 def slot_values(tile, source_ref, live_ref, recv_ref):
-    grads = recv_ref[source_ref[tile], 0:VT, :].astype(F32)
+    pieces, rest = unpack(recv_ref, source_ref[tile], 0)
+    rest = jnp.where(lax.broadcasted_iota(jnp.int32, (VT, 128), 1) < FEAT - 384, rest, 0.0)
+    grads = jnp.concatenate(pieces + [rest], axis=1)
     grads = jnp.where(live_ref[tile] > 0, grads, 0.0)
-    feats = recv_ref[tile, VT : 2 * VT, :].astype(F32)
-    marks = feats[0:PR, 384:512]
+    pieces, rest = unpack(recv_ref, tile, 1)
+    feats = jnp.concatenate(pieces + [rest], axis=1)
+    marks = rest[0:PR]
     lane = lax.broadcasted_iota(jnp.int32, (PR, 128), 1) + 384
     in_mean = (lane >= FEAT) & (lane < FEAT + 3)
     in_std = (lane >= FEAT + 3) & (lane < FEAT + 6)
@@ -94,12 +117,10 @@
         out_ref[part] = turned
 
 
-def dot_nt(left, right):
-    return lax.dot_general(left, right, (((1,), (1,)), ((), ())), preferred_element_type=F32)
-
-
-ROWS1, ROWS2, ROWS3, GAIN = 416, 208, 64, 16
-AT2, AT3, AT4, AT5 = ROWS1, ROWS1 + ROWS2, ROWS1 + ROWS2 + ROWS3, ROWS1 + ROWS2 + ROWS3 + GAIN
+COLS, GROUP, GAIN = 208, 48, 16
+AT1, AT2, AT3 = COLS, 2 * COLS, 3 * COLS
+AT4 = AT3 + GROUP
+AT5 = AT4 + GAIN
 MESSAGE = AT5 + GAIN
 
 
@@ -137,29 +158,26 @@
     gain = jnp.concatenate([gain[:, q * 128 : (q + 1) * 128] for q in range(4)], axis=0)
     gain_high = gain.astype(BF16)
     gain_low = (gain - gain_high.astype(F32)).astype(BF16)
-    turned = branch_ref[...].T
-    turned_ref[...] = turned[:FEAT]
     attn_copy.wait()
-    half = lax.broadcasted_iota(jnp.int32, (ROWS2, 128), 1) < 64
-    group = lax.broadcasted_iota(jnp.int32, (ROWS3, 128), 1) >> 4
     copies = []
     for part in range(NMP):
-        attn = attn_ref[part]
-        terms_ref[part, 0:AT2, :] = dot_nt(turned[:ROWS1], attn[0:128]).astype(BF16)
-        second = dot_nt(turned[:ROWS1], jnp.concatenate([attn[128:192]] * 2, axis=0))
-        second = jnp.where(half, second[:ROWS2], second[ROWS2:])
-        terms_ref[part, AT2:AT3, :] = second.astype(BF16)
-        third = dot_nt(turned[: 7 * ROWS3], jnp.concatenate([attn[192:208]] * 8, axis=0))
-        packed = third[:ROWS3]
-        for g in range(1, 7):
-            packed = jnp.where(group == g, third[g * ROWS3 : (g + 1) * ROWS3], packed)
-        terms_ref[part, AT3:AT4, :] = packed.astype(BF16)
+        term = jnp.dot(attn_ref[part], branch_ref[...], preferred_element_type=F32)
+        for q in range(3):
+            terms_ref[part, q * COLS : (q + 1) * COLS, :] = term[:, q * 128 : q * 128 + 128].astype(BF16)
+        last = term[:, 384:512]
+        rest = last[0:GROUP]
+        for g in range(1, 4):
+            rest = rest + pltpu.roll(last[g * GROUP : (g + 1) * GROUP], 24 * g, 1)
+        tail = pltpu.roll(last[4 * GROUP : COLS], 96, 1)
+        rest = jnp.concatenate([rest[0:16] + tail, rest[16:]], axis=0)
+        terms_ref[part, AT3:AT4, :] = rest.astype(BF16)
         terms_ref[part, AT4:AT5, :] = gain_high
         terms_ref[part, AT5:MESSAGE, :] = gain_low
         copies.append(
             pltpu.make_async_copy(terms_ref.at[part], terms_hbm.at[part], terms_sems.at[part])
         )
         copies[-1].start()
+    turned_ref[...] = branch_ref[...].T[:FEAT]
     for copy in copies:
         copy.wait()
 
@@ -168,14 +186,12 @@
     total = recv_ref[0].astype(F32)
     for part in range(1, NY):
         total = total + recv_ref[part].astype(F32)
-    second = total[AT2:AT3]
-    second = jnp.concatenate([second, pltpu.roll(second, 64, 1)], axis=0)
-    third = total[AT3:AT4]
-    third = [pltpu.roll(third, (64 - 16 * g) % 128, 1) if g != 4 else third for g in range(7)]
-    third = jnp.concatenate(third, axis=0)[:ROWS1]
-    lane = lax.broadcasted_iota(jnp.int32, (ROWS1, 128), 1)
-    wide_ref[:, 0:128] = total[0:ROWS1]
-    wide_ref[:, 128:256] = jnp.where(lane < 64, second, jnp.where(lane < 80, third, 0.0))
+    rest = total[AT3:AT4]
+    rest = [rest] + [pltpu.roll(rest, 128 - 24 * g, 1) for g in range(1, 5)]
+    rest = jnp.concatenate(rest[:4] + [rest[4][0:16]], axis=0)
+    wide = jnp.concatenate([total[0:AT1], total[AT1:AT2], total[AT2:AT3], rest], axis=1)
+    wide = jnp.concatenate([wide, jnp.zeros((256 - COLS, WIDE), F32)], axis=0)
+    wide_ref[...] = wide.T
     gain = total[AT4:AT5] + total[AT5:MESSAGE]
     gain = jnp.concatenate([gain[0:8], gain[8:16]], axis=1)
     for z in range(NZ):
@@ -247,7 +263,7 @@
 
     send = pl.pallas_call(
         cut_kernel,
-        out_shape=jax.ShapeDtypeStruct((NMP, 2 * VT, WIDE), BF16),
+        out_shape=jax.ShapeDtypeStruct((NMP, REST + 2 * PR, 128), BF16),
         in_specs=in_hbm(2),
         out_specs=whole(1)[0],
         scratch_shapes=[
@@ -255,7 +271,7 @@
             pltpu.VMEM((PR, PW), BF16),
             pltpu.SemaphoreType.DMA((2,)),
         ],
-        compiler_params=VMEM,
+        compiler_params=pltpu.CompilerParams(vmem_limit_bytes=60 * 1024 * 1024),
         name="cut",
     )(grad_proj, saved_feat)
     recv = lax.all_to_all(send, MP, 0, 0)
@@ -308,7 +324,7 @@
         out_shape=jax.ShapeDtypeStruct((NZ, 48, 256), BF16),
         in_specs=whole(1),
         out_specs=whole(1)[0],
-        scratch_shapes=[pltpu.VMEM((ROWS1, 256), F32)],
+        scratch_shapes=[pltpu.VMEM((WIDE, 256), F32)],
         compiler_params=VMEM,
         name="fold",
     )(terms)

time: 163 us -> 161 us (0.988)
  local copies, waits for them, and re-layouts: 6.71 us -> 4.71 us
    pallas_call x1, Pallas kernels: 2.19 us -> 4.79 us  [body(): pl.pallas_call(cut_kernel, out_shape=jax.ShapeDtypeStruct((NMP, REST + 2...]
    all_to_all x1, waiting for transfers between devices: 11.9 us -> 9.78 us  [body(): recv = lax.all_to_all(send, MP, 0, 0)]
    unnamed x17 -> x13, local copies, waits for them, and re-layouts: 6.03 us -> 4.03 us
    pallas_call x1, Pallas kernels: 9.3 us -> 7.33 us  [body(): pl.pallas_call(branch_kernel, out_shape=(jax.ShapeDtypeStruct((FEAT, TILE...]
  transfers between devices with their start and end apart: 7 -> 7, of which waited for: 5 -> 5; matrix products, arithmetic and copies ran while one was open for 0% -> 0% of each run, Pallas kernels for 4% -> 6%
where the time goes in v4:
time: 161 us; the launch traced here: 160 us
  waiting for transfers between devices  49.9 us (31%)
  blocking collectives  44.3 us (28%)
  starting transfers between devices  28.9 us (18%)
  Pallas kernels  17.5 us (11%)
  between operations  14.8 us (9%)
  local copies, waits for them, and re-layouts  4.71 us (3%)
    all_to_all x1, blocking collectives, body(): terms = lax.all_to_all(terms, 'y', 0, 0)  44.3 us
    ppermute x1, waiting for transfers between devices, body(): proj_grad = lax.ppermute(part, DP + MP, last_places())  16 us
    all_to_all x1, waiting for transfers between devices, body(): terms = lax.all_to_all(terms, 'z', 0, 0)  12.2 us
    all_to_all x1, starting transfers between devices, body(): terms = lax.all_to_all(terms, 'z', 0, 0)  10.9 us
    all_to_all x1, waiting for transfers between devices, body(): recv = lax.all_to_all(send, MP, 0, 0)  9.78 us
    all_gather x1, waiting for transfers between devices, body(): attn = lax.all_gather(attn_saved.T, MP, axis=0)  8.27 us
    pallas_call x1, Pallas kernels, body(): pl.pallas_call(branch_kernel, out_shape=(jax.ShapeDtypeStruct((FEAT, TILE...  7.33 us
    all_to_all x1, starting transfers between devices, body(): sums = lax.all_to_all(sums, MP, 0, 0)  6.42 us
  transfers between devices with their start and end apart: 7, of which 5 were waited for; matrix products, arithmetic and copies ran while one was open for 0% of the time, Pallas kernels for 6%

profile of v4, /device:TPU:68, one launch (start us, length us, event | category | flops | bytes accessed | tf_op | source)
XLA Modules:
  0.0 160.3 jit_solution(5520809640078511619)
XLA Ops:
  7.2 0.0 all-gather.6.cloned.1.call-start
  7.2 0.7 all-gather.6.cloned.1.call-update
  7.9 0.0 copy-start.4
  7.9 0.0 copy-start.5
  7.9 4.8 %cut.1 = bf16[8,416,128]{2,1,0:T(8,128)(2,1)} custom-call(bf16[16,12800]{1,0:T(8,128)(2,1)} %grad_hbm.1, bf16[16,12800]{1,0:T(8,128)(2,1)} %feat_hbm.1), custom_call_target="tpu_custom_call" | custom-call | tf_op jit(solution)/shard_map/cut/pallas_call | solution.py:264
  12.7 0.0 copy-start.3
  12.7 4.8 %all-to-all-start = ((bf16[8,416,128]{2,1,0:T(8,128)(2,1)}), bf16[8,416,128]{2,1,0:T(8,128)(2,1)S(1)}, u32[]{:S(2)}, u32[]{:S(2)}) async-start(bf16[8,416,128]{2,1,0:T(8,128)(2,1)} %cut.1), calls=%async_computation | async-start | bytes 1703936 | tf_op jit(solution)/shard_map/all_to_all | solution.py:277
  18.2 0.0 copy-done.4
  18.3 0.0 copy-done.5
  18.3 0.1 select_reduce_fusion.source_ref
  18.4 0.1 fusion.gain_ref
  18.5 9.8 %all-to-all-done.recv_ref = bf16[8,416,128]{2,1,0:T(8,128)(2,1)S(1)} async-done(((bf16[8,416,128]{2,1,0:T(8,128)(2,1)}), bf16[8,416,128]{2,1,0:T(8,128)(2,1)S(1)}, u32[]{:S(2)}, u32[]{:S(2)}) %all-to-all-start) | async-done | bytes 852000 | tf_op jit(solution)/shard_map/all_to_all | solution.py:277
  28.3 1.9 %sums.1 = f32[8,8,128]{2,1,0:T(8,128)} custom-call(s32[8]{0:T(128)S(1)} %select_reduce_fusion.source_ref, s32[8]{0:T(128)S(1)} %compare_convert_fusion.live_ref, bf16[8,416,128]{2,1,0:T(8,128)(2,1)S(1)} %all-to-all-done.recv_ref, f32[4,512]{1,0:T(4,128)S(1)} %fusion.gain_ref), custom_call_target="tpu_custom_call" | custom-call | tf_op jit(solution)/shard_map/sums/pallas_call | solution.py:292
  30.2 6.4 %all-to-all-start.1 = ((f32[8,8,128]{2,1,0:T(8,128)}), f32[8,8,128]{2,1,0:T(8,128)S(1)}, u32[]{:S(2)}, u32[]{:S(2)}) async-start(f32[8,8,128]{2,1,0:T(8,128)} %sums.1), calls=%async_computation.1 | async-start | bytes 65536 | tf_op jit(solution)/shard_map/all_to_all | solution.py:300
  36.6 0.0 all-gather.4.cloned.1.call-start
  36.6 0.0 copy-done.3
  36.6 0.1 fusion.1
  36.7 2.9 %all-to-all-done.1.sums_ref = f32[8,8,128]{2,1,0:T(8,128)S(1)} async-done(((f32[8,8,128]{2,1,0:T(8,128)}), f32[8,8,128]{2,1,0:T(8,128)S(1)}, u32[]{:S(2)}, u32[]{:S(2)}) %all-to-all-start.1) | async-done | bytes 32800 | tf_op jit(solution)/shard_map/all_to_all | solution.py:300
  39.6 8.3 %all-gather.6.cloned.1.call-done = bf16[1664,512]{1,0:T(8,128)(2,1)} async-done(((bf16[208,512]{1,0:T(8,128)(2,1)}), bf16[1664,512]{1,0:T(8,128)(2,1)}) %all-gather.6.cloned.1.call-update) | async-done | bytes 1703952 | tf_op jit(solution)/shard_map/all_gather | solution.py:262
  47.9 0.0 copy-start.1
  47.9 1.5 copy-done.1
  49.4 7.3 %branch.1 = (bf16[408,512]{1,0:T(8,128)(2,1)}, bf16[8,704,128]{2,1,0:T(8,128)(2,1)S(1)}) custom-call(s32[8]{0:T(128)S(1)} %select_reduce_fusion.source_ref, s32[8]{0:T(128)S(1)} %compare_convert_fusion.live_ref, bf16[8,416,128]{2,1,0:T(8,128)(2,1)S(1)} %all-to-all-done.recv_ref, f32[4,512]{1,0:T(4,128)S(1)} %fusion.gain_ref, f32[1,512]{1,0:T(1,128)S(1)} %bitcast.11, ...), custom_call_target="tpu_custom_call" | custom-call | tf_op jit(solution)/shard_map/branch/pallas_call | solution.py:302
  56.7 0.0 all-gather.4.cloned.1.call-update
  56.7 44.3 %all_to_all.25.recv_ref = bf16[8,704,128]{2,1,0:T(8,128)(2,1)S(1)} all-to-all(bf16[8,704,128]{2,1,0:T(8,128)(2,1)S(1)} %get-tuple-element.13), channel_id=1, replica_groups=mesh['z'=12,'y'=8,'x'=4,'c'=2] {'y'}, dimensions={0} | all-to-all | bytes 2883584 | tf_op jit(solution)/shard_map/all_to_all | solution.py:321
  101.0 0.0 copy-start.2
  101.0 1.0 fold.1
  102.0 10.9 %all-to-all-start.3 = ((bf16[12,48,256]{2,1,0:T(8,128)(2,1)}), bf16[12,48,256]{2,1,0:T(8,128)(2,1)S(1)}, u32[]{:S(2)}, u32[]{:S(2)}) async-start(bf16[12,48,256]{2,1,0:T(8,128)(2,1)} %fold.1), calls=%async_computation.3 | async-start | bytes 589824 | tf_op jit(solution)/shard_map/all_to_all | solution.py:331
  112.9 0.0 all-gather.4.cloned.1.call-done.turned_ref
  112.9 0.0 copy-done.2
  112.9 0.0 copy-start
  112.9 1.9 %copy-done = bf16[3264,512]{1,0:T(8,128)(2,1)S(1)} copy-done((bf16[3264,512]{1,0:T(8,128)(2,1)S(1)}, bf16[3264,512]{1,0:T(8,128)(2,1)}, u32[]{:S(2)}) %copy-start) | copy-done | bytes 3342360
  114.9 1.7 %gathered.1 = (bf16[208,512]{1,0:T(8,128)(2,1)}, bf16[64,3200]{1,0:T(8,128)(2,1)}) custom-call(s32[1]{0:T(128)} %bitcast.5.own_ref, bf16[3264,512]{1,0:T(8,128)(2,1)S(1)} %copy-done, bf16[208,3200]{1,0:T(8,128)(2,1)S(1)} %bitcast.10, f32[1,3200]{1,0:T(1,128)S(1)} %broadcast_in_dim.44.scale_ref), custom_call_target="tpu_custom_call" | custom-call | tf_op jit(solution)/shard_map/gathered/pallas_call | solution.py:334
  116.6 12.2 %all-to-all-done.3.recv_ref = bf16[12,48,256]{2,1,0:T(8,128)(2,1)S(1)} async-done(((bf16[12,48,256]{2,1,0:T(8,128)(2,1)}), bf16[12,48,256]{2,1,0:T(8,128)(2,1)S(1)}, u32[]{:S(2)}, u32[]{:S(2)}) %all-to-all-start.3) | async-done | bytes 294944 | tf_op jit(solution)/shard_map/all_to_all | solution.py:331
  128.7 0.6 settle.1
  129.4 4.8 %all-to-all-start.4 = ((f32[8,16,128]{2,1,0:T(8,128)}), f32[8,16,128]{2,1,0:T(8,128)S(1)}, u32[]{:S(2)}, u32[]{:S(2)}) async-start(f32[8,16,128]{2,1,0:T(8,128)} %get-tuple-element.21), calls=%async_computation.4 | async-start | bytes 131072 | tf_op jit(solution)/shard_map/all_to_all | solution.py:360
  134.2 1.9 %collective-permute-start = (f32[34,208]{1,0:T(8,128)S(1)}, f32[34,208]{1,0:T(8,128)S(1)}, u32[]{:S(2)}, u32[]{:S(2)}) collective-permute-start(f32[34,208]{1,0:T(8,128)S(1)} %get-tuple-element.20), channel_id=1, source_target_pairs={{0,0},{1,96},{2,192},{3,288},{4,384},{5,480},{6,576},{7,672},{8,1}... | collective-permute-start | bytes 84872 | tf_op jit(solution)/shard_map/ppermute | solution.py:359
  136.1 16.0 %collective-permute-done = f32[34,208]{1,0:T(8,128)S(1)} collective-permute-done((f32[34,208]{1,0:T(8,128)S(1)}, f32[34,208]{1,0:T(8,128)S(1)}, u32[]{:S(2)}, u32[]{:S(2)}) %collective-permute-start) | collective-permute-done | bytes 28320 | tf_op jit(solution)/shard_map/ppermute | solution.py:359
  152.1 0.0 all-to-all-done.4.gain_ref
  152.1 0.1 spread.1
  152.2 0.6 reshape.21
  152.9 0.6 copy.14
  (4 shorter events, 0.0 us)
Async XLA Ops:
  7.2 40.8 %all-gather.6.cloned.1.call-start = ((), (), s32[]{:S(2)}) async-start(), calls=%async_computation.6 | async-start | bytes 1916928 | tf_op jit(solution)/shard_map/all_gather | solution.py:262
  7.9 10.3 %copy-start.4 = (f32[12800]{0:T(1024)S(1)}, f32[12800]{0:T(1024)}, u32[]{:S(2)}) copy-start(f32[12800]{0:T(1024)} %param.12) | copy-start | bytes 153604
  7.9 10.3 %copy-start.5 = (s32[1,8]{1,0:T(1,128)S(1)}, s32[1,8]{1,0:T(1,128)}, u32[]{:S(2)}) copy-start(s32[1,8]{1,0:T(1,128)} %param.10) | copy-start | bytes 100
  12.7 23.9 %copy-start.3 = (f32[3200]{0:T(1024)S(1)}, f32[3200]{0:T(1024)}, u32[]{:S(2)}) copy-start(f32[3200]{0:T(1024)} %param.13) | copy-start | bytes 38404
  12.7 15.5 %all-to-all-start = ((bf16[8,416,128]{2,1,0:T(8,128)(2,1)}), bf16[8,416,128]{2,1,0:T(8,128)(2,1)S(1)}, u32[]{:S(2)}, u32[]{:S(2)}) async-start(bf16[8,416,128]{2,1,0:T(8,128)(2,1)} %cut.1), calls=%async_computation | async-start | bytes 1703936 | tf_op jit(solution)/shard_map/all_to_all | solution.py:277
  30.2 9.4 %all-to-all-start.1 = ((f32[8,8,128]{2,1,0:T(8,128)}), f32[8,8,128]{2,1,0:T(8,128)S(1)}, u32[]{:S(2)}, u32[]{:S(2)}) async-start(f32[8,8,128]{2,1,0:T(8,128)} %sums.1), calls=%async_computation.1 | async-start | bytes 65536 | tf_op jit(solution)/shard_map/all_to_all | solution.py:300
  36.6 76.3 %all-gather.4.cloned.1.call-start = ((), (), s32[]{:S(2)}) async-start(), calls=%async_computation.5 | async-start | bytes 3760128 | tf_op jit(solution)/shard_map/all_gather | solution.py:333
  47.9 1.5 copy-start.1
  101.0 11.9 %copy-start.2 = (bf16[3200,208]{0,1:T(8,128)(2,1)S(1)}, bf16[3200,208]{0,1:T(8,128)(2,1)}, u32[]{:S(2)}) copy-start(bf16[3200,208]{0,1:T(8,128)(2,1)} %param.15) | copy-start | bytes 3993604
  102.0 26.7 %all-to-all-start.3 = ((bf16[12,48,256]{2,1,0:T(8,128)(2,1)}), bf16[12,48,256]{2,1,0:T(8,128)(2,1)S(1)}, u32[]{:S(2)}, u32[]{:S(2)}) async-start(bf16[12,48,256]{2,1,0:T(8,128)(2,1)} %fold.1), calls=%async_computation.3 | async-start | bytes 589824 | tf_op jit(solution)/shard_map/all_to_all | solution.py:331
  112.9 1.9 %copy-start = (bf16[3264,512]{1,0:T(8,128)(2,1)S(1)}, bf16[3264,512]{1,0:T(8,128)(2,1)}, u32[]{:S(2)}) copy-start(bf16[3264,512]{1,0:T(8,128)(2,1)} %all-gather.4.cloned.1.call-done.turned_ref) | copy-start | bytes 10027012
  129.4 22.7 %all-to-all-start.4 = ((f32[8,16,128]{2,1,0:T(8,128)}), f32[8,16,128]{2,1,0:T(8,128)S(1)}, u32[]{:S(2)}, u32[]{:S(2)}) async-start(f32[8,16,128]{2,1,0:T(8,128)} %get-tuple-element.21), calls=%async_computation.4 | async-start | bytes 131072 | tf_op jit(solution)/shard_map/all_to_all | solution.py:360
  134.2 17.9 %collective-permute-start = (f32[34,208]{1,0:T(8,128)S(1)}, f32[34,208]{1,0:T(8,128)S(1)}, u32[]{:S(2)}, u32[]{:S(2)}) collective-permute-start(f32[34,208]{1,0:T(8,128)S(1)} %get-tuple-element.20), channel_id=1, source_target_pairs={{0,0},{1,96},{2,192},{3,288},{4,384},{5,480},{6,576},{7,672},{8,1}... | collective-permute-start | bytes 84872 | tf_op jit(solution)/shard_map/ppermute | solution.py:359
Sparse Core Ops, SparseCore 0:
  10.4 37.4 all-gather.5
  56.9 37.1 all-gather.3

commit v5 on v4

--- a/solution.py
+++ b/solution.py
@@ -15,6 +15,7 @@
 BLOCK = 34
 FEAT = NZ * BLOCK
 WIDE = 512
+ROWS = 416
 REST = 384
 TILES, PR, SUB, VT = 8, 16, 4, 64
 VMEM = pltpu.CompilerParams(vmem_limit_bytes=48 * 1024 * 1024)
@@ -125,11 +126,9 @@
 
 
 def branch_kernel(
-    source_ref, live_ref, recv_ref, gain_ref, scale_ref, sums_ref, attn_hbm,
-    turned_ref, terms_hbm, attn_ref, terms_ref, branch_ref, attn_sem, terms_sems,
+    source_ref, live_ref, parts_ref, recv_ref, gain_ref, scale_ref, sums_ref,
+    own_ref, before_ref, after_ref, far_ref, other_ref, turned_ref, terms_ref, branch_ref,
 ):
-    attn_copy = pltpu.make_async_copy(attn_hbm, attn_ref, attn_sem)
-    attn_copy.start()
     total = sums_ref[0]
     for part in range(1, NMP):
         total = total + sums_ref[part]
@@ -158,10 +157,10 @@
     gain = jnp.concatenate([gain[:, q * 128 : (q + 1) * 128] for q in range(4)], axis=0)
     gain_high = gain.astype(BF16)
     gain_low = (gain - gain_high.astype(F32)).astype(BF16)
-    attn_copy.wait()
-    copies = []
-    for part in range(NMP):
-        term = jnp.dot(attn_ref[part], branch_ref[...], preferred_element_type=F32)
+    attns = [own_ref, before_ref, after_ref, far_ref] + [other_ref.at[p] for p in range(4)]
+    for place, attn in enumerate(attns):
+        part = parts_ref[place]
+        term = jnp.dot(attn[...], branch_ref[...], preferred_element_type=F32)
         for q in range(3):
             terms_ref[part, q * COLS : (q + 1) * COLS, :] = term[:, q * 128 : q * 128 + 128].astype(BF16)
         last = term[:, 384:512]
@@ -173,13 +172,7 @@
         terms_ref[part, AT3:AT4, :] = rest.astype(BF16)
         terms_ref[part, AT4:AT5, :] = gain_high
         terms_ref[part, AT5:MESSAGE, :] = gain_low
-        copies.append(
-            pltpu.make_async_copy(terms_ref.at[part], terms_hbm.at[part], terms_sems.at[part])
-        )
-        copies[-1].start()
-    turned_ref[...] = branch_ref[...].T[:FEAT]
-    for copy in copies:
-        copy.wait()
+    turned_ref[...] = branch_ref[...].T[:ROWS]
 
 
 def fold_kernel(recv_ref, out_ref, wide_ref):
@@ -223,13 +216,33 @@
     out_ref[...] = wide_ref[:, 0:VW]
 
 
-def gathered_kernel(own_ref, turned_ref, weight_ref, scale_ref, attn_ref, residual_ref):
-    attn = jnp.dot(weight_ref[...], turned_ref[0:VW, :], preferred_element_type=F32)
-    attn_ref[...] = attn.astype(BF16)
-    own = own_ref[0]
-    at = pl.multiple_of((own >> 1) * 128, 128)
-    tokens = turned_ref[0:VW, pl.ds(at, 128)].astype(F32).T
-    tokens = jnp.where((own & 1) == 0, tokens[0:VT], tokens[VT : 2 * VT])
+def gathered_kernel(
+    tile_ref, parts_ref, weight_ref, scale_ref, own_ref, before_ref, after_ref, far_ref, other_ref,
+    attn_ref, residual_ref, all_ref,
+):
+    pieces = [own_ref, before_ref, after_ref, far_ref] + [other_ref.at[p] for p in range(4)]
+    for place, piece in enumerate(pieces):
+        all_ref[parts_ref[place]] = piece[...]
+    tile = tile_ref[0]
+    at = pl.multiple_of((tile >> 1) * 128, 128)
+    lane = lax.broadcasted_iota(jnp.int32, (COLS, WIDE), 1)
+    total = jnp.zeros((COLS, TILES * VT), F32)
+    tokens = []
+    for part in range(NMP):
+        low = part * FEAT
+        start = low // 128 * 128
+        width = min(640, VW - start)
+        weight = weight_ref[:, start : start + width].astype(F32)
+        if width < 640:
+            weight = jnp.concatenate([weight, jnp.zeros((COLS, 640 - width), F32)], axis=1)
+        if low > start:
+            weight = pltpu.roll(weight, 640 - (low - start), 1)
+        weight = jnp.where(lane < min(FEAT, VW - low), weight[:, :WIDE], 0.0).astype(BF16)
+        total += jnp.dot(weight[:, :ROWS], all_ref[part], preferred_element_type=F32)
+        tokens.append(all_ref[part, :, pl.ds(at, 128)].astype(F32)[:FEAT])
+    attn_ref[...] = total.astype(BF16)
+    tokens = jnp.concatenate(tokens, axis=0)[:VW].T
+    tokens = jnp.where((tile & 1) == 0, tokens[0:VT], tokens[VT : 2 * VT])
     residual_ref[...] = (tokens / scale_ref[...]).astype(BF16)
 
 
@@ -239,6 +252,14 @@
 
 def scalars(count):
     return [pl.BlockSpec(memory_space=pltpu.SMEM)] * count
+
+
+def gather(own):
+    before, after, far = (
+        lax.ppermute(own, "x", [(x, (x + step) % 4) for x in range(4)]) for step in (1, 3, 2)
+    )
+    other = lax.ppermute(jnp.stack([own, before, after, far]), "c", [(0, 1), (1, 0)])
+    return own, before, after, far, other
 
 
 def last_places():
@@ -259,8 +280,6 @@
 ):
     mp_index = lax.axis_index(MP)
     cols = attn_saved.shape[1]
-    attn = lax.all_gather(attn_saved.T, MP, axis=0)
-
     send = pl.pallas_call(
         cut_kernel,
         out_shape=jax.ShapeDtypeStruct((NMP, REST + 2 * PR, 128), BF16),
@@ -274,7 +293,12 @@
         compiler_params=pltpu.CompilerParams(vmem_limit_bytes=60 * 1024 * 1024),
         name="cut",
     )(grad_proj, saved_feat)
+    attn_own, send = lax.optimization_barrier((attn_saved.T, send))
     recv = lax.all_to_all(send, MP, 0, 0)
+    attns = gather(attn_own)
+    x_index, c_index = lax.axis_index("x"), lax.axis_index("c")
+    near = jnp.stack([x_index, (x_index + 3) % 4, (x_index + 1) % 4, (x_index + 2) % 4]) * 2
+    parts = jnp.concatenate([near + c_index, near + 1 - c_index]).astype(jnp.int32)
 
     slot_ids = jnp.arange(TILES, dtype=jnp.int32)
     matches = tile_home[0][None, :] == slot_ids[:, None]
@@ -302,21 +326,15 @@
     turned, terms = pl.pallas_call(
         branch_kernel,
         out_shape=(
-            jax.ShapeDtypeStruct((FEAT, TILES * VT), BF16),
+            jax.ShapeDtypeStruct((ROWS, TILES * VT), BF16),
             jax.ShapeDtypeStruct((NMP, MESSAGE, 128), BF16),
         ),
-        in_specs=scalars(2) + whole(4) + in_hbm(1),
-        out_specs=(whole(1)[0], in_hbm(1)[0]),
-        scratch_shapes=[
-            pltpu.VMEM((NMP, cols, TILES * VT), BF16),
-            pltpu.VMEM((NMP, MESSAGE, 128), BF16),
-            pltpu.VMEM((TILES * VT, WIDE), BF16),
-            pltpu.SemaphoreType.DMA,
-            pltpu.SemaphoreType.DMA((NMP,)),
-        ],
+        in_specs=scalars(3) + whole(9),
+        out_specs=tuple(whole(2)),
+        scratch_shapes=[pltpu.VMEM((TILES * VT, WIDE), BF16)],
         compiler_params=VMEM,
         name="branch",
-    )(source, live, recv, gain, scale, sums, attn)
+    )(source, live, parts, recv, gain, scale, sums, *attns)
 
     terms = lax.all_to_all(terms, "y", 0, 0)
     terms = pl.pallas_call(
@@ -330,18 +348,19 @@
     )(terms)
     terms = lax.all_to_all(terms, "z", 0, 0)
 
-    turned = lax.all_gather(turned, MP, axis=0, tiled=True)
+    turned = gather(turned)
     attn_grad, residual_grad = pl.pallas_call(
         gathered_kernel,
         out_shape=(
             jax.ShapeDtypeStruct((cols, TILES * VT), BF16),
             jax.ShapeDtypeStruct((VT, VW), BF16),
         ),
-        in_specs=scalars(1) + whole(3),
+        in_specs=scalars(2) + whole(7),
         out_specs=tuple(whole(2)),
+        scratch_shapes=[pltpu.VMEM((NMP, ROWS, TILES * VT), BF16)],
         compiler_params=VMEM,
         name="gathered",
-    )(mp_index.astype(jnp.int32)[None], turned, proj_weight.T, layer_scale[None])
+    )(mp_index.astype(jnp.int32)[None], parts, proj_weight.T, layer_scale[None], *turned)
 
     terms, attn_grad, residual_grad = lax.optimization_barrier((terms, attn_grad, residual_grad))
     part, gains = pl.pallas_call(

time: 161 us -> 148 us (0.919)
  blocking collectives: 44.3 us -> 0 us
  starting transfers between devices: 28.9 us -> 65 us
  between operations: 14.8 us -> 1.54 us
  waiting for transfers between devices: 49.9 us -> 56.1 us
  Pallas kernels: 17.5 us -> 14.8 us
  other arithmetic: 0.3 us -> 2.95 us
  local copies, waits for them, and re-layouts: 4.71 us -> 6.67 us
    all_to_all x1 -> x0, blocking collectives: 44.3 us -> none  [body(): terms = lax.all_to_all(terms, 'y', 0, 0)]
    ppermute x0 -> x8, starting transfers between devices: none -> 22.5 us  [the longest x6 18.6 us: gather(): lax.ppermute(own, 'x', [(x, (x + step) % 4) for x in range(4)])]
    ppermute x0 -> x8, waiting for transfers between devices: none -> 13.7 us  [the longest x6 13.7 us: gather(): lax.ppermute(own, 'x', [(x, (x + step) % 4) for x in range(4)])]
    all_to_all x0 -> x1, waiting for transfers between devices: none -> 9.83 us  [body(): terms = lax.all_to_all(terms, 'y', 0, 0)]
    all_gather x2 -> x0, waiting for transfers between devices: 8.29 us -> none  [the longest x1 8.27 us: body(): attn = lax.all_gather(attn_saved.T, MP, axis=0)]
    all_to_all x0 -> x1, starting transfers between devices: none -> 7.1 us  [body(): terms = lax.all_to_all(terms, 'y', 0, 0)]
    all_to_all x1, waiting for transfers between devices: 12.2 us -> 6.86 us  [body(): terms = lax.all_to_all(terms, 'z', 0, 0)]
    all_to_all x1, starting transfers between devices: 10.9 us -> 14.8 us  [body(): terms = lax.all_to_all(terms, 'z', 0, 0)]
  transfers between devices with their start and end apart: 7 -> 14, of which waited for: 5 -> 7; matrix products, arithmetic and copies ran while one was open for 0% -> 2% of each run, Pallas kernels for 6% -> 4%
where the time goes in v5:
time: 148 us; the launch traced here: 147 us
  starting transfers between devices  65 us (44%)
  waiting for transfers between devices  56.1 us (38%)
  Pallas kernels  14.8 us (10%)
  local copies, waits for them, and re-layouts  6.67 us (5%)
  other arithmetic  2.95 us (2%)
  between operations  1.54 us (1%)
    ppermute x6, starting transfers between devices, gather(): lax.ppermute(own, 'x', [(x, (x + step) % 4) for x in range(4)])  18.6 us
    ppermute x1, waiting for transfers between devices, body(): proj_grad = lax.ppermute(part, DP + MP, last_places())  16.3 us
    all_to_all x1, starting transfers between devices, body(): terms = lax.all_to_all(terms, 'z', 0, 0)  14.8 us
    ppermute x6, waiting for transfers between devices, gather(): lax.ppermute(own, 'x', [(x, (x + step) % 4) for x in range(4)])  13.7 us
    all_to_all x1, waiting for transfers between devices, body(): terms = lax.all_to_all(terms, 'y', 0, 0)  9.83 us
    all_to_all x1, starting transfers between devices, body(): terms = lax.all_to_all(terms, 'y', 0, 0)  7.1 us
    all_to_all x1, waiting for transfers between devices, body(): terms = lax.all_to_all(terms, 'z', 0, 0)  6.86 us
    all_to_all x1, starting transfers between devices, body(): recv = lax.all_to_all(send, MP, 0, 0)  6.52 us
  transfers between devices with their start and end apart: 14, of which 7 were waited for; matrix products, arithmetic and copies ran while one was open for 2% of the time, Pallas kernels for 4%

profile of v5, /device:TPU:68, one launch (start us, length us, event | category | flops | bytes accessed | tf_op | source)
XLA Modules:
  0.0 147.0 jit_solution(5201622493624362858)
XLA Ops:
  0.6 0.0 copy-start.9
  0.7 4.8 %cut.1 = bf16[8,416,128]{2,1,0:T(8,128)(2,1)} custom-call(bf16[16,12800]{1,0:T(8,128)(2,1)} %grad_hbm.1, bf16[16,12800]{1,0:T(8,128)(2,1)} %feat_hbm.1), custom_call_target="tpu_custom_call" | custom-call | tf_op jit(solution)/shard_map/cut/pallas_call | solution.py:283
  5.5 2.4 %collective-permute-start.2 = (bf16[208,512]{1,0:T(8,128)(2,1)}, bf16[208,512]{1,0:T(8,128)(2,1)S(1)}, u32[]{:S(2)}, u32[]{:S(2)}) collective-permute-start(bf16[208,512]{1,0:T(8,128)(2,1)} %bitcast.25), channel_id=1, source_target_pairs={{0,4},{2,6},{4,0},{6,2},{1,5},{3,7},{5,1},{7,3},{8,12},{10,14},{12... | collective-permute-start | bytes 638984 | tf_op jit(solution)/shard_map/ppermute | solution.py:259
  7.9 4.1 %collective-permute-start.1 = (bf16[208,512]{1,0:T(8,128)(2,1)}, bf16[208,512]{1,0:T(8,128)(2,1)S(1)}, u32[]{:S(2)}, u32[]{:S(2)}) collective-permute-start(bf16[208,512]{1,0:T(8,128)(2,1)} %bitcast.26), channel_id=1, source_target_pairs={{0,6},{2,0},{4,2},{6,4},{1,7},{3,1},{5,3},{7,5},{8,14},{10,8},{12,... | collective-permute-start | bytes 638984 | tf_op jit(solution)/shard_map/ppermute | solution.py:259
  12.0 1.9 %collective-permute-start = (bf16[208,512]{1,0:T(8,128)(2,1)}, bf16[208,512]{1,0:T(8,128)(2,1)S(1)}, u32[]{:S(2)}, u32[]{:S(2)}) collective-permute-start(bf16[208,512]{1,0:T(8,128)(2,1)} %bitcast.27), channel_id=1, source_target_pairs={{0,2},{2,4},{4,6},{6,0},{1,3},{3,5},{5,7},{7,1},{8,10},{10,12},{12... | collective-permute-start | bytes 638984 | tf_op jit(solution)/shard_map/ppermute | solution.py:259
  13.9 6.5 %all-to-all-start = ((bf16[8,416,128]{2,1,0:T(8,128)(2,1)}), bf16[8,416,128]{2,1,0:T(8,128)(2,1)S(1)}, u32[]{:S(2)}, u32[]{:S(2)}) async-start(bf16[8,416,128]{2,1,0:T(8,128)(2,1)} %cut.1), calls=%async_computation | async-start | bytes 1703936 | tf_op jit(solution)/shard_map/all_to_all | solution.py:297
  21.1 0.1 fusion.1
  21.2 0.1 broadcast_add_fusion
  21.3 0.1 select_reduce_fusion.source_ref
  21.4 0.0 collective-permute-done.2.far_ref
  21.4 0.0 collective-permute-done.1.after_ref
  21.4 1.0 pad_maximum_fusion.1
  22.5 2.0 %collective-permute-start.3 = (bf16[4,208,512]{2,1,0:T(8,128)(2,1)}, bf16[4,208,512]{2,1,0:T(8,128)(2,1)S(1)}, u32[]{:S(2)}, u32[]{:S(2)}) collective-permute-start(bf16[4,208,512]{2,1,0:T(8,128)(2,1)} %pad_maximum_fusion.1), channel_id=1, source_target_pairs={{0,1},{1,0},{2,3},{3,2},{4,5},{5,4},{6,7},{7,6},{8,9},{9,8},{10,11... | collective-permute-start | bytes 2555912 | tf_op jit(solution)/shard_map/ppermute | solution.py:261
  24.6 0.1 fusion.gain_ref
  24.7 6.4 %all-to-all-done.recv_ref = bf16[8,416,128]{2,1,0:T(8,128)(2,1)S(1)} async-done(((bf16[8,416,128]{2,1,0:T(8,128)(2,1)}), bf16[8,416,128]{2,1,0:T(8,128)(2,1)S(1)}, u32[]{:S(2)}, u32[]{:S(2)}) %all-to-all-start) | async-done | bytes 852000 | tf_op jit(solution)/shard_map/all_to_all | solution.py:297
  31.1 2.0 %sums.1 = f32[8,8,128]{2,1,0:T(8,128)} custom-call(s32[8]{0:T(128)S(1)} %select_reduce_fusion.source_ref, s32[8]{0:T(128)S(1)} %compare_convert_fusion.live_ref, bf16[8,416,128]{2,1,0:T(8,128)(2,1)S(1)} %all-to-all-done.recv_ref, f32[4,512]{1,0:T(4,128)S(1)} %fusion.gain_ref), custom_call_target="tpu_custom_call" | custom-call | tf_op jit(solution)/shard_map/sums/pallas_call | solution.py:316
  33.1 6.4 %all-to-all-start.1 = ((f32[8,8,128]{2,1,0:T(8,128)}), f32[8,8,128]{2,1,0:T(8,128)S(1)}, u32[]{:S(2)}, u32[]{:S(2)}) async-start(f32[8,8,128]{2,1,0:T(8,128)} %sums.1), calls=%async_computation.1 | async-start | bytes 65536 | tf_op jit(solution)/shard_map/all_to_all | solution.py:324
  39.5 0.1 pad_add_fusion.parts_ref
  39.6 2.9 %all-to-all-done.1.sums_ref = f32[8,8,128]{2,1,0:T(8,128)S(1)} async-done(((f32[8,8,128]{2,1,0:T(8,128)}), f32[8,8,128]{2,1,0:T(8,128)S(1)}, u32[]{:S(2)}, u32[]{:S(2)}) %all-to-all-start.1) | async-done | bytes 32800 | tf_op jit(solution)/shard_map/all_to_all | solution.py:324
  42.5 0.0 collective-permute-done.3.other_ref
  42.5 3.6 %branch.1 = (bf16[416,512]{1,0:T(8,128)(2,1)S(1)}, bf16[8,704,128]{2,1,0:T(8,128)(2,1)}) custom-call(s32[8]{0:T(128)S(1)} %select_reduce_fusion.source_ref, s32[8]{0:T(128)S(1)} %compare_convert_fusion.live_ref, s32[8]{0:T(128)S(1)} %pad_add_fusion.parts_ref, bf16[8,416,128]{2,1,0:T(8,128)(2,1)S(1)} %all-to-all-done.recv_ref, f32[4,512]{1,0:T(4,128)S(1)} %fusion.gain_ref, ...), custom_call_target="tpu_custom_call" | custom-call | tf_op jit(solution)/shard_map/branch/pallas_call | solution.py:326
  46.1 7.1 %all-to-all-start.2 = ((bf16[8,704,128]{2,1,0:T(8,128)(2,1)}), bf16[8,704,128]{2,1,0:T(8,128)(2,1)S(1)}, u32[]{:S(2)}, u32[]{:S(2)}) async-start(bf16[8,704,128]{2,1,0:T(8,128)(2,1)} %get-tuple-element.17), calls=%async_computation.2 | async-start | bytes 2883584 | tf_op jit(solution)/shard_map/all_to_all | solution.py:339
  53.2 4.3 %collective-permute-start.6 = (bf16[416,512]{1,0:T(8,128)(2,1)S(1)}, bf16[416,512]{1,0:T(8,128)(2,1)S(1)}, u32[]{:S(2)}, u32[]{:S(2)}) collective-permute-start(bf16[416,512]{1,0:T(8,128)(2,1)S(1)} %get-tuple-element.18.own_ref), channel_id=1, source_target_pairs={{0,4},{2,6},{4,0},{6,2},{1,5},{3,7},{5,1},{7,3},{8,12},{10,14},{12... | collective-permute-start | bytes 1277960 | tf_op jit(solution)/shard_map/ppermute | solution.py:259
  57.6 2.5 %collective-permute-start.5 = (bf16[416,512]{1,0:T(8,128)(2,1)S(1)}, bf16[416,512]{1,0:T(8,128)(2,1)S(1)}, u32[]{:S(2)}, u32[]{:S(2)}) collective-permute-start(bf16[416,512]{1,0:T(8,128)(2,1)S(1)} %get-tuple-element.18.own_ref), channel_id=1, source_target_pairs={{0,6},{2,0},{4,2},{6,4},{1,7},{3,1},{5,3},{7,5},{8,14},{10,8},{12,... | collective-permute-start | bytes 1277960 | tf_op jit(solution)/shard_map/ppermute | solution.py:259
  60.0 3.4 %collective-permute-start.4 = (bf16[416,512]{1,0:T(8,128)(2,1)S(1)}, bf16[416,512]{1,0:T(8,128)(2,1)S(1)}, u32[]{:S(2)}, u32[]{:S(2)}) collective-permute-start(bf16[416,512]{1,0:T(8,128)(2,1)S(1)} %get-tuple-element.18.own_ref), channel_id=1, source_target_pairs={{0,2},{2,4},{4,6},{6,0},{1,3},{3,5},{5,7},{7,1},{8,10},{10,12},{12... | collective-permute-start | bytes 1277960 | tf_op jit(solution)/shard_map/ppermute | solution.py:259
  63.4 6.0 %collective-permute-done.6.far_ref = bf16[416,512]{1,0:T(8,128)(2,1)S(1)} collective-permute-done((bf16[416,512]{1,0:T(8,128)(2,1)S(1)}, bf16[416,512]{1,0:T(8,128)(2,1)S(1)}, u32[]{:S(2)}, u32[]{:S(2)}) %collective-permute-start.6) | collective-permute-done | bytes 426016 | tf_op jit(solution)/shard_map/ppermute | solution.py:259
  69.4 7.7 %collective-permute-done.5.after_ref = bf16[416,512]{1,0:T(8,128)(2,1)S(1)} collective-permute-done((bf16[416,512]{1,0:T(8,128)(2,1)S(1)}, bf16[416,512]{1,0:T(8,128)(2,1)S(1)}, u32[]{:S(2)}, u32[]{:S(2)}) %collective-permute-start.5) | collective-permute-done | bytes 426016 | tf_op jit(solution)/shard_map/ppermute | solution.py:259
  77.1 1.5 pad_maximum_fusion
  78.6 1.9 %collective-permute-start.7 = (bf16[4,416,512]{2,1,0:T(8,128)(2,1)}, bf16[4,416,512]{2,1,0:T(8,128)(2,1)S(1)}, u32[]{:S(2)}, u32[]{:S(2)}) collective-permute-start(bf16[4,416,512]{2,1,0:T(8,128)(2,1)} %pad_maximum_fusion), channel_id=1, source_target_pairs={{0,1},{1,0},{2,3},{3,2},{4,5},{5,4},{6,7},{7,6},{8,9},{9,8},{10,11... | collective-permute-start | bytes 5111816 | tf_op jit(solution)/shard_map/ppermute | solution.py:261
  80.5 9.8 %all-to-all-done.2.recv_ref = bf16[8,704,128]{2,1,0:T(8,128)(2,1)S(1)} async-done(((bf16[8,704,128]{2,1,0:T(8,128)(2,1)}), bf16[8,704,128]{2,1,0:T(8,128)(2,1)S(1)}, u32[]{:S(2)}, u32[]{:S(2)}) %all-to-all-start.2) | async-done | bytes 1441824 | tf_op jit(solution)/shard_map/all_to_all | solution.py:339
  90.3 1.0 fold.1
  91.3 14.8 %all-to-all-start.3 = ((bf16[12,48,256]{2,1,0:T(8,128)(2,1)}), bf16[12,48,256]{2,1,0:T(8,128)(2,1)S(1)}, u32[]{:S(2)}, u32[]{:S(2)}) async-start(bf16[12,48,256]{2,1,0:T(8,128)(2,1)} %fold.1), calls=%async_computation.3 | async-start | bytes 589824 | tf_op jit(solution)/shard_map/all_to_all | solution.py:349
  106.1 0.0 collective-permute-done.7.other_ref
  106.1 1.0 copy-done.1
  107.1 1.0 copy-done.3
  108.1 1.0 copy-done.5
  109.1 1.0 copy-done.7
  110.1 1.3 copy-done.8
  111.5 2.7 %gathered.1 = (bf16[208,512]{1,0:T(8,128)(2,1)}, bf16[64,3200]{1,0:T(8,128)(2,1)}) custom-call(s32[1]{0:T(128)} %bitcast.12.tile_ref, s32[8]{0:T(128)S(1)} %pad_add_fusion.parts_ref, bf16[208,3200]{1,0:T(8,128)(2,1)S(1)} %bitcast.24, f32[1,3200]{1,0:T(1,128)S(1)} %broadcast_in_dim.44.scale_ref, bf16[416,512]{1,0:T(8,128)(2,1)S(1)} %copy-done.1, ...), custom_call_target="tpu_custom_call" | custom-call | tf_op jit(solution)/shard_map/gathered/pallas_call | solution.py:352
  114.2 6.9 %all-to-all-done.3.recv_ref = bf16[12,48,256]{2,1,0:T(8,128)(2,1)S(1)} async-done(((bf16[12,48,256]{2,1,0:T(8,128)(2,1)}), bf16[12,48,256]{2,1,0:T(8,128)(2,1)S(1)}, u32[]{:S(2)}, u32[]{:S(2)}) %all-to-all-start.3) | async-done | bytes 294944 | tf_op jit(solution)/shard_map/all_to_all | solution.py:349
  121.0 0.6 settle.1
  121.7 5.7 %all-to-all-start.4 = ((f32[8,16,128]{2,1,0:T(8,128)}), f32[8,16,128]{2,1,0:T(8,128)S(1)}, u32[]{:S(2)}, u32[]{:S(2)}) async-start(f32[8,16,128]{2,1,0:T(8,128)} %get-tuple-element.25), calls=%async_computation.4 | async-start | bytes 131072 | tf_op jit(solution)/shard_map/all_to_all | solution.py:379
  127.4 1.9 %collective-permute-start.8 = (f32[34,208]{1,0:T(8,128)S(1)}, f32[34,208]{1,0:T(8,128)S(1)}, u32[]{:S(2)}, u32[]{:S(2)}) collective-permute-start(f32[34,208]{1,0:T(8,128)S(1)} %get-tuple-element.24), channel_id=1, source_target_pairs={{0,0},{1,96},{2,192},{3,288},{4,384},{5,480},{6,576},{7,672},{8,1}... | collective-permute-start | bytes 84872 | tf_op jit(solution)/shard_map/ppermute | solution.py:378
  129.3 16.3 %collective-permute-done.8 = f32[34,208]{1,0:T(8,128)S(1)} collective-permute-done((f32[34,208]{1,0:T(8,128)S(1)}, f32[34,208]{1,0:T(8,128)S(1)}, u32[]{:S(2)}, u32[]{:S(2)}) %collective-permute-start.8) | collective-permute-done | bytes 28320 | tf_op jit(solution)/shard_map/ppermute | solution.py:378
  145.6 0.0 all-to-all-done.4.gain_ref
  145.6 0.1 spread.1
  145.7 0.6 reshape.21
  146.4 0.6 copy.14
  (27 shorter events, 0.1 us)
Async XLA Ops:
  0.6 20.8 %copy-start.9 = (bf16[512,208]{0,1:T(8,128)(2,1)S(1)}, bf16[512,208]{0,1:T(8,128)(2,1)}, u32[]{:S(2)}) copy-start(bf16[512,208]{0,1:T(8,128)(2,1)} %param.14) | copy-start | bytes 638980
  0.6 20.4 %copy-start.11 = (f32[12800]{0:T(1024)S(1)}, f32[12800]{0:T(1024)}, u32[]{:S(2)}) copy-start(f32[12800]{0:T(1024)} %param.12) | copy-start | bytes 153604
  0.7 20.5 %copy-start.10 = (f32[3200]{0:T(1024)S(1)}, f32[3200]{0:T(1024)}, u32[]{:S(2)}) copy-start(f32[3200]{0:T(1024)} %param.13) | copy-start | bytes 38404
  0.7 20.6 %copy-start.12 = (s32[1,8]{1,0:T(1,128)S(1)}, s32[1,8]{1,0:T(1,128)}, u32[]{:S(2)}) copy-start(s32[1,8]{1,0:T(1,128)} %param.10) | copy-start | bytes 100
  5.5 16.0 %collective-permute-start.2 = (bf16[208,512]{1,0:T(8,128)(2,1)}, bf16[208,512]{1,0:T(8,128)(2,1)S(1)}, u32[]{:S(2)}, u32[]{:S(2)}) collective-permute-start(bf16[208,512]{1,0:T(8,128)(2,1)} %bitcast.25), channel_id=1, source_target_pairs={{0,4},{2,6},{4,0},{6,2},{1,5},{3,7},{5,1},{7,3},{8,12},{10,14},{12... | collective-permute-start | bytes 638984 | tf_op jit(solution)/shard_map/ppermute | solution.py:259
  7.9 13.5 %collective-permute-start.1 = (bf16[208,512]{1,0:T(8,128)(2,1)}, bf16[208,512]{1,0:T(8,128)(2,1)S(1)}, u32[]{:S(2)}, u32[]{:S(2)}) collective-permute-start(bf16[208,512]{1,0:T(8,128)(2,1)} %bitcast.26), channel_id=1, source_target_pairs={{0,6},{2,0},{4,2},{6,4},{1,7},{3,1},{5,3},{7,5},{8,14},{10,8},{12,... | collective-permute-start | bytes 638984 | tf_op jit(solution)/shard_map/ppermute | solution.py:259
  12.0 9.5 %collective-permute-start = (bf16[208,512]{1,0:T(8,128)(2,1)}, bf16[208,512]{1,0:T(8,128)(2,1)S(1)}, u32[]{:S(2)}, u32[]{:S(2)}) collective-permute-start(bf16[208,512]{1,0:T(8,128)(2,1)} %bitcast.27), channel_id=1, source_target_pairs={{0,2},{2,4},{4,6},{6,0},{1,3},{3,5},{5,7},{7,1},{8,10},{10,12},{12... | collective-permute-start | bytes 638984 | tf_op jit(solution)/shard_map/ppermute | solution.py:259
  13.9 17.2 %all-to-all-start = ((bf16[8,416,128]{2,1,0:T(8,128)(2,1)}), bf16[8,416,128]{2,1,0:T(8,128)(2,1)S(1)}, u32[]{:S(2)}, u32[]{:S(2)}) async-start(bf16[8,416,128]{2,1,0:T(8,128)(2,1)} %cut.1), calls=%async_computation | async-start | bytes 1703936 | tf_op jit(solution)/shard_map/all_to_all | solution.py:297
  22.5 20.0 %collective-permute-start.3 = (bf16[4,208,512]{2,1,0:T(8,128)(2,1)}, bf16[4,208,512]{2,1,0:T(8,128)(2,1)S(1)}, u32[]{:S(2)}, u32[]{:S(2)}) collective-permute-start(bf16[4,208,512]{2,1,0:T(8,128)(2,1)} %pad_maximum_fusion.1), channel_id=1, source_target_pairs={{0,1},{1,0},{2,3},{3,2},{4,5},{5,4},{6,7},{7,6},{8,9},{9,8},{10,11... | collective-permute-start | bytes 2555912 | tf_op jit(solution)/shard_map/ppermute | solution.py:261
  33.1 9.4 %all-to-all-start.1 = ((f32[8,8,128]{2,1,0:T(8,128)}), f32[8,8,128]{2,1,0:T(8,128)S(1)}, u32[]{:S(2)}, u32[]{:S(2)}) async-start(f32[8,8,128]{2,1,0:T(8,128)} %sums.1), calls=%async_computation.1 | async-start | bytes 65536 | tf_op jit(solution)/shard_map/all_to_all | solution.py:324
  46.1 31.0 %copy-start = (bf16[416,512]{1,0:T(8,128)(2,1)}, bf16[416,512]{1,0:T(8,128)(2,1)S(1)}, u32[]{:S(2)}) copy-start(bf16[416,512]{1,0:T(8,128)(2,1)S(1)} %get-tuple-element.18.own_ref) | copy-start | bytes 1277956
  46.1 44.2 %all-to-all-start.2 = ((bf16[8,704,128]{2,1,0:T(8,128)(2,1)}), bf16[8,704,128]{2,1,0:T(8,128)(2,1)S(1)}, u32[]{:S(2)}, u32[]{:S(2)}) async-start(bf16[8,704,128]{2,1,0:T(8,128)(2,1)} %get-tuple-element.17), calls=%async_computation.2 | async-start | bytes 2883584 | tf_op jit(solution)/shard_map/all_to_all | solution.py:339
  53.2 16.2 %collective-permute-start.6 = (bf16[416,512]{1,0:T(8,128)(2,1)S(1)}, bf16[416,512]{1,0:T(8,128)(2,1)S(1)}, u32[]{:S(2)}, u32[]{:S(2)}) collective-permute-start(bf16[416,512]{1,0:T(8,128)(2,1)S(1)} %get-tuple-element.18.own_ref), channel_id=1, source_target_pairs={{0,4},{2,6},{4,0},{6,2},{1,5},{3,7},{5,1},{7,3},{8,12},{10,14},{12... | collective-permute-start | bytes 1277960 | tf_op jit(solution)/shard_map/ppermute | solution.py:259
  57.6 19.5 %collective-permute-start.5 = (bf16[416,512]{1,0:T(8,128)(2,1)S(1)}, bf16[416,512]{1,0:T(8,128)(2,1)S(1)}, u32[]{:S(2)}, u32[]{:S(2)}) collective-permute-start(bf16[416,512]{1,0:T(8,128)(2,1)S(1)} %get-tuple-element.18.own_ref), channel_id=1, source_target_pairs={{0,6},{2,0},{4,2},{6,4},{1,7},{3,1},{5,3},{7,5},{8,14},{10,8},{12,... | collective-permute-start | bytes 1277960 | tf_op jit(solution)/shard_map/ppermute | solution.py:259
  60.0 17.1 %collective-permute-start.4 = (bf16[416,512]{1,0:T(8,128)(2,1)S(1)}, bf16[416,512]{1,0:T(8,128)(2,1)S(1)}, u32[]{:S(2)}, u32[]{:S(2)}) collective-permute-start(bf16[416,512]{1,0:T(8,128)(2,1)S(1)} %get-tuple-element.18.own_ref), channel_id=1, source_target_pairs={{0,2},{2,4},{4,6},{6,0},{1,3},{3,5},{5,7},{7,1},{8,10},{10,12},{12... | collective-permute-start | bytes 1277960 | tf_op jit(solution)/shard_map/ppermute | solution.py:259
  69.4 9.2 %copy-start.2 = (bf16[416,512]{1,0:T(8,128)(2,1)}, bf16[416,512]{1,0:T(8,128)(2,1)S(1)}, u32[]{:S(2)}) copy-start(bf16[416,512]{1,0:T(8,128)(2,1)S(1)} %collective-permute-done.6.far_ref) | copy-start | bytes 1277956
  77.1 1.5 %copy-start.4 = (bf16[416,512]{1,0:T(8,128)(2,1)}, bf16[416,512]{1,0:T(8,128)(2,1)S(1)}, u32[]{:S(2)}) copy-start(bf16[416,512]{1,0:T(8,128)(2,1)S(1)} %collective-permute-done.5.after_ref) | copy-start | bytes 1277956
  77.1 1.5 %copy-start.6 = (bf16[416,512]{1,0:T(8,128)(2,1)}, bf16[416,512]{1,0:T(8,128)(2,1)S(1)}, u32[]{:S(2)}) copy-start(bf16[416,512]{1,0:T(8,128)(2,1)S(1)} %collective-permute-done.4.before_ref) | copy-start | bytes 1277956
  78.6 27.5 %collective-permute-start.7 = (bf16[4,416,512]{2,1,0:T(8,128)(2,1)}, bf16[4,416,512]{2,1,0:T(8,128)(2,1)S(1)}, u32[]{:S(2)}, u32[]{:S(2)}) collective-permute-start(bf16[4,416,512]{2,1,0:T(8,128)(2,1)} %pad_maximum_fusion), channel_id=1, source_target_pairs={{0,1},{1,0},{2,3},{3,2},{4,5},{5,4},{6,7},{7,6},{8,9},{9,8},{10,11... | collective-permute-start | bytes 5111816 | tf_op jit(solution)/shard_map/ppermute | solution.py:261
  91.3 29.7 %all-to-all-start.3 = ((bf16[12,48,256]{2,1,0:T(8,128)(2,1)}), bf16[12,48,256]{2,1,0:T(8,128)(2,1)S(1)}, u32[]{:S(2)}, u32[]{:S(2)}) async-start(bf16[12,48,256]{2,1,0:T(8,128)(2,1)} %fold.1), calls=%async_computation.3 | async-start | bytes 589824 | tf_op jit(solution)/shard_map/all_to_all | solution.py:349
  106.1 1.0 copy-start.1
  107.1 1.0 copy-start.3
  108.1 1.0 copy-start.5
  109.1 1.0 copy-start.7
  110.1 1.3 copy-start.8
  121.7 24.0 %all-to-all-start.4 = ((f32[8,16,128]{2,1,0:T(8,128)}), f32[8,16,128]{2,1,0:T(8,128)S(1)}, u32[]{:S(2)}, u32[]{:S(2)}) async-start(f32[8,16,128]{2,1,0:T(8,128)} %get-tuple-element.25), calls=%async_computation.4 | async-start | bytes 131072 | tf_op jit(solution)/shard_map/all_to_all | solution.py:379
  127.4 18.2 %collective-permute-start.8 = (f32[34,208]{1,0:T(8,128)S(1)}, f32[34,208]{1,0:T(8,128)S(1)}, u32[]{:S(2)}, u32[]{:S(2)}) collective-permute-start(f32[34,208]{1,0:T(8,128)S(1)} %get-tuple-element.24), channel_id=1, source_target_pairs={{0,0},{1,96},{2,192},{3,288},{4,384},{5,480},{6,576},{7,672},{8,1}... | collective-permute-start | bytes 84872 | tf_op jit(solution)/shard_map/ppermute | solution.py:378

commit v6 on v5

--- a/solution.py
+++ b/solution.py
@@ -29,7 +29,7 @@
     return high, middle, low
 
 
-def cut_kernel(grad_hbm, feat_hbm, out_ref, grad_ref, feat_ref, sems):
+def cut_kernel(grad_hbm, feat_hbm, out_ref, grad_ref, feat_ref, last_ref, sems):
     feat_copy = pltpu.make_async_copy(feat_hbm, feat_ref, sems.at[0])
     grad_copy = pltpu.make_async_copy(grad_hbm, grad_ref, sems.at[1])
     feat_copy.start()
@@ -43,7 +43,6 @@
     lane = lax.broadcasted_iota(jnp.int32, (PR, WIDE), 1)
     grad_copy.wait()
     for part in range(NMP):
-        rest = [jnp.zeros((PR, 128), F32), jnp.zeros((PR, 128), F32)]
         live = lane < min(FEAT, VW - part * FEAT)
         for sub in range(SUB):
             low = sub * VW + part * FEAT
@@ -63,11 +62,12 @@
                 for tile in range(3):
                     at = tile * 2 * VT + row
                     out_ref[part, at : at + PR, :] = chunk[:, tile * 128 : tile * 128 + 128].astype(BF16)
-                group = row // 32
-                last = chunk[:, 384:512]
-                rest[sub % 2] += pltpu.roll(last, 32 * group, 1) if group else last
-        out_ref[part, REST : REST + PR, :] = rest[0].astype(BF16)
-        out_ref[part, REST + PR : REST + 2 * PR, :] = rest[1].astype(BF16)
+                last_ref[part, row : row + PR, :] = chunk[:, 384:512]
+    for part in range(NMP):
+        rest = last_ref[part, 0:32, :]
+        for group in range(1, 4):
+            rest = rest + pltpu.roll(last_ref[part, 32 * group : 32 * group + 32, :], 32 * group, 1)
+        out_ref[part, REST : REST + 2 * PR, :] = rest.astype(BF16)
 
 
 def unpack(ref, tile, which):
@@ -254,12 +254,14 @@
     return [pl.BlockSpec(memory_space=pltpu.SMEM)] * count
 
 
-def gather(own):
-    before, after, far = (
+def gather_x(own):
+    return tuple(
         lax.ppermute(own, "x", [(x, (x + step) % 4) for x in range(4)]) for step in (1, 3, 2)
     )
-    other = lax.ppermute(jnp.stack([own, before, after, far]), "c", [(0, 1), (1, 0)])
-    return own, before, after, far, other
+
+
+def gather_core(own, before, after, far):
+    return lax.ppermute(jnp.stack([own, before, after, far]), "c", [(0, 1), (1, 0)])
 
 
 def last_places():
@@ -288,6 +290,7 @@
         scratch_shapes=[
             pltpu.VMEM((PR, PW), BF16),
             pltpu.VMEM((PR, PW), BF16),
+            pltpu.VMEM((NMP, 2 * VT, 128), F32),
             pltpu.SemaphoreType.DMA((2,)),
         ],
         compiler_params=pltpu.CompilerParams(vmem_limit_bytes=60 * 1024 * 1024),
@@ -295,7 +298,7 @@
     )(grad_proj, saved_feat)
     attn_own, send = lax.optimization_barrier((attn_saved.T, send))
     recv = lax.all_to_all(send, MP, 0, 0)
-    attns = gather(attn_own)
+    attns = (attn_own,) + gather_x(attn_own)
     x_index, c_index = lax.axis_index("x"), lax.axis_index("c")
     near = jnp.stack([x_index, (x_index + 3) % 4, (x_index + 1) % 4, (x_index + 2) % 4]) * 2
     parts = jnp.concatenate([near + c_index, near + 1 - c_index]).astype(jnp.int32)
@@ -321,6 +324,8 @@
         compiler_params=VMEM,
         name="sums",
     )(source, live, recv, gain)
+    attns = lax.optimization_barrier(attns + (sums,))[:4]
+    attns = attns + (gather_core(*attns),)
     sums = lax.all_to_all(sums, MP, 0, 0)
 
     turned, terms = pl.pallas_call(
@@ -348,7 +353,8 @@
     )(terms)
     terms = lax.all_to_all(terms, "z", 0, 0)
 
-    turned = gather(turned)
+    turned = (turned,) + gather_x(turned)
+    turned = turned + (gather_core(*turned),)
     attn_grad, residual_grad = pl.pallas_call(
         gathered_kernel,
         out_shape=(

time: 148 us -> 146 us (0.986)
  waiting for transfers between devices: 56.1 us -> 58.9 us
  starting transfers between devices: 65 us -> 62.4 us
  Pallas kernels: 14.8 us -> 12.8 us
    ppermute x8, waiting for transfers between devices: 13.7 us -> 21.5 us  [the longest x6 21.5 us: gather_x(): lax.ppermute(own, 'x', [(x, (x + step) % 4) for x in range(4)])]
    all_to_all x1, waiting for transfers between devices: 6.44 us -> 1.46 us  [body(): recv = lax.all_to_all(send, MP, 0, 0)]
    pallas_call x1, Pallas kernels: 4.77 us -> 2.79 us  [body(): pl.pallas_call(cut_kernel, out_shape=jax.ShapeDtypeStruct((NMP, REST + 2...]
    all_to_all x1, starting transfers between devices: 6.52 us -> 4.82 us  [body(): recv = lax.all_to_all(send, MP, 0, 0)]
  transfers between devices with their start and end apart: 14 -> 14, of which waited for: 7 -> 9; matrix products, arithmetic and copies ran while one was open for 2% -> 1% of each run, Pallas kernels for 4% -> 4%
where the time goes in v6:
time: 146 us; the launch traced here: 145 us
  starting transfers between devices  62.4 us (43%)
  waiting for transfers between devices  58.9 us (40%)
  Pallas kernels  12.8 us (9%)
  local copies, waits for them, and re-layouts  6.67 us (5%)
  other arithmetic  2.92 us (2%)
  between operations  1.5 us (1%)
    ppermute x6, waiting for transfers between devices, gather_x(): lax.ppermute(own, 'x', [(x, (x + step) % 4) for x in range(4)])  21.5 us
    ppermute x6, starting transfers between devices, gather_x(): lax.ppermute(own, 'x', [(x, (x + step) % 4) for x in range(4)])  18.7 us
    ppermute x1, waiting for transfers between devices, body(): proj_grad = lax.ppermute(part, DP + MP, last_places())  16.3 us
    all_to_all x1, starting transfers between devices, body(): terms = lax.all_to_all(terms, 'z', 0, 0)  14.8 us
    all_to_all x1, waiting for transfers between devices, body(): terms = lax.all_to_all(terms, 'y', 0, 0)  9.83 us
    all_to_all x1, starting transfers between devices, body(): terms = lax.all_to_all(terms, 'y', 0, 0)  7.1 us
    all_to_all x1, waiting for transfers between devices, body(): terms = lax.all_to_all(terms, 'z', 0, 0)  6.86 us
    unnamed x27, local copies, waits for them, and re-layouts  5.99 us
  transfers between devices with their start and end apart: 14, of which 9 were waited for; matrix products, arithmetic and copies ran while one was open for 1% of the time, Pallas kernels for 4%

profile of v6, /device:TPU:68, one launch (start us, length us, event | category | flops | bytes accessed | tf_op | source)
XLA Modules:
  0.0 145.2 jit_solution(1580367016310399784)
XLA Ops:
  0.7 2.8 %cut.1 = bf16[8,416,128]{2,1,0:T(8,128)(2,1)} custom-call(bf16[16,12800]{1,0:T(8,128)(2,1)} %grad_hbm.1, bf16[16,12800]{1,0:T(8,128)(2,1)} %feat_hbm.1), custom_call_target="tpu_custom_call" | custom-call | tf_op jit(solution)/shard_map/cut/pallas_call | solution.py:285
  3.5 4.8 %all-to-all-start = ((bf16[8,416,128]{2,1,0:T(8,128)(2,1)}), bf16[8,416,128]{2,1,0:T(8,128)(2,1)S(1)}, u32[]{:S(2)}, u32[]{:S(2)}) async-start(bf16[8,416,128]{2,1,0:T(8,128)(2,1)} %cut.1), calls=%async_computation | async-start | bytes 1703936 | tf_op jit(solution)/shard_map/all_to_all | solution.py:300
  8.3 2.0 %collective-permute-start.2 = (bf16[208,512]{1,0:T(8,128)(2,1)S(1)}, bf16[208,512]{1,0:T(8,128)(2,1)S(1)}, u32[]{:S(2)}, u32[]{:S(2)}) collective-permute-start(bf16[208,512]{1,0:T(8,128)(2,1)S(1)} %bitcast.25), channel_id=1, source_target_pairs={{0,4},{2,6},{4,0},{6,2},{1,5},{3,7},{5,1},{7,3},{8,12},{10,14},{12... | collective-permute-start | bytes 638984 | tf_op jit(solution)/shard_map/ppermute | solution.py:259
  10.3 4.5 %collective-permute-start.1 = (bf16[208,512]{1,0:T(8,128)(2,1)S(1)}, bf16[208,512]{1,0:T(8,128)(2,1)S(1)}, u32[]{:S(2)}, u32[]{:S(2)}) collective-permute-start(bf16[208,512]{1,0:T(8,128)(2,1)S(1)} %bitcast.26), channel_id=1, source_target_pairs={{0,6},{2,0},{4,2},{6,4},{1,7},{3,1},{5,3},{7,5},{8,14},{10,8},{12,... | collective-permute-start | bytes 638984 | tf_op jit(solution)/shard_map/ppermute | solution.py:259
  14.9 1.9 %collective-permute-start = (bf16[208,512]{1,0:T(8,128)(2,1)S(1)}, bf16[208,512]{1,0:T(8,128)(2,1)S(1)}, u32[]{:S(2)}, u32[]{:S(2)}) collective-permute-start(bf16[208,512]{1,0:T(8,128)(2,1)S(1)} %bitcast.27), channel_id=1, source_target_pairs={{0,2},{2,4},{4,6},{6,0},{1,3},{3,5},{5,7},{7,1},{8,10},{10,12},{12... | collective-permute-start | bytes 638984 | tf_op jit(solution)/shard_map/ppermute | solution.py:259
  17.5 0.1 select_reduce_fusion.source_ref
  17.6 0.1 fusion.gain_ref
  17.7 1.5 %all-to-all-done.recv_ref = bf16[8,416,128]{2,1,0:T(8,128)(2,1)S(1)} async-done(((bf16[8,416,128]{2,1,0:T(8,128)(2,1)}), bf16[8,416,128]{2,1,0:T(8,128)(2,1)S(1)}, u32[]{:S(2)}, u32[]{:S(2)}) %all-to-all-start) | async-done | bytes 852000 | tf_op jit(solution)/shard_map/all_to_all | solution.py:300
  19.2 1.9 %sums.1 = f32[8,8,128]{2,1,0:T(8,128)} custom-call(s32[8]{0:T(128)S(1)} %select_reduce_fusion.source_ref, s32[8]{0:T(128)S(1)} %compare_convert_fusion.live_ref, bf16[8,416,128]{2,1,0:T(8,128)(2,1)S(1)} %all-to-all-done.recv_ref, f32[4,512]{1,0:T(4,128)S(1)} %fusion.gain_ref), custom_call_target="tpu_custom_call" | custom-call | tf_op jit(solution)/shard_map/sums/pallas_call | solution.py:319
  21.1 2.6 %collective-permute-done.2.far_ref = bf16[208,512]{1,0:T(8,128)(2,1)S(1)} collective-permute-done((bf16[208,512]{1,0:T(8,128)(2,1)S(1)}, bf16[208,512]{1,0:T(8,128)(2,1)S(1)}, u32[]{:S(2)}, u32[]{:S(2)}) %collective-permute-start.2) | collective-permute-done | bytes 213024 | tf_op jit(solution)/shard_map/ppermute | solution.py:259
  23.8 5.2 %collective-permute-done.1.after_ref = bf16[208,512]{1,0:T(8,128)(2,1)S(1)} collective-permute-done((bf16[208,512]{1,0:T(8,128)(2,1)S(1)}, bf16[208,512]{1,0:T(8,128)(2,1)S(1)}, u32[]{:S(2)}, u32[]{:S(2)}) %collective-permute-start.1) | collective-permute-done | bytes 213024 | tf_op jit(solution)/shard_map/ppermute | solution.py:259
  28.9 0.0 collective-permute-done.before_ref
  29.0 1.0 pad_maximum_fusion.1
  30.0 1.9 %collective-permute-start.3 = (bf16[4,208,512]{2,1,0:T(8,128)(2,1)}, bf16[4,208,512]{2,1,0:T(8,128)(2,1)S(1)}, u32[]{:S(2)}, u32[]{:S(2)}) collective-permute-start(bf16[4,208,512]{2,1,0:T(8,128)(2,1)} %pad_maximum_fusion.1), channel_id=1, source_target_pairs={{0,1},{1,0},{2,3},{3,2},{4,5},{5,4},{6,7},{7,6},{8,9},{9,8},{10,11... | collective-permute-start | bytes 2555912 | tf_op jit(solution)/shard_map/ppermute | solution.py:264
  31.9 0.1 broadcast_add_fusion
  32.0 0.1 fusion.1
  32.1 5.6 %all-to-all-start.1 = ((f32[8,8,128]{2,1,0:T(8,128)}), f32[8,8,128]{2,1,0:T(8,128)S(1)}, u32[]{:S(2)}, u32[]{:S(2)}) async-start(f32[8,8,128]{2,1,0:T(8,128)} %sums.1), calls=%async_computation.1 | async-start | bytes 65536 | tf_op jit(solution)/shard_map/all_to_all | solution.py:329
  37.7 0.1 pad_add_fusion.parts_ref
  37.7 2.9 %all-to-all-done.1.sums_ref = f32[8,8,128]{2,1,0:T(8,128)S(1)} async-done(((f32[8,8,128]{2,1,0:T(8,128)}), f32[8,8,128]{2,1,0:T(8,128)S(1)}, u32[]{:S(2)}, u32[]{:S(2)}) %all-to-all-start.1) | async-done | bytes 32800 | tf_op jit(solution)/shard_map/all_to_all | solution.py:329
  40.7 0.0 collective-permute-done.3.other_ref
  40.7 3.6 %branch.1 = (bf16[416,512]{1,0:T(8,128)(2,1)S(1)}, bf16[8,704,128]{2,1,0:T(8,128)(2,1)}) custom-call(s32[8]{0:T(128)S(1)} %select_reduce_fusion.source_ref, s32[8]{0:T(128)S(1)} %compare_convert_fusion.live_ref, s32[8]{0:T(128)S(1)} %pad_add_fusion.parts_ref, bf16[8,416,128]{2,1,0:T(8,128)(2,1)S(1)} %all-to-all-done.recv_ref, f32[4,512]{1,0:T(4,128)S(1)} %fusion.gain_ref, ...), custom_call_target="tpu_custom_call" | custom-call | tf_op jit(solution)/shard_map/branch/pallas_call | solution.py:331
  44.3 7.1 %all-to-all-start.2 = ((bf16[8,704,128]{2,1,0:T(8,128)(2,1)}), bf16[8,704,128]{2,1,0:T(8,128)(2,1)S(1)}, u32[]{:S(2)}, u32[]{:S(2)}) async-start(bf16[8,704,128]{2,1,0:T(8,128)(2,1)} %get-tuple-element.25), calls=%async_computation.2 | async-start | bytes 2883584 | tf_op jit(solution)/shard_map/all_to_all | solution.py:344
  51.4 4.3 %collective-permute-start.6 = (bf16[416,512]{1,0:T(8,128)(2,1)S(1)}, bf16[416,512]{1,0:T(8,128)(2,1)S(1)}, u32[]{:S(2)}, u32[]{:S(2)}) collective-permute-start(bf16[416,512]{1,0:T(8,128)(2,1)S(1)} %get-tuple-element.26.own_ref), channel_id=1, source_target_pairs={{0,4},{2,6},{4,0},{6,2},{1,5},{3,7},{5,1},{7,3},{8,12},{10,14},{12... | collective-permute-start | bytes 1277960 | tf_op jit(solution)/shard_map/ppermute | solution.py:259
  55.7 2.5 %collective-permute-start.5 = (bf16[416,512]{1,0:T(8,128)(2,1)S(1)}, bf16[416,512]{1,0:T(8,128)(2,1)S(1)}, u32[]{:S(2)}, u32[]{:S(2)}) collective-permute-start(bf16[416,512]{1,0:T(8,128)(2,1)S(1)} %get-tuple-element.26.own_ref), channel_id=1, source_target_pairs={{0,6},{2,0},{4,2},{6,4},{1,7},{3,1},{5,3},{7,5},{8,14},{10,8},{12,... | collective-permute-start | bytes 1277960 | tf_op jit(solution)/shard_map/ppermute | solution.py:259
  58.2 3.4 %collective-permute-start.4 = (bf16[416,512]{1,0:T(8,128)(2,1)S(1)}, bf16[416,512]{1,0:T(8,128)(2,1)S(1)}, u32[]{:S(2)}, u32[]{:S(2)}) collective-permute-start(bf16[416,512]{1,0:T(8,128)(2,1)S(1)} %get-tuple-element.26.own_ref), channel_id=1, source_target_pairs={{0,2},{2,4},{4,6},{6,0},{1,3},{3,5},{5,7},{7,1},{8,10},{10,12},{12... | collective-permute-start | bytes 1277960 | tf_op jit(solution)/shard_map/ppermute | solution.py:259
  61.6 6.0 %collective-permute-done.6.far_ref = bf16[416,512]{1,0:T(8,128)(2,1)S(1)} collective-permute-done((bf16[416,512]{1,0:T(8,128)(2,1)S(1)}, bf16[416,512]{1,0:T(8,128)(2,1)S(1)}, u32[]{:S(2)}, u32[]{:S(2)}) %collective-permute-start.6) | collective-permute-done | bytes 426016 | tf_op jit(solution)/shard_map/ppermute | solution.py:259
  67.6 7.7 %collective-permute-done.5.after_ref = bf16[416,512]{1,0:T(8,128)(2,1)S(1)} collective-permute-done((bf16[416,512]{1,0:T(8,128)(2,1)S(1)}, bf16[416,512]{1,0:T(8,128)(2,1)S(1)}, u32[]{:S(2)}, u32[]{:S(2)}) %collective-permute-start.5) | collective-permute-done | bytes 426016 | tf_op jit(solution)/shard_map/ppermute | solution.py:259
  75.3 1.5 %pad_maximum_fusion = bf16[4,416,512]{2,1,0:T(8,128)(2,1)} fusion(bf16[1,416,512]{2,1,0:T(8,128)(2,1)S(1)} %bitcast.21, bf16[1,416,512]{2,1,0:T(8,128)(2,1)S(1)} %bitcast.22, bf16[1,416,512]{2,1,0:T(8,128)(2,1)S(1)} %bitcast.23, bf16[1,416,512]{2,1,0:T(8,128)(2,1)S(1)} %bitcast.20), kind=kLoop, calls=%fused_computation | loop fusion | flops 2555904 | bytes 3407872 | tf_op jit(solution)/shard_map/stack | solution.py:264
  76.7 1.9 %collective-permute-start.7 = (bf16[4,416,512]{2,1,0:T(8,128)(2,1)}, bf16[4,416,512]{2,1,0:T(8,128)(2,1)S(1)}, u32[]{:S(2)}, u32[]{:S(2)}) collective-permute-start(bf16[4,416,512]{2,1,0:T(8,128)(2,1)} %pad_maximum_fusion), channel_id=1, source_target_pairs={{0,1},{1,0},{2,3},{3,2},{4,5},{5,4},{6,7},{7,6},{8,9},{9,8},{10,11... | collective-permute-start | bytes 5111816 | tf_op jit(solution)/shard_map/ppermute | solution.py:264
  78.7 9.8 %all-to-all-done.2.recv_ref = bf16[8,704,128]{2,1,0:T(8,128)(2,1)S(1)} async-done(((bf16[8,704,128]{2,1,0:T(8,128)(2,1)}), bf16[8,704,128]{2,1,0:T(8,128)(2,1)S(1)}, u32[]{:S(2)}, u32[]{:S(2)}) %all-to-all-start.2) | async-done | bytes 1441824 | tf_op jit(solution)/shard_map/all_to_all | solution.py:344
  88.5 1.0 fold.1
  89.5 14.8 %all-to-all-start.3 = ((bf16[12,48,256]{2,1,0:T(8,128)(2,1)}), bf16[12,48,256]{2,1,0:T(8,128)(2,1)S(1)}, u32[]{:S(2)}, u32[]{:S(2)}) async-start(bf16[12,48,256]{2,1,0:T(8,128)(2,1)} %fold.1), calls=%async_computation.3 | async-start | bytes 589824 | tf_op jit(solution)/shard_map/all_to_all | solution.py:354
  104.3 0.0 collective-permute-done.7.other_ref
  104.3 1.0 copy-done.1
  105.3 1.0 copy-done.3
  106.3 1.0 copy-done.5
  107.3 1.0 copy-done.7
  108.3 1.3 copy-done.8
  109.6 2.7 %gathered.1 = (bf16[208,512]{1,0:T(8,128)(2,1)}, bf16[64,3200]{1,0:T(8,128)(2,1)}) custom-call(s32[1]{0:T(128)} %bitcast.12.tile_ref, s32[8]{0:T(128)S(1)} %pad_add_fusion.parts_ref, bf16[208,3200]{1,0:T(8,128)(2,1)S(1)} %bitcast.24, f32[1,3200]{1,0:T(1,128)S(1)} %broadcast_in_dim.44.scale_ref, bf16[416,512]{1,0:T(8,128)(2,1)S(1)} %copy-done.1, ...), custom_call_target="tpu_custom_call" | custom-call | tf_op jit(solution)/shard_map/gathered/pallas_call | solution.py:358
  112.4 6.9 %all-to-all-done.3.recv_ref = bf16[12,48,256]{2,1,0:T(8,128)(2,1)S(1)} async-done(((bf16[12,48,256]{2,1,0:T(8,128)(2,1)}), bf16[12,48,256]{2,1,0:T(8,128)(2,1)S(1)}, u32[]{:S(2)}, u32[]{:S(2)}) %all-to-all-start.3) | async-done | bytes 294944 | tf_op jit(solution)/shard_map/all_to_all | solution.py:354
  119.2 0.6 settle.1
  119.9 5.7 %all-to-all-start.4 = ((f32[8,16,128]{2,1,0:T(8,128)}), f32[8,16,128]{2,1,0:T(8,128)S(1)}, u32[]{:S(2)}, u32[]{:S(2)}) async-start(f32[8,16,128]{2,1,0:T(8,128)} %get-tuple-element.33), calls=%async_computation.4 | async-start | bytes 131072 | tf_op jit(solution)/shard_map/all_to_all | solution.py:385
  125.6 1.9 %collective-permute-start.8 = (f32[34,208]{1,0:T(8,128)S(1)}, f32[34,208]{1,0:T(8,128)S(1)}, u32[]{:S(2)}, u32[]{:S(2)}) collective-permute-start(f32[34,208]{1,0:T(8,128)S(1)} %get-tuple-element.32), channel_id=1, source_target_pairs={{0,0},{1,96},{2,192},{3,288},{4,384},{5,480},{6,576},{7,672},{8,1}... | collective-permute-start | bytes 84872 | tf_op jit(solution)/shard_map/ppermute | solution.py:384
  127.5 16.3 %collective-permute-done.8 = f32[34,208]{1,0:T(8,128)S(1)} collective-permute-done((f32[34,208]{1,0:T(8,128)S(1)}, f32[34,208]{1,0:T(8,128)S(1)}, u32[]{:S(2)}, u32[]{:S(2)}) %collective-permute-start.8) | collective-permute-done | bytes 28320 | tf_op jit(solution)/shard_map/ppermute | solution.py:384
  143.8 0.0 all-to-all-done.4.gain_ref
  143.8 0.1 spread.1
  143.9 0.6 reshape.21
  144.6 0.6 copy.14
  (27 shorter events, 0.1 us)
Async XLA Ops:
  0.6 7.6 %copy-start.9 = (bf16[512,208]{0,1:T(8,128)(2,1)S(1)}, bf16[512,208]{0,1:T(8,128)(2,1)}, u32[]{:S(2)}) copy-start(bf16[512,208]{0,1:T(8,128)(2,1)} %param.14) | copy-start | bytes 638980
  0.6 16.8 %copy-start.11 = (f32[12800]{0:T(1024)S(1)}, f32[12800]{0:T(1024)}, u32[]{:S(2)}) copy-start(f32[12800]{0:T(1024)} %param.12) | copy-start | bytes 153604
  0.7 16.9 %copy-start.12 = (s32[1,8]{1,0:T(1,128)S(1)}, s32[1,8]{1,0:T(1,128)}, u32[]{:S(2)}) copy-start(s32[1,8]{1,0:T(1,128)} %param.10) | copy-start | bytes 100
  3.5 15.7 %all-to-all-start = ((bf16[8,416,128]{2,1,0:T(8,128)(2,1)}), bf16[8,416,128]{2,1,0:T(8,128)(2,1)S(1)}, u32[]{:S(2)}, u32[]{:S(2)}) async-start(bf16[8,416,128]{2,1,0:T(8,128)(2,1)} %cut.1), calls=%async_computation | async-start | bytes 1703936 | tf_op jit(solution)/shard_map/all_to_all | solution.py:300
  8.3 23.7 %copy-start.10 = (f32[3200]{0:T(1024)S(1)}, f32[3200]{0:T(1024)}, u32[]{:S(2)}) copy-start(f32[3200]{0:T(1024)} %param.13) | copy-start | bytes 38404
  8.3 15.5 %collective-permute-start.2 = (bf16[208,512]{1,0:T(8,128)(2,1)S(1)}, bf16[208,512]{1,0:T(8,128)(2,1)S(1)}, u32[]{:S(2)}, u32[]{:S(2)}) collective-permute-start(bf16[208,512]{1,0:T(8,128)(2,1)S(1)} %bitcast.25), channel_id=1, source_target_pairs={{0,4},{2,6},{4,0},{6,2},{1,5},{3,7},{5,1},{7,3},{8,12},{10,14},{12... | collective-permute-start | bytes 638984 | tf_op jit(solution)/shard_map/ppermute | solution.py:259
  10.3 18.6 %collective-permute-start.1 = (bf16[208,512]{1,0:T(8,128)(2,1)S(1)}, bf16[208,512]{1,0:T(8,128)(2,1)S(1)}, u32[]{:S(2)}, u32[]{:S(2)}) collective-permute-start(bf16[208,512]{1,0:T(8,128)(2,1)S(1)} %bitcast.26), channel_id=1, source_target_pairs={{0,6},{2,0},{4,2},{6,4},{1,7},{3,1},{5,3},{7,5},{8,14},{10,8},{12,... | collective-permute-start | bytes 638984 | tf_op jit(solution)/shard_map/ppermute | solution.py:259
  14.9 14.1 %collective-permute-start = (bf16[208,512]{1,0:T(8,128)(2,1)S(1)}, bf16[208,512]{1,0:T(8,128)(2,1)S(1)}, u32[]{:S(2)}, u32[]{:S(2)}) collective-permute-start(bf16[208,512]{1,0:T(8,128)(2,1)S(1)} %bitcast.27), channel_id=1, source_target_pairs={{0,2},{2,4},{4,6},{6,0},{1,3},{3,5},{5,7},{7,1},{8,10},{10,12},{12... | collective-permute-start | bytes 638984 | tf_op jit(solution)/shard_map/ppermute | solution.py:259
  30.0 10.7 %collective-permute-start.3 = (bf16[4,208,512]{2,1,0:T(8,128)(2,1)}, bf16[4,208,512]{2,1,0:T(8,128)(2,1)S(1)}, u32[]{:S(2)}, u32[]{:S(2)}) collective-permute-start(bf16[4,208,512]{2,1,0:T(8,128)(2,1)} %pad_maximum_fusion.1), channel_id=1, source_target_pairs={{0,1},{1,0},{2,3},{3,2},{4,5},{5,4},{6,7},{7,6},{8,9},{9,8},{10,11... | collective-permute-start | bytes 2555912 | tf_op jit(solution)/shard_map/ppermute | solution.py:264
  32.1 8.6 %all-to-all-start.1 = ((f32[8,8,128]{2,1,0:T(8,128)}), f32[8,8,128]{2,1,0:T(8,128)S(1)}, u32[]{:S(2)}, u32[]{:S(2)}) async-start(f32[8,8,128]{2,1,0:T(8,128)} %sums.1), calls=%async_computation.1 | async-start | bytes 65536 | tf_op jit(solution)/shard_map/all_to_all | solution.py:329
  44.3 31.0 %copy-start = (bf16[416,512]{1,0:T(8,128)(2,1)}, bf16[416,512]{1,0:T(8,128)(2,1)S(1)}, u32[]{:S(2)}) copy-start(bf16[416,512]{1,0:T(8,128)(2,1)S(1)} %get-tuple-element.26.own_ref) | copy-start | bytes 1277956
  44.3 44.2 %all-to-all-start.2 = ((bf16[8,704,128]{2,1,0:T(8,128)(2,1)}), bf16[8,704,128]{2,1,0:T(8,128)(2,1)S(1)}, u32[]{:S(2)}, u32[]{:S(2)}) async-start(bf16[8,704,128]{2,1,0:T(8,128)(2,1)} %get-tuple-element.25), calls=%async_computation.2 | async-start | bytes 2883584 | tf_op jit(solution)/shard_map/all_to_all | solution.py:344
  51.4 16.2 %collective-permute-start.6 = (bf16[416,512]{1,0:T(8,128)(2,1)S(1)}, bf16[416,512]{1,0:T(8,128)(2,1)S(1)}, u32[]{:S(2)}, u32[]{:S(2)}) collective-permute-start(bf16[416,512]{1,0:T(8,128)(2,1)S(1)} %get-tuple-element.26.own_ref), channel_id=1, source_target_pairs={{0,4},{2,6},{4,0},{6,2},{1,5},{3,7},{5,1},{7,3},{8,12},{10,14},{12... | collective-permute-start | bytes 1277960 | tf_op jit(solution)/shard_map/ppermute | solution.py:259
  55.7 19.5 %collective-permute-start.5 = (bf16[416,512]{1,0:T(8,128)(2,1)S(1)}, bf16[416,512]{1,0:T(8,128)(2,1)S(1)}, u32[]{:S(2)}, u32[]{:S(2)}) collective-permute-start(bf16[416,512]{1,0:T(8,128)(2,1)S(1)} %get-tuple-element.26.own_ref), channel_id=1, source_target_pairs={{0,6},{2,0},{4,2},{6,4},{1,7},{3,1},{5,3},{7,5},{8,14},{10,8},{12,... | collective-permute-start | bytes 1277960 | tf_op jit(solution)/shard_map/ppermute | solution.py:259
  58.2 17.1 %collective-permute-start.4 = (bf16[416,512]{1,0:T(8,128)(2,1)S(1)}, bf16[416,512]{1,0:T(8,128)(2,1)S(1)}, u32[]{:S(2)}, u32[]{:S(2)}) collective-permute-start(bf16[416,512]{1,0:T(8,128)(2,1)S(1)} %get-tuple-element.26.own_ref), channel_id=1, source_target_pairs={{0,2},{2,4},{4,6},{6,0},{1,3},{3,5},{5,7},{7,1},{8,10},{10,12},{12... | collective-permute-start | bytes 1277960 | tf_op jit(solution)/shard_map/ppermute | solution.py:259
  67.6 9.2 %copy-start.2 = (bf16[416,512]{1,0:T(8,128)(2,1)}, bf16[416,512]{1,0:T(8,128)(2,1)S(1)}, u32[]{:S(2)}) copy-start(bf16[416,512]{1,0:T(8,128)(2,1)S(1)} %collective-permute-done.6.far_ref) | copy-start | bytes 1277956
  75.3 1.5 %copy-start.4 = (bf16[416,512]{1,0:T(8,128)(2,1)}, bf16[416,512]{1,0:T(8,128)(2,1)S(1)}, u32[]{:S(2)}) copy-start(bf16[416,512]{1,0:T(8,128)(2,1)S(1)} %collective-permute-done.5.after_ref) | copy-start | bytes 1277956
  75.3 1.5 %copy-start.6 = (bf16[416,512]{1,0:T(8,128)(2,1)}, bf16[416,512]{1,0:T(8,128)(2,1)S(1)}, u32[]{:S(2)}) copy-start(bf16[416,512]{1,0:T(8,128)(2,1)S(1)} %collective-permute-done.4.before_ref) | copy-start | bytes 1277956
  76.7 27.5 %collective-permute-start.7 = (bf16[4,416,512]{2,1,0:T(8,128)(2,1)}, bf16[4,416,512]{2,1,0:T(8,128)(2,1)S(1)}, u32[]{:S(2)}, u32[]{:S(2)}) collective-permute-start(bf16[4,416,512]{2,1,0:T(8,128)(2,1)} %pad_maximum_fusion), channel_id=1, source_target_pairs={{0,1},{1,0},{2,3},{3,2},{4,5},{5,4},{6,7},{7,6},{8,9},{9,8},{10,11... | collective-permute-start | bytes 5111816 | tf_op jit(solution)/shard_map/ppermute | solution.py:264
  89.5 29.7 %all-to-all-start.3 = ((bf16[12,48,256]{2,1,0:T(8,128)(2,1)}), bf16[12,48,256]{2,1,0:T(8,128)(2,1)S(1)}, u32[]{:S(2)}, u32[]{:S(2)}) async-start(bf16[12,48,256]{2,1,0:T(8,128)(2,1)} %fold.1), calls=%async_computation.3 | async-start | bytes 589824 | tf_op jit(solution)/shard_map/all_to_all | solution.py:354
  104.3 1.0 copy-start.1
  105.3 1.0 copy-start.3
  106.3 1.0 copy-start.5
  107.3 1.0 copy-start.7
  108.3 1.3 copy-start.8
  119.9 24.0 %all-to-all-start.4 = ((f32[8,16,128]{2,1,0:T(8,128)}), f32[8,16,128]{2,1,0:T(8,128)S(1)}, u32[]{:S(2)}, u32[]{:S(2)}) async-start(f32[8,16,128]{2,1,0:T(8,128)} %get-tuple-element.33), calls=%async_computation.4 | async-start | bytes 131072 | tf_op jit(solution)/shard_map/all_to_all | solution.py:385
  125.6 18.2 %collective-permute-start.8 = (f32[34,208]{1,0:T(8,128)S(1)}, f32[34,208]{1,0:T(8,128)S(1)}, u32[]{:S(2)}, u32[]{:S(2)}) collective-permute-start(f32[34,208]{1,0:T(8,128)S(1)} %get-tuple-element.32), channel_id=1, source_target_pairs={{0,0},{1,96},{2,192},{3,288},{4,384},{5,480},{6,576},{7,672},{8,1}... | collective-permute-start | bytes 84872 | tf_op jit(solution)/shard_map/ppermute | solution.py:384

commit v7 on v6

--- a/solution.py
+++ b/solution.py
@@ -126,8 +126,7 @@
 
 
 def branch_kernel(
-    source_ref, live_ref, parts_ref, recv_ref, gain_ref, scale_ref, sums_ref,
-    own_ref, before_ref, after_ref, far_ref, other_ref, turned_ref, terms_ref, branch_ref,
+    source_ref, live_ref, recv_ref, gain_ref, scale_ref, sums_ref, branch_ref, gain_out_ref
 ):
     total = sums_ref[0]
     for part in range(1, NMP):
@@ -156,7 +155,14 @@
     gain = jnp.concatenate([jnp.sum(g, axis=0, keepdims=True) for g in gains], axis=0)
     gain = jnp.concatenate([gain[:, q * 128 : (q + 1) * 128] for q in range(4)], axis=0)
     gain_high = gain.astype(BF16)
-    gain_low = (gain - gain_high.astype(F32)).astype(BF16)
+    gain_out_ref[0:GAIN, :] = gain_high
+    gain_out_ref[GAIN : 2 * GAIN, :] = (gain - gain_high.astype(F32)).astype(BF16)
+
+
+def terms_kernel(
+    parts_ref, branch_ref, gain_ref, own_ref, before_ref, after_ref, far_ref, other_ref,
+    turned_ref, terms_ref,
+):
     attns = [own_ref, before_ref, after_ref, far_ref] + [other_ref.at[p] for p in range(4)]
     for place, attn in enumerate(attns):
         part = parts_ref[place]
@@ -170,8 +176,7 @@
         tail = pltpu.roll(last[4 * GROUP : COLS], 96, 1)
         rest = jnp.concatenate([rest[0:16] + tail, rest[16:]], axis=0)
         terms_ref[part, AT3:AT4, :] = rest.astype(BF16)
-        terms_ref[part, AT4:AT5, :] = gain_high
-        terms_ref[part, AT5:MESSAGE, :] = gain_low
+        terms_ref[part, AT4:MESSAGE, :] = gain_ref[...]
     turned_ref[...] = branch_ref[...].T[:ROWS]
 
 
@@ -196,7 +201,7 @@
     total = recv_ref[0].astype(F32)
     for part in range(1, NZ):
         total = total + recv_ref[part].astype(F32)
-    block_ref[...] = total[0:BLOCK, 0 : block_ref.shape[1]]
+    block_ref[...] = jnp.concatenate([total, jnp.zeros((16, 256), F32)], axis=0)
     gain = jnp.concatenate([total[40:48, 0:128], total[40:48, 128:256]], axis=0)
     for part in range(NMP):
         gain_ref[part] = gain
@@ -260,8 +265,8 @@
     )
 
 
-def gather_core(own, before, after, far):
-    return lax.ppermute(jnp.stack([own, before, after, far]), "c", [(0, 1), (1, 0)])
+def swap_cores(four):
+    return lax.ppermute(four, "c", [(0, 1), (1, 0)])
 
 
 def last_places():
@@ -324,22 +329,32 @@
         compiler_params=VMEM,
         name="sums",
     )(source, live, recv, gain)
-    attns = lax.optimization_barrier(attns + (sums,))[:4]
-    attns = attns + (gather_core(*attns),)
     sums = lax.all_to_all(sums, MP, 0, 0)
-
+    four, sums = lax.optimization_barrier((jnp.stack(attns), sums))
+    attns = attns + (swap_cores(four),)
+
+    branch, gains = pl.pallas_call(
+        branch_kernel,
+        out_shape=(
+            jax.ShapeDtypeStruct((TILES * VT, WIDE), BF16),
+            jax.ShapeDtypeStruct((2 * GAIN, 128), BF16),
+        ),
+        in_specs=scalars(2) + whole(4),
+        out_specs=tuple(whole(2)),
+        compiler_params=VMEM,
+        name="branch",
+    )(source, live, recv, gain, scale, sums)
     turned, terms = pl.pallas_call(
-        branch_kernel,
+        terms_kernel,
         out_shape=(
             jax.ShapeDtypeStruct((ROWS, TILES * VT), BF16),
             jax.ShapeDtypeStruct((NMP, MESSAGE, 128), BF16),
         ),
-        in_specs=scalars(3) + whole(9),
+        in_specs=scalars(1) + whole(7),
         out_specs=tuple(whole(2)),
-        scratch_shapes=[pltpu.VMEM((TILES * VT, WIDE), BF16)],
-        compiler_params=VMEM,
-        name="branch",
-    )(source, live, parts, recv, gain, scale, sums, *attns)
+        compiler_params=VMEM,
+        name="terms",
+    )(parts, branch, gains, *attns)
 
     terms = lax.all_to_all(terms, "y", 0, 0)
     terms = pl.pallas_call(
@@ -354,7 +369,7 @@
     terms = lax.all_to_all(terms, "z", 0, 0)
 
     turned = (turned,) + gather_x(turned)
-    turned = turned + (gather_core(*turned),)
+    turned = turned + (swap_cores(jnp.stack(turned)),)
     attn_grad, residual_grad = pl.pallas_call(
         gathered_kernel,
         out_shape=(
@@ -372,7 +387,7 @@
     part, gains = pl.pallas_call(
         settle_kernel,
         out_shape=(
-            jax.ShapeDtypeStruct((BLOCK, cols), F32),
+            jax.ShapeDtypeStruct((64, 256), F32),
             jax.ShapeDtypeStruct((NMP, GAIN, 128), F32),
         ),
         in_specs=whole(1),
@@ -381,7 +396,7 @@
         name="settle",
     )(terms)
 
-    proj_grad = lax.ppermute(part, DP + MP, last_places())
+    proj_grad = lax.ppermute(part, DP + MP, last_places())[:BLOCK, :cols]
     gains = lax.all_to_all(gains, MP, 0, 0)
     gain_grad = pl.pallas_call(
         spread_kernel,

time: 146 us -> 135 us (0.925)
  waiting for transfers between devices: 58.9 us -> 43.1 us
  blocking collectives: 0 us -> 8.29 us
  starting transfers between devices: 62.4 us -> 58.8 us
    ppermute x3, waiting for transfers between devices: 16.3 us -> 7 us  [the longest x1 6.18 us: body(): proj_grad = lax.ppermute(part, DP + MP, last_places())[:BLOCK, :cols]]
    all_to_all x0 -> x1, blocking collectives: none -> 8.29 us  [body(): gains = lax.all_to_all(gains, MP, 0, 0)]
    ppermute x6, waiting for transfers between devices: 21.5 us -> 15.1 us  [gather_x(): lax.ppermute(own, 'x', [(x, (x + step) % 4) for x in range(4)])]
    all_to_all x1 -> x0, starting transfers between devices: 5.71 us -> none  [body(): gains = lax.all_to_all(gains, MP, 0, 0)]
    all_to_all x1, waiting for transfers between devices: 2.94 us -> 0.9 us  [body(): sums = lax.all_to_all(sums, MP, 0, 0)]
    all_to_all x1, waiting for transfers between devices: 6.86 us -> 8.77 us  [body(): terms = lax.all_to_all(terms, 'z', 0, 0)]
    unnamed x27 -> x26, local copies, waits for them, and re-layouts: 5.99 us -> 5.37 us
    pallas_call x2 -> x3, Pallas kernels: 4.25 us -> 4.3 us  [the longest x1 2.79 us: body(): pl.pallas_call(terms_kernel, out_shape=(jax.ShapeDtypeStruct((ROWS, TILES...]
  transfers between devices with their start and end apart: 14 -> 13, of which waited for: 9 -> 9; matrix products, arithmetic and copies ran while one was open for 1% -> 3% of each run, Pallas kernels for 4% -> 5%
where the time goes in v7:
time: 135 us; the launch traced here: 134 us
  starting transfers between devices  58.8 us (44%)
  waiting for transfers between devices  43.1 us (32%)
  Pallas kernels  12.9 us (10%)
  blocking collectives  8.29 us (6%)
  local copies, waits for them, and re-layouts  6.68 us (5%)
  other arithmetic  2.95 us (2%)
  between operations  1.51 us (1%)
    ppermute x6, starting transfers between devices, gather_x(): lax.ppermute(own, 'x', [(x, (x + step) % 4) for x in range(4)])  18.7 us
    ppermute x6, waiting for transfers between devices, gather_x(): lax.ppermute(own, 'x', [(x, (x + step) % 4) for x in range(4)])  15.1 us
    all_to_all x1, starting transfers between devices, body(): terms = lax.all_to_all(terms, 'z', 0, 0)  14.8 us
    all_to_all x1, waiting for transfers between devices, body(): terms = lax.all_to_all(terms, 'y', 0, 0)  9.84 us
    all_to_all x1, waiting for transfers between devices, body(): terms = lax.all_to_all(terms, 'z', 0, 0)  8.77 us
    all_to_all x1, blocking collectives, body(): gains = lax.all_to_all(gains, MP, 0, 0)  8.29 us
    all_to_all x1, starting transfers between devices, body(): terms = lax.all_to_all(terms, 'y', 0, 0)  7.1 us
    all_to_all x1, starting transfers between devices, body(): sums = lax.all_to_all(sums, MP, 0, 0)  6.73 us
  transfers between devices with their start and end apart: 13, of which 9 were waited for; matrix products, arithmetic and copies ran while one was open for 3% of the time, Pallas kernels for 5%

profile of v7, /device:TPU:68, one launch (start us, length us, event | category | flops | bytes accessed | tf_op | source)
XLA Modules:
  0.0 134.2 jit_solution(5215022305758642170)
XLA Ops:
  0.7 2.8 %cut.1 = bf16[8,416,128]{2,1,0:T(8,128)(2,1)} custom-call(bf16[16,12800]{1,0:T(8,128)(2,1)} %grad_hbm.1, bf16[16,12800]{1,0:T(8,128)(2,1)} %feat_hbm.1), custom_call_target="tpu_custom_call" | custom-call | tf_op jit(solution)/shard_map/cut/pallas_call | solution.py:290
  3.5 4.8 %all-to-all-start = ((bf16[8,416,128]{2,1,0:T(8,128)(2,1)}), bf16[8,416,128]{2,1,0:T(8,128)(2,1)S(1)}, u32[]{:S(2)}, u32[]{:S(2)}) async-start(bf16[8,416,128]{2,1,0:T(8,128)(2,1)} %cut.1), calls=%async_computation | async-start | bytes 1703936 | tf_op jit(solution)/shard_map/all_to_all | solution.py:305
  8.3 2.0 %collective-permute-start.2 = (bf16[208,512]{1,0:T(8,128)(2,1)S(1)}, bf16[208,512]{1,0:T(8,128)(2,1)S(1)}, u32[]{:S(2)}, u32[]{:S(2)}) collective-permute-start(bf16[208,512]{1,0:T(8,128)(2,1)S(1)} %bitcast.25), channel_id=1, source_target_pairs={{0,4},{2,6},{4,0},{6,2},{1,5},{3,7},{5,1},{7,3},{8,12},{10,14},{12... | collective-permute-start | bytes 638984 | tf_op jit(solution)/shard_map/ppermute | solution.py:264
  10.3 4.5 %collective-permute-start.1 = (bf16[208,512]{1,0:T(8,128)(2,1)S(1)}, bf16[208,512]{1,0:T(8,128)(2,1)S(1)}, u32[]{:S(2)}, u32[]{:S(2)}) collective-permute-start(bf16[208,512]{1,0:T(8,128)(2,1)S(1)} %bitcast.26), channel_id=1, source_target_pairs={{0,6},{2,0},{4,2},{6,4},{1,7},{3,1},{5,3},{7,5},{8,14},{10,8},{12,... | collective-permute-start | bytes 638984 | tf_op jit(solution)/shard_map/ppermute | solution.py:264
  14.9 1.9 %collective-permute-start = (bf16[208,512]{1,0:T(8,128)(2,1)S(1)}, bf16[208,512]{1,0:T(8,128)(2,1)S(1)}, u32[]{:S(2)}, u32[]{:S(2)}) collective-permute-start(bf16[208,512]{1,0:T(8,128)(2,1)S(1)} %bitcast.27), channel_id=1, source_target_pairs={{0,2},{2,4},{4,6},{6,0},{1,3},{3,5},{5,7},{7,1},{8,10},{10,12},{12... | collective-permute-start | bytes 638984 | tf_op jit(solution)/shard_map/ppermute | solution.py:264
  17.5 0.1 select_reduce_fusion.source_ref
  17.6 0.1 fusion.gain_ref
  17.7 1.5 %all-to-all-done.recv_ref = bf16[8,416,128]{2,1,0:T(8,128)(2,1)S(1)} async-done(((bf16[8,416,128]{2,1,0:T(8,128)(2,1)}), bf16[8,416,128]{2,1,0:T(8,128)(2,1)S(1)}, u32[]{:S(2)}, u32[]{:S(2)}) %all-to-all-start) | async-done | bytes 852000 | tf_op jit(solution)/shard_map/all_to_all | solution.py:305
  19.2 1.9 %sums.1 = f32[8,8,128]{2,1,0:T(8,128)} custom-call(s32[8]{0:T(128)S(1)} %select_reduce_fusion.source_ref, s32[8]{0:T(128)S(1)} %compare_convert_fusion.live_ref, bf16[8,416,128]{2,1,0:T(8,128)(2,1)S(1)} %all-to-all-done.recv_ref, f32[4,512]{1,0:T(4,128)S(1)} %fusion.gain_ref), custom_call_target="tpu_custom_call" | custom-call | tf_op jit(solution)/shard_map/sums/pallas_call | solution.py:324
  21.1 6.7 %all-to-all-start.1 = ((f32[8,8,128]{2,1,0:T(8,128)}), f32[8,8,128]{2,1,0:T(8,128)S(1)}, u32[]{:S(2)}, u32[]{:S(2)}) async-start(f32[8,8,128]{2,1,0:T(8,128)} %sums.1), calls=%async_computation.1 | async-start | bytes 65536 | tf_op jit(solution)/shard_map/all_to_all | solution.py:332
  27.9 0.0 collective-permute-done.2.far_ref
  27.9 1.1 collective-permute-done.1.after_ref
  29.0 0.0 collective-permute-done.before_ref
  29.0 1.0 pad_maximum_fusion.1
  30.0 0.9 all-to-all-done.1.sums_ref
  30.9 1.9 %collective-permute-start.3 = (bf16[4,208,512]{2,1,0:T(8,128)(2,1)}, bf16[4,208,512]{2,1,0:T(8,128)(2,1)S(1)}, u32[]{:S(2)}, u32[]{:S(2)}) collective-permute-start(bf16[4,208,512]{2,1,0:T(8,128)(2,1)} %pad_maximum_fusion.1), channel_id=1, source_target_pairs={{0,1},{1,0},{2,3},{3,2},{4,5},{5,4},{6,7},{7,6},{8,9},{9,8},{10,11... | collective-permute-start | bytes 2555912 | tf_op jit(solution)/shard_map/ppermute | solution.py:269
  32.8 0.1 broadcast_add_fusion
  32.9 0.1 pad_add_fusion.parts_ref
  33.0 0.1 fusion.1
  33.1 1.5 %branch.1 = (bf16[512,512]{1,0:T(8,128)(2,1)S(1)}, bf16[32,128]{1,0:T(8,128)(2,1)S(1)}) custom-call(s32[8]{0:T(128)S(1)} %select_reduce_fusion.source_ref, s32[8]{0:T(128)S(1)} %compare_convert_fusion.live_ref, bf16[8,416,128]{2,1,0:T(8,128)(2,1)S(1)} %all-to-all-done.recv_ref, f32[4,512]{1,0:T(4,128)S(1)} %fusion.gain_ref, f32[1,512]{1,0:T(1,128)S(1)} %bitcast.33, ...), custom_call_target="tpu_custom_call" | custom-call | tf_op jit(solution)/shard_map/branch/pallas_call | solution.py:336
  34.5 0.8 collective-permute-done.3.other_ref
  35.4 2.8 %terms.1 = (bf16[416,512]{1,0:T(8,128)(2,1)S(1)}, bf16[8,704,128]{2,1,0:T(8,128)(2,1)}) custom-call(s32[8]{0:T(128)S(1)} %pad_add_fusion.parts_ref, bf16[512,512]{1,0:T(8,128)(2,1)S(1)} %get-tuple-element.22.branch_ref, bf16[32,128]{1,0:T(8,128)(2,1)S(1)} %get-tuple-element.23.gain_ref, bf16[208,512]{1,0:T(8,128)(2,1)S(1)} %bitcast.29, ...), custom_call_target="tpu_custom_call" | custom-call | tf_op jit(solution)/shard_map/terms/pallas_call | solution.py:347
  38.2 7.1 %all-to-all-start.2 = ((bf16[8,704,128]{2,1,0:T(8,128)(2,1)}), bf16[8,704,128]{2,1,0:T(8,128)(2,1)S(1)}, u32[]{:S(2)}, u32[]{:S(2)}) async-start(bf16[8,704,128]{2,1,0:T(8,128)(2,1)} %get-tuple-element.25), calls=%async_computation.2 | async-start | bytes 2883584 | tf_op jit(solution)/shard_map/all_to_all | solution.py:359
  45.3 4.3 %collective-permute-start.6 = (bf16[416,512]{1,0:T(8,128)(2,1)S(1)}, bf16[416,512]{1,0:T(8,128)(2,1)S(1)}, u32[]{:S(2)}, u32[]{:S(2)}) collective-permute-start(bf16[416,512]{1,0:T(8,128)(2,1)S(1)} %get-tuple-element.26.own_ref), channel_id=1, source_target_pairs={{0,4},{2,6},{4,0},{6,2},{1,5},{3,7},{5,1},{7,3},{8,12},{10,14},{12... | collective-permute-start | bytes 1277960 | tf_op jit(solution)/shard_map/ppermute | solution.py:264
  49.6 2.5 %collective-permute-start.5 = (bf16[416,512]{1,0:T(8,128)(2,1)S(1)}, bf16[416,512]{1,0:T(8,128)(2,1)S(1)}, u32[]{:S(2)}, u32[]{:S(2)}) collective-permute-start(bf16[416,512]{1,0:T(8,128)(2,1)S(1)} %get-tuple-element.26.own_ref), channel_id=1, source_target_pairs={{0,6},{2,0},{4,2},{6,4},{1,7},{3,1},{5,3},{7,5},{8,14},{10,8},{12,... | collective-permute-start | bytes 1277960 | tf_op jit(solution)/shard_map/ppermute | solution.py:264
  52.1 3.4 %collective-permute-start.4 = (bf16[416,512]{1,0:T(8,128)(2,1)S(1)}, bf16[416,512]{1,0:T(8,128)(2,1)S(1)}, u32[]{:S(2)}, u32[]{:S(2)}) collective-permute-start(bf16[416,512]{1,0:T(8,128)(2,1)S(1)} %get-tuple-element.26.own_ref), channel_id=1, source_target_pairs={{0,2},{2,4},{4,6},{6,0},{1,3},{3,5},{5,7},{7,1},{8,10},{10,12},{12... | collective-permute-start | bytes 1277960 | tf_op jit(solution)/shard_map/ppermute | solution.py:264
  55.5 5.9 %collective-permute-done.6.far_ref = bf16[416,512]{1,0:T(8,128)(2,1)S(1)} collective-permute-done((bf16[416,512]{1,0:T(8,128)(2,1)S(1)}, bf16[416,512]{1,0:T(8,128)(2,1)S(1)}, u32[]{:S(2)}, u32[]{:S(2)}) %collective-permute-start.6) | collective-permute-done | bytes 426016 | tf_op jit(solution)/shard_map/ppermute | solution.py:264
  61.4 8.1 %collective-permute-done.5.after_ref = bf16[416,512]{1,0:T(8,128)(2,1)S(1)} collective-permute-done((bf16[416,512]{1,0:T(8,128)(2,1)S(1)}, bf16[416,512]{1,0:T(8,128)(2,1)S(1)}, u32[]{:S(2)}, u32[]{:S(2)}) %collective-permute-start.5) | collective-permute-done | bytes 426016 | tf_op jit(solution)/shard_map/ppermute | solution.py:264
  69.5 0.0 collective-permute-done.4.before_ref
  69.5 1.5 %pad_maximum_fusion = bf16[4,416,512]{2,1,0:T(8,128)(2,1)} fusion(bf16[1,416,512]{2,1,0:T(8,128)(2,1)S(1)} %bitcast.21, bf16[1,416,512]{2,1,0:T(8,128)(2,1)S(1)} %bitcast.22, bf16[1,416,512]{2,1,0:T(8,128)(2,1)S(1)} %bitcast.23, bf16[1,416,512]{2,1,0:T(8,128)(2,1)S(1)} %bitcast.20), kind=kLoop, calls=%fused_computation | loop fusion | flops 2555904 | bytes 3407872 | tf_op jit(solution)/shard_map/stack | solution.py:372
  71.0 1.9 %collective-permute-start.7 = (bf16[4,416,512]{2,1,0:T(8,128)(2,1)}, bf16[4,416,512]{2,1,0:T(8,128)(2,1)S(1)}, u32[]{:S(2)}, u32[]{:S(2)}) collective-permute-start(bf16[4,416,512]{2,1,0:T(8,128)(2,1)} %pad_maximum_fusion), channel_id=1, source_target_pairs={{0,1},{1,0},{2,3},{3,2},{4,5},{5,4},{6,7},{7,6},{8,9},{9,8},{10,11... | collective-permute-start | bytes 5111816 | tf_op jit(solution)/shard_map/ppermute | solution.py:269
  72.9 9.8 %all-to-all-done.2.recv_ref = bf16[8,704,128]{2,1,0:T(8,128)(2,1)S(1)} async-done(((bf16[8,704,128]{2,1,0:T(8,128)(2,1)}), bf16[8,704,128]{2,1,0:T(8,128)(2,1)S(1)}, u32[]{:S(2)}, u32[]{:S(2)}) %all-to-all-start.2) | async-done | bytes 1441824 | tf_op jit(solution)/shard_map/all_to_all | solution.py:359
  82.7 1.0 fold.1
  83.7 14.8 %all-to-all-start.3 = ((bf16[12,48,256]{2,1,0:T(8,128)(2,1)}), bf16[12,48,256]{2,1,0:T(8,128)(2,1)S(1)}, u32[]{:S(2)}, u32[]{:S(2)}) async-start(bf16[12,48,256]{2,1,0:T(8,128)(2,1)} %fold.1), calls=%async_computation.3 | async-start | bytes 589824 | tf_op jit(solution)/shard_map/all_to_all | solution.py:369
  98.5 0.0 collective-permute-done.7.other_ref
  98.5 1.0 copy-done.1
  99.5 1.0 copy-done.3
  100.5 1.0 copy-done.5
  101.6 1.0 copy-done.7
  102.6 1.3 copy-done.8
  103.9 2.7 %gathered.1 = (bf16[208,512]{1,0:T(8,128)(2,1)}, bf16[64,3200]{1,0:T(8,128)(2,1)}) custom-call(s32[1]{0:T(128)} %bitcast.12.tile_ref, s32[8]{0:T(128)S(1)} %pad_add_fusion.parts_ref, bf16[208,3200]{1,0:T(8,128)(2,1)S(1)} %bitcast.24, f32[1,3200]{1,0:T(1,128)S(1)} %broadcast_in_dim.44.scale_ref, bf16[416,512]{1,0:T(8,128)(2,1)S(1)} %copy-done.1, ...), custom_call_target="tpu_custom_call" | custom-call | tf_op jit(solution)/shard_map/gathered/pallas_call | solution.py:373
  106.6 8.8 %all-to-all-done.3.recv_ref = bf16[12,48,256]{2,1,0:T(8,128)(2,1)S(1)} async-done(((bf16[12,48,256]{2,1,0:T(8,128)(2,1)}), bf16[12,48,256]{2,1,0:T(8,128)(2,1)S(1)}, u32[]{:S(2)}, u32[]{:S(2)}) %all-to-all-start.3) | async-done | bytes 294944 | tf_op jit(solution)/shard_map/all_to_all | solution.py:369
  115.4 2.9 %collective-permute-start.8 = (f32[64,256]{1,0:T(8,128)S(1)}, f32[64,256]{1,0:T(8,128)S(1)}, u32[]{:S(2)}, u32[]{:S(2)}) collective-permute-start(f32[64,256]{1,0:T(8,128)S(1)} %get-tuple-element.32), channel_id=1, source_target_pairs={{0,0},{1,96},{2,192},{3,288},{4,384},{5,480},{6,576},{7,672},{8,1}... | collective-permute-start | bytes 196616 | tf_op jit(solution)/shard_map/ppermute | solution.py:399
  118.4 8.3 %all_to_all.25.gain_ref = f32[8,16,128]{2,1,0:T(8,128)S(1)} all-to-all(f32[8,16,128]{2,1,0:T(8,128)S(1)} %get-tuple-element.33), channel_id=1, replica_groups=mesh['z'=12,'y'=8,'x'=4,'c'=2] {'x','c'}, dimensions={0} | all-to-all | bytes 131072 | tf_op jit(solution)/shard_map/all_to_all | solution.py:400
  126.6 0.1 spread.1
  126.8 0.6 reshape.21
  127.4 6.2 %collective-permute-done.8 = f32[64,256]{1,0:T(8,128)S(1)} collective-permute-done((f32[64,256]{1,0:T(8,128)S(1)}, f32[64,256]{1,0:T(8,128)S(1)}, u32[]{:S(2)}, u32[]{:S(2)}) %collective-permute-start.8) | collective-permute-done | bytes 65568 | tf_op jit(solution)/shard_map/ppermute | solution.py:399
  133.6 0.6 slice.4
  (27 shorter events, 0.1 us)
Async XLA Ops:
  0.6 7.7 %copy-start.9 = (bf16[512,208]{0,1:T(8,128)(2,1)S(1)}, bf16[512,208]{0,1:T(8,128)(2,1)}, u32[]{:S(2)}) copy-start(bf16[512,208]{0,1:T(8,128)(2,1)} %param.14) | copy-start | bytes 638980
  0.6 16.8 %copy-start.11 = (f32[12800]{0:T(1024)S(1)}, f32[12800]{0:T(1024)}, u32[]{:S(2)}) copy-start(f32[12800]{0:T(1024)} %param.12) | copy-start | bytes 153604
  0.7 16.9 %copy-start.12 = (s32[1,8]{1,0:T(1,128)S(1)}, s32[1,8]{1,0:T(1,128)}, u32[]{:S(2)}) copy-start(s32[1,8]{1,0:T(1,128)} %param.10) | copy-start | bytes 100
  3.5 15.7 %all-to-all-start = ((bf16[8,416,128]{2,1,0:T(8,128)(2,1)}), bf16[8,416,128]{2,1,0:T(8,128)(2,1)S(1)}, u32[]{:S(2)}, u32[]{:S(2)}) async-start(bf16[8,416,128]{2,1,0:T(8,128)(2,1)} %cut.1), calls=%async_computation | async-start | bytes 1703936 | tf_op jit(solution)/shard_map/all_to_all | solution.py:305
  8.3 24.7 %copy-start.10 = (f32[3200]{0:T(1024)S(1)}, f32[3200]{0:T(1024)}, u32[]{:S(2)}) copy-start(f32[3200]{0:T(1024)} %param.13) | copy-start | bytes 38404
  8.3 19.6 %collective-permute-start.2 = (bf16[208,512]{1,0:T(8,128)(2,1)S(1)}, bf16[208,512]{1,0:T(8,128)(2,1)S(1)}, u32[]{:S(2)}, u32[]{:S(2)}) collective-permute-start(bf16[208,512]{1,0:T(8,128)(2,1)S(1)} %bitcast.25), channel_id=1, source_target_pairs={{0,4},{2,6},{4,0},{6,2},{1,5},{3,7},{5,1},{7,3},{8,12},{10,14},{12... | collective-permute-start | bytes 638984 | tf_op jit(solution)/shard_map/ppermute | solution.py:264
  10.3 18.6 %collective-permute-start.1 = (bf16[208,512]{1,0:T(8,128)(2,1)S(1)}, bf16[208,512]{1,0:T(8,128)(2,1)S(1)}, u32[]{:S(2)}, u32[]{:S(2)}) collective-permute-start(bf16[208,512]{1,0:T(8,128)(2,1)S(1)} %bitcast.26), channel_id=1, source_target_pairs={{0,6},{2,0},{4,2},{6,4},{1,7},{3,1},{5,3},{7,5},{8,14},{10,8},{12,... | collective-permute-start | bytes 638984 | tf_op jit(solution)/shard_map/ppermute | solution.py:264
  14.9 14.1 %collective-permute-start = (bf16[208,512]{1,0:T(8,128)(2,1)S(1)}, bf16[208,512]{1,0:T(8,128)(2,1)S(1)}, u32[]{:S(2)}, u32[]{:S(2)}) collective-permute-start(bf16[208,512]{1,0:T(8,128)(2,1)S(1)} %bitcast.27), channel_id=1, source_target_pairs={{0,2},{2,4},{4,6},{6,0},{1,3},{3,5},{5,7},{7,1},{8,10},{10,12},{12... | collective-permute-start | bytes 638984 | tf_op jit(solution)/shard_map/ppermute | solution.py:264
  21.1 9.7 %all-to-all-start.1 = ((f32[8,8,128]{2,1,0:T(8,128)}), f32[8,8,128]{2,1,0:T(8,128)S(1)}, u32[]{:S(2)}, u32[]{:S(2)}) async-start(f32[8,8,128]{2,1,0:T(8,128)} %sums.1), calls=%async_computation.1 | async-start | bytes 65536 | tf_op jit(solution)/shard_map/all_to_all | solution.py:332
  30.9 4.5 %collective-permute-start.3 = (bf16[4,208,512]{2,1,0:T(8,128)(2,1)}, bf16[4,208,512]{2,1,0:T(8,128)(2,1)S(1)}, u32[]{:S(2)}, u32[]{:S(2)}) collective-permute-start(bf16[4,208,512]{2,1,0:T(8,128)(2,1)} %pad_maximum_fusion.1), channel_id=1, source_target_pairs={{0,1},{1,0},{2,3},{3,2},{4,5},{5,4},{6,7},{7,6},{8,9},{9,8},{10,11... | collective-permute-start | bytes 2555912 | tf_op jit(solution)/shard_map/ppermute | solution.py:269
  38.2 31.3 %copy-start = (bf16[416,512]{1,0:T(8,128)(2,1)}, bf16[416,512]{1,0:T(8,128)(2,1)S(1)}, u32[]{:S(2)}) copy-start(bf16[416,512]{1,0:T(8,128)(2,1)S(1)} %get-tuple-element.26.own_ref) | copy-start | bytes 1277956
  38.2 44.6 %all-to-all-start.2 = ((bf16[8,704,128]{2,1,0:T(8,128)(2,1)}), bf16[8,704,128]{2,1,0:T(8,128)(2,1)S(1)}, u32[]{:S(2)}, u32[]{:S(2)}) async-start(bf16[8,704,128]{2,1,0:T(8,128)(2,1)} %get-tuple-element.25), calls=%async_computation.2 | async-start | bytes 2883584 | tf_op jit(solution)/shard_map/all_to_all | solution.py:359
  45.3 16.1 %collective-permute-start.6 = (bf16[416,512]{1,0:T(8,128)(2,1)S(1)}, bf16[416,512]{1,0:T(8,128)(2,1)S(1)}, u32[]{:S(2)}, u32[]{:S(2)}) collective-permute-start(bf16[416,512]{1,0:T(8,128)(2,1)S(1)} %get-tuple-element.26.own_ref), channel_id=1, source_target_pairs={{0,4},{2,6},{4,0},{6,2},{1,5},{3,7},{5,1},{7,3},{8,12},{10,14},{12... | collective-permute-start | bytes 1277960 | tf_op jit(solution)/shard_map/ppermute | solution.py:264
  49.6 19.9 %collective-permute-start.5 = (bf16[416,512]{1,0:T(8,128)(2,1)S(1)}, bf16[416,512]{1,0:T(8,128)(2,1)S(1)}, u32[]{:S(2)}, u32[]{:S(2)}) collective-permute-start(bf16[416,512]{1,0:T(8,128)(2,1)S(1)} %get-tuple-element.26.own_ref), channel_id=1, source_target_pairs={{0,6},{2,0},{4,2},{6,4},{1,7},{3,1},{5,3},{7,5},{8,14},{10,8},{12,... | collective-permute-start | bytes 1277960 | tf_op jit(solution)/shard_map/ppermute | solution.py:264
  52.1 17.4 %collective-permute-start.4 = (bf16[416,512]{1,0:T(8,128)(2,1)S(1)}, bf16[416,512]{1,0:T(8,128)(2,1)S(1)}, u32[]{:S(2)}, u32[]{:S(2)}) collective-permute-start(bf16[416,512]{1,0:T(8,128)(2,1)S(1)} %get-tuple-element.26.own_ref), channel_id=1, source_target_pairs={{0,2},{2,4},{4,6},{6,0},{1,3},{3,5},{5,7},{7,1},{8,10},{10,12},{12... | collective-permute-start | bytes 1277960 | tf_op jit(solution)/shard_map/ppermute | solution.py:264
  61.4 9.6 %copy-start.2 = (bf16[416,512]{1,0:T(8,128)(2,1)}, bf16[416,512]{1,0:T(8,128)(2,1)S(1)}, u32[]{:S(2)}) copy-start(bf16[416,512]{1,0:T(8,128)(2,1)S(1)} %collective-permute-done.6.far_ref) | copy-start | bytes 1277956
  69.5 1.5 %copy-start.4 = (bf16[416,512]{1,0:T(8,128)(2,1)}, bf16[416,512]{1,0:T(8,128)(2,1)S(1)}, u32[]{:S(2)}) copy-start(bf16[416,512]{1,0:T(8,128)(2,1)S(1)} %collective-permute-done.5.after_ref) | copy-start | bytes 1277956
  69.5 1.5 %copy-start.6 = (bf16[416,512]{1,0:T(8,128)(2,1)}, bf16[416,512]{1,0:T(8,128)(2,1)S(1)}, u32[]{:S(2)}) copy-start(bf16[416,512]{1,0:T(8,128)(2,1)S(1)} %collective-permute-done.4.before_ref) | copy-start | bytes 1277956
  71.0 27.5 %collective-permute-start.7 = (bf16[4,416,512]{2,1,0:T(8,128)(2,1)}, bf16[4,416,512]{2,1,0:T(8,128)(2,1)S(1)}, u32[]{:S(2)}, u32[]{:S(2)}) collective-permute-start(bf16[4,416,512]{2,1,0:T(8,128)(2,1)} %pad_maximum_fusion), channel_id=1, source_target_pairs={{0,1},{1,0},{2,3},{3,2},{4,5},{5,4},{6,7},{7,6},{8,9},{9,8},{10,11... | collective-permute-start | bytes 5111816 | tf_op jit(solution)/shard_map/ppermute | solution.py:269
  83.7 31.6 %all-to-all-start.3 = ((bf16[12,48,256]{2,1,0:T(8,128)(2,1)}), bf16[12,48,256]{2,1,0:T(8,128)(2,1)S(1)}, u32[]{:S(2)}, u32[]{:S(2)}) async-start(bf16[12,48,256]{2,1,0:T(8,128)(2,1)} %fold.1), calls=%async_computation.3 | async-start | bytes 589824 | tf_op jit(solution)/shard_map/all_to_all | solution.py:369
  98.5 1.0 copy-start.1
  99.5 1.0 copy-start.3
  100.5 1.0 copy-start.5
  101.6 1.0 copy-start.7
  102.6 1.3 copy-start.8
  115.4 18.2 %collective-permute-start.8 = (f32[64,256]{1,0:T(8,128)S(1)}, f32[64,256]{1,0:T(8,128)S(1)}, u32[]{:S(2)}, u32[]{:S(2)}) collective-permute-start(f32[64,256]{1,0:T(8,128)S(1)} %get-tuple-element.32), channel_id=1, source_target_pairs={{0,0},{1,96},{2,192},{3,288},{4,384},{5,480},{6,576},{7,672},{8,1}... | collective-permute-start | bytes 196616 | tf_op jit(solution)/shard_map/ppermute | solution.py:399

commit v8 on v7

--- a/solution.py
+++ b/solution.py
@@ -121,8 +121,9 @@
 COLS, GROUP, GAIN = 208, 48, 16
 AT1, AT2, AT3 = COLS, 2 * COLS, 3 * COLS
 AT4 = AT3 + GROUP
-AT5 = AT4 + GAIN
-MESSAGE = AT5 + GAIN
+MESSAGE = AT4 + GAIN
+THIRD = 72
+SPARE = 3 * BLOCK
 
 
 def branch_kernel(
@@ -154,14 +155,12 @@
         branch_ref[tile * VT : (tile + 1) * VT, :] = branch.astype(BF16)
     gain = jnp.concatenate([jnp.sum(g, axis=0, keepdims=True) for g in gains], axis=0)
     gain = jnp.concatenate([gain[:, q * 128 : (q + 1) * 128] for q in range(4)], axis=0)
-    gain_high = gain.astype(BF16)
-    gain_out_ref[0:GAIN, :] = gain_high
-    gain_out_ref[GAIN : 2 * GAIN, :] = (gain - gain_high.astype(F32)).astype(BF16)
+    gain_out_ref[...] = gain.astype(BF16)
 
 
 def terms_kernel(
     parts_ref, branch_ref, gain_ref, own_ref, before_ref, after_ref, far_ref, other_ref,
-    turned_ref, terms_ref,
+    terms_ref,
 ):
     attns = [own_ref, before_ref, after_ref, far_ref] + [other_ref.at[p] for p in range(4)]
     for place, attn in enumerate(attns):
@@ -177,32 +176,60 @@
         rest = jnp.concatenate([rest[0:16] + tail, rest[16:]], axis=0)
         terms_ref[part, AT3:AT4, :] = rest.astype(BF16)
         terms_ref[part, AT4:MESSAGE, :] = gain_ref[...]
+
+
+def turn_kernel(branch_ref, turned_ref):
     turned_ref[...] = branch_ref[...].T[:ROWS]
 
 
-def fold_kernel(recv_ref, out_ref, wide_ref):
+def left(array, lanes):
+    lanes = lanes % 128
+    return pltpu.roll(array, 128 - lanes, 1) if lanes else array
+
+
+def fold_kernel(recv_ref, out_ref):
     total = recv_ref[0].astype(F32)
     for part in range(1, NY):
         total = total + recv_ref[part].astype(F32)
     rest = total[AT3:AT4]
-    rest = [rest] + [pltpu.roll(rest, 128 - 24 * g, 1) for g in range(1, 5)]
+    rest = [left(rest, 24 * g) for g in range(5)]
     rest = jnp.concatenate(rest[:4] + [rest[4][0:16]], axis=0)
-    wide = jnp.concatenate([total[0:AT1], total[AT1:AT2], total[AT2:AT3], rest], axis=1)
-    wide = jnp.concatenate([wide, jnp.zeros((256 - COLS, WIDE), F32)], axis=0)
-    wide_ref[...] = wide.T
-    gain = total[AT4:AT5] + total[AT5:MESSAGE]
-    gain = jnp.concatenate([gain[0:8], gain[8:16]], axis=1)
+    tiles = [total[0:AT1], total[AT1:AT2], total[AT2:AT3], rest]
+    gain = total[AT4:MESSAGE]
+    gains = [left(gain[0:12], 26 * e - SPARE) for e in range(5)] + [left(gain[12:16], -SPARE)]
+    gains = jnp.concatenate(gains + [jnp.zeros((THIRD - 64, 128), F32)], axis=0)
+    lane = lax.broadcasted_iota(jnp.int32, (THIRD, 128), 1)
     for z in range(NZ):
-        rows = wide_ref[z * BLOCK : z * BLOCK + 40, :]
-        out_ref[z] = jnp.concatenate([rows, gain], axis=0).astype(BF16)
+        tile, at = divmod(z * BLOCK, 128)
+        packed = gains
+        for group in range(3):
+            rows = slice(group * THIRD, min(COLS, (group + 1) * THIRD))
+            shift = at - group * BLOCK
+            piece = left(tiles[tile][rows], shift)
+            if at + BLOCK > 128:
+                inside = lane[: piece.shape[0]] < group * BLOCK + 128 - at
+                piece = jnp.where(inside, piece, left(tiles[tile + 1][rows], shift))
+            if group == 2:
+                piece = jnp.concatenate([piece, jnp.zeros((3 * THIRD - COLS, 128), F32)], axis=0)
+            inside = (lane >= group * BLOCK) & (lane < (group + 1) * BLOCK)
+            packed = jnp.where(inside, piece, packed)
+        out_ref[z] = packed.astype(BF16)
 
 
 def settle_kernel(recv_ref, block_ref, gain_ref):
     total = recv_ref[0].astype(F32)
     for part in range(1, NZ):
         total = total + recv_ref[part].astype(F32)
-    block_ref[...] = jnp.concatenate([total, jnp.zeros((16, 256), F32)], axis=0)
-    gain = jnp.concatenate([total[40:48, 0:128], total[40:48, 128:256]], axis=0)
+    block = [total, left(total, BLOCK), left(total, 2 * BLOCK)[0 : COLS - 2 * THIRD]]
+    block = jnp.concatenate(block + [jnp.zeros((256 - COLS, 128), F32)], axis=0).T
+    block_ref[...] = block[0 : block_ref.shape[0]]
+    lane = lax.broadcasted_iota(jnp.int32, (12, 128), 1)
+    gain = jnp.zeros((12, 128), F32)
+    for e in range(5):
+        inside = (lane >= 26 * e) & (lane < 26 * e + 26)
+        gain = jnp.where(inside, left(total[12 * e : 12 * e + 12], SPARE - 26 * e), gain)
+    rest = jnp.where(lane[0:4] < FEAT - 384, left(total[60:64], SPARE), 0.0)
+    gain = jnp.concatenate([gain, rest], axis=0)
     for part in range(NMP):
         gain_ref[part] = gain
 
@@ -337,21 +364,18 @@
         branch_kernel,
         out_shape=(
             jax.ShapeDtypeStruct((TILES * VT, WIDE), BF16),
-            jax.ShapeDtypeStruct((2 * GAIN, 128), BF16),
+            jax.ShapeDtypeStruct((GAIN, 128), BF16),
         ),
         in_specs=scalars(2) + whole(4),
         out_specs=tuple(whole(2)),
         compiler_params=VMEM,
         name="branch",
     )(source, live, recv, gain, scale, sums)
-    turned, terms = pl.pallas_call(
+    terms = pl.pallas_call(
         terms_kernel,
-        out_shape=(
-            jax.ShapeDtypeStruct((ROWS, TILES * VT), BF16),
-            jax.ShapeDtypeStruct((NMP, MESSAGE, 128), BF16),
-        ),
+        out_shape=jax.ShapeDtypeStruct((NMP, MESSAGE, 128), BF16),
         in_specs=scalars(1) + whole(7),
-        out_specs=tuple(whole(2)),
+        out_specs=whole(1)[0],
         compiler_params=VMEM,
         name="terms",
     )(parts, branch, gains, *attns)
@@ -359,15 +383,22 @@
     terms = lax.all_to_all(terms, "y", 0, 0)
     terms = pl.pallas_call(
         fold_kernel,
-        out_shape=jax.ShapeDtypeStruct((NZ, 48, 256), BF16),
+        out_shape=jax.ShapeDtypeStruct((NZ, THIRD, 128), BF16),
         in_specs=whole(1),
         out_specs=whole(1)[0],
-        scratch_shapes=[pltpu.VMEM((WIDE, 256), F32)],
         compiler_params=VMEM,
         name="fold",
     )(terms)
     terms = lax.all_to_all(terms, "z", 0, 0)
 
+    turned = pl.pallas_call(
+        turn_kernel,
+        out_shape=jax.ShapeDtypeStruct((ROWS, TILES * VT), BF16),
+        in_specs=whole(1),
+        out_specs=whole(1)[0],
+        compiler_params=VMEM,
+        name="turn",
+    )(branch)
     turned = (turned,) + gather_x(turned)
     turned = turned + (swap_cores(jnp.stack(turned)),)
     attn_grad, residual_grad = pl.pallas_call(

time: 135 us -> 132 us (0.978)
  waiting for transfers between devices: 43.1 us -> 39.9 us
    all_to_all x1, waiting for transfers between devices: 8.77 us -> 6.69 us  [body(): terms = lax.all_to_all(terms, 'z', 0, 0)]
    pallas_call x2 -> x3, Pallas kernels: 3.78 us -> 3.31 us  [the longest x1 2.76 us: body(): pl.pallas_call(terms_kernel, out_shape=jax.ShapeDtypeStruct((NMP, MESSAGE...]
    unnamed x26 -> x24, local copies, waits for them, and re-layouts: 5.37 us -> 5.04 us
where the time goes in v8:
time: 132 us; the launch traced here: 131 us
  starting transfers between devices  59.3 us (45%)
  waiting for transfers between devices  39.9 us (30%)
  Pallas kernels  12.5 us (9%)
  blocking collectives  8.07 us (6%)
  local copies, waits for them, and re-layouts  7.06 us (5%)
  other arithmetic  2.96 us (2%)
  between operations  1.52 us (1%)
    ppermute x6, starting transfers between devices, gather_x(): lax.ppermute(own, 'x', [(x, (x + step) % 4) for x in range(4)])  18.7 us
    ppermute x6, waiting for transfers between devices, gather_x(): lax.ppermute(own, 'x', [(x, (x + step) % 4) for x in range(4)])  15.1 us
    all_to_all x1, starting transfers between devices, body(): terms = lax.all_to_all(terms, 'z', 0, 0)  14.8 us
    all_to_all x1, waiting for transfers between devices, body(): terms = lax.all_to_all(terms, 'y', 0, 0)  8.91 us
    all_to_all x1, blocking collectives, body(): gains = lax.all_to_all(gains, MP, 0, 0)  8.07 us
    all_to_all x1, starting transfers between devices, body(): terms = lax.all_to_all(terms, 'y', 0, 0)  7.1 us
    all_to_all x1, starting transfers between devices, body(): sums = lax.all_to_all(sums, MP, 0, 0)  6.73 us
    all_to_all x1, waiting for transfers between devices, body(): terms = lax.all_to_all(terms, 'z', 0, 0)  6.69 us
  transfers between devices with their start and end apart: 13, of which 9 were waited for; matrix products, arithmetic and copies ran while one was open for 3% of the time, Pallas kernels for 5%

profile of v8, /device:TPU:68, one launch (start us, length us, event | category | flops | bytes accessed | tf_op | source)
XLA Modules:
  0.0 131.3 jit_solution(12650537898958771971)
XLA Ops:
  0.7 2.8 %cut.1 = bf16[8,416,128]{2,1,0:T(8,128)(2,1)} custom-call(bf16[16,12800]{1,0:T(8,128)(2,1)} %grad_hbm.1, bf16[16,12800]{1,0:T(8,128)(2,1)} %feat_hbm.1), custom_call_target="tpu_custom_call" | custom-call | tf_op jit(solution)/shard_map/cut/pallas_call | solution.py:317
  3.5 4.8 %all-to-all-start = ((bf16[8,416,128]{2,1,0:T(8,128)(2,1)}), bf16[8,416,128]{2,1,0:T(8,128)(2,1)S(1)}, u32[]{:S(2)}, u32[]{:S(2)}) async-start(bf16[8,416,128]{2,1,0:T(8,128)(2,1)} %cut.1), calls=%async_computation | async-start | bytes 1703936 | tf_op jit(solution)/shard_map/all_to_all | solution.py:332
  8.3 2.0 %collective-permute-start.2 = (bf16[208,512]{1,0:T(8,128)(2,1)S(1)}, bf16[208,512]{1,0:T(8,128)(2,1)S(1)}, u32[]{:S(2)}, u32[]{:S(2)}) collective-permute-start(bf16[208,512]{1,0:T(8,128)(2,1)S(1)} %bitcast.25), channel_id=1, source_target_pairs={{0,4},{2,6},{4,0},{6,2},{1,5},{3,7},{5,1},{7,3},{8,12},{10,14},{12... | collective-permute-start | bytes 638984 | tf_op jit(solution)/shard_map/ppermute | solution.py:291
  10.4 4.5 %collective-permute-start.1 = (bf16[208,512]{1,0:T(8,128)(2,1)S(1)}, bf16[208,512]{1,0:T(8,128)(2,1)S(1)}, u32[]{:S(2)}, u32[]{:S(2)}) collective-permute-start(bf16[208,512]{1,0:T(8,128)(2,1)S(1)} %bitcast.26), channel_id=1, source_target_pairs={{0,6},{2,0},{4,2},{6,4},{1,7},{3,1},{5,3},{7,5},{8,14},{10,8},{12,... | collective-permute-start | bytes 638984 | tf_op jit(solution)/shard_map/ppermute | solution.py:291
  14.9 1.9 %collective-permute-start = (bf16[208,512]{1,0:T(8,128)(2,1)S(1)}, bf16[208,512]{1,0:T(8,128)(2,1)S(1)}, u32[]{:S(2)}, u32[]{:S(2)}) collective-permute-start(bf16[208,512]{1,0:T(8,128)(2,1)S(1)} %bitcast.27), channel_id=1, source_target_pairs={{0,2},{2,4},{4,6},{6,0},{1,3},{3,5},{5,7},{7,1},{8,10},{10,12},{12... | collective-permute-start | bytes 638984 | tf_op jit(solution)/shard_map/ppermute | solution.py:291
  17.5 0.1 select_reduce_fusion.source_ref
  17.6 0.1 fusion.gain_ref
  17.7 1.5 %all-to-all-done.recv_ref = bf16[8,416,128]{2,1,0:T(8,128)(2,1)S(1)} async-done(((bf16[8,416,128]{2,1,0:T(8,128)(2,1)}), bf16[8,416,128]{2,1,0:T(8,128)(2,1)S(1)}, u32[]{:S(2)}, u32[]{:S(2)}) %all-to-all-start) | async-done | bytes 852000 | tf_op jit(solution)/shard_map/all_to_all | solution.py:332
  19.2 2.0 %sums.1 = f32[8,8,128]{2,1,0:T(8,128)} custom-call(s32[8]{0:T(128)S(1)} %select_reduce_fusion.source_ref, s32[8]{0:T(128)S(1)} %compare_convert_fusion.live_ref, bf16[8,416,128]{2,1,0:T(8,128)(2,1)S(1)} %all-to-all-done.recv_ref, f32[4,512]{1,0:T(4,128)S(1)} %fusion.gain_ref), custom_call_target="tpu_custom_call" | custom-call | tf_op jit(solution)/shard_map/sums/pallas_call | solution.py:351
  21.1 6.7 %all-to-all-start.1 = ((f32[8,8,128]{2,1,0:T(8,128)}), f32[8,8,128]{2,1,0:T(8,128)S(1)}, u32[]{:S(2)}, u32[]{:S(2)}) async-start(f32[8,8,128]{2,1,0:T(8,128)} %sums.1), calls=%async_computation.1 | async-start | bytes 65536 | tf_op jit(solution)/shard_map/all_to_all | solution.py:359
  27.9 0.0 collective-permute-done.2.far_ref
  27.9 1.1 collective-permute-done.1.after_ref
  29.0 1.0 pad_maximum_fusion.1
  30.0 0.9 all-to-all-done.1.sums_ref
  30.9 1.9 %collective-permute-start.3 = (bf16[4,208,512]{2,1,0:T(8,128)(2,1)}, bf16[4,208,512]{2,1,0:T(8,128)(2,1)S(1)}, u32[]{:S(2)}, u32[]{:S(2)}) collective-permute-start(bf16[4,208,512]{2,1,0:T(8,128)(2,1)} %pad_maximum_fusion.1), channel_id=1, source_target_pairs={{0,1},{1,0},{2,3},{3,2},{4,5},{5,4},{6,7},{7,6},{8,9},{9,8},{10,11... | collective-permute-start | bytes 2555912 | tf_op jit(solution)/shard_map/ppermute | solution.py:296
  32.8 0.1 broadcast_add_fusion
  32.9 0.1 pad_add_fusion.parts_ref
  33.0 0.1 fusion.1
  33.1 1.5 %branch.1 = (bf16[512,512]{1,0:T(8,128)(2,1)S(1)}, bf16[16,128]{1,0:T(8,128)(2,1)S(1)}) custom-call(s32[8]{0:T(128)S(1)} %select_reduce_fusion.source_ref, s32[8]{0:T(128)S(1)} %compare_convert_fusion.live_ref, bf16[8,416,128]{2,1,0:T(8,128)(2,1)S(1)} %all-to-all-done.recv_ref, f32[4,512]{1,0:T(4,128)S(1)} %fusion.gain_ref, f32[1,512]{1,0:T(1,128)S(1)} %bitcast.33, ...), custom_call_target="tpu_custom_call" | custom-call | tf_op jit(solution)/shard_map/branch/pallas_call | solution.py:363
  34.6 0.8 collective-permute-done.3.other_ref
  35.4 2.8 %terms.1 = bf16[8,688,128]{2,1,0:T(8,128)(2,1)} custom-call(s32[8]{0:T(128)S(1)} %pad_add_fusion.parts_ref, bf16[512,512]{1,0:T(8,128)(2,1)S(1)} %get-tuple-element.20.branch_ref, bf16[16,128]{1,0:T(8,128)(2,1)S(1)} %get-tuple-element.21.gain_ref, bf16[208,512]{1,0:T(8,128)(2,1)S(1)} %bitcast.29, bf16[208,512]{1,0:T(8,128)(2,1)S(1)} %collective-permute-done.before_ref, ...), custom_call_target="tpu_custom_call" | custom-call | tf_op jit(solution)/shard_map/terms/pallas_call | solution.py:374
  38.1 7.1 %all-to-all-start.2 = ((bf16[8,688,128]{2,1,0:T(8,128)(2,1)}), bf16[8,688,128]{2,1,0:T(8,128)(2,1)S(1)}, u32[]{:S(2)}, u32[]{:S(2)}) async-start(bf16[8,688,128]{2,1,0:T(8,128)(2,1)} %terms.1), calls=%async_computation.2 | async-start | bytes 2818048 | tf_op jit(solution)/shard_map/all_to_all | solution.py:383
  45.2 0.2 turn.1.own_ref
  45.4 4.3 %collective-permute-start.6 = (bf16[416,512]{1,0:T(8,128)(2,1)S(1)}, bf16[416,512]{1,0:T(8,128)(2,1)S(1)}, u32[]{:S(2)}, u32[]{:S(2)}) collective-permute-start(bf16[416,512]{1,0:T(8,128)(2,1)S(1)} %turn.1.own_ref), channel_id=1, source_target_pairs={{0,4},{2,6},{4,0},{6,2},{1,5},{3,7},{5,1},{7,3},{8,12},{10,14},{12... | collective-permute-start | bytes 1277960 | tf_op jit(solution)/shard_map/ppermute | solution.py:291
  49.8 2.5 %collective-permute-start.5 = (bf16[416,512]{1,0:T(8,128)(2,1)S(1)}, bf16[416,512]{1,0:T(8,128)(2,1)S(1)}, u32[]{:S(2)}, u32[]{:S(2)}) collective-permute-start(bf16[416,512]{1,0:T(8,128)(2,1)S(1)} %turn.1.own_ref), channel_id=1, source_target_pairs={{0,6},{2,0},{4,2},{6,4},{1,7},{3,1},{5,3},{7,5},{8,14},{10,8},{12,... | collective-permute-start | bytes 1277960 | tf_op jit(solution)/shard_map/ppermute | solution.py:291
  52.2 3.4 %collective-permute-start.4 = (bf16[416,512]{1,0:T(8,128)(2,1)S(1)}, bf16[416,512]{1,0:T(8,128)(2,1)S(1)}, u32[]{:S(2)}, u32[]{:S(2)}) collective-permute-start(bf16[416,512]{1,0:T(8,128)(2,1)S(1)} %turn.1.own_ref), channel_id=1, source_target_pairs={{0,2},{2,4},{4,6},{6,0},{1,3},{3,5},{5,7},{7,1},{8,10},{10,12},{12... | collective-permute-start | bytes 1277960 | tf_op jit(solution)/shard_map/ppermute | solution.py:291
  55.6 5.9 %collective-permute-done.6.far_ref = bf16[416,512]{1,0:T(8,128)(2,1)S(1)} collective-permute-done((bf16[416,512]{1,0:T(8,128)(2,1)S(1)}, bf16[416,512]{1,0:T(8,128)(2,1)S(1)}, u32[]{:S(2)}, u32[]{:S(2)}) %collective-permute-start.6) | collective-permute-done | bytes 426016 | tf_op jit(solution)/shard_map/ppermute | solution.py:291
  61.6 8.1 %collective-permute-done.5.after_ref = bf16[416,512]{1,0:T(8,128)(2,1)S(1)} collective-permute-done((bf16[416,512]{1,0:T(8,128)(2,1)S(1)}, bf16[416,512]{1,0:T(8,128)(2,1)S(1)}, u32[]{:S(2)}, u32[]{:S(2)}) %collective-permute-start.5) | collective-permute-done | bytes 426016 | tf_op jit(solution)/shard_map/ppermute | solution.py:291
  69.7 1.5 %pad_maximum_fusion = bf16[4,416,512]{2,1,0:T(8,128)(2,1)} fusion(bf16[1,416,512]{2,1,0:T(8,128)(2,1)S(1)} %bitcast.21, bf16[1,416,512]{2,1,0:T(8,128)(2,1)S(1)} %bitcast.22, bf16[1,416,512]{2,1,0:T(8,128)(2,1)S(1)} %bitcast.23, bf16[1,416,512]{2,1,0:T(8,128)(2,1)S(1)} %bitcast.20), kind=kLoop, calls=%fused_computation | loop fusion | flops 2555904 | bytes 3407872 | tf_op jit(solution)/shard_map/stack | solution.py:403
  71.2 1.9 %collective-permute-start.7 = (bf16[4,416,512]{2,1,0:T(8,128)(2,1)}, bf16[4,416,512]{2,1,0:T(8,128)(2,1)S(1)}, u32[]{:S(2)}, u32[]{:S(2)}) collective-permute-start(bf16[4,416,512]{2,1,0:T(8,128)(2,1)} %pad_maximum_fusion), channel_id=1, source_target_pairs={{0,1},{1,0},{2,3},{3,2},{4,5},{5,4},{6,7},{7,6},{8,9},{9,8},{10,11... | collective-permute-start | bytes 5111816 | tf_op jit(solution)/shard_map/ppermute | solution.py:296
  73.1 8.9 %all-to-all-done.2.recv_ref = bf16[8,688,128]{2,1,0:T(8,128)(2,1)S(1)} async-done(((bf16[8,688,128]{2,1,0:T(8,128)(2,1)}), bf16[8,688,128]{2,1,0:T(8,128)(2,1)S(1)}, u32[]{:S(2)}, u32[]{:S(2)}) %all-to-all-start.2) | async-done | bytes 1409056 | tf_op jit(solution)/shard_map/all_to_all | solution.py:383
  82.0 0.4 fold.1
  82.4 0.7 copy-done.7
  83.0 14.8 %all-to-all-start.3 = ((bf16[12,72,128]{2,1,0:T(8,128)(2,1)}), bf16[12,72,128]{2,1,0:T(8,128)(2,1)S(1)}, u32[]{:S(2)}, u32[]{:S(2)}) async-start(bf16[12,72,128]{2,1,0:T(8,128)(2,1)} %copy-done.7), calls=%async_computation.3 | async-start | bytes 442368 | tf_op jit(solution)/shard_map/all_to_all | solution.py:392
  97.9 0.7 broadcast_in_dim.44.scale_ref
  98.6 1.0 copy-done.1
  99.6 1.0 copy-done.3
  100.6 1.0 copy-done.5
  101.6 1.3 %copy-done.6 = bf16[3200,208]{0,1:T(8,128)(2,1)S(1)} copy-done((bf16[3200,208]{0,1:T(8,128)(2,1)S(1)}, bf16[3200,208]{0,1:T(8,128)(2,1)}, u32[]{:S(2)}) %copy-start.6) | copy-done | bytes 1331224
  103.0 2.7 %gathered.1 = (bf16[208,512]{1,0:T(8,128)(2,1)}, bf16[64,3200]{1,0:T(8,128)(2,1)}) custom-call(s32[1]{0:T(128)} %bitcast.12.tile_ref, s32[8]{0:T(128)S(1)} %pad_add_fusion.parts_ref, bf16[208,3200]{1,0:T(8,128)(2,1)S(1)} %bitcast.24, f32[1,3200]{1,0:T(1,128)S(1)} %broadcast_in_dim.44.scale_ref, bf16[416,512]{1,0:T(8,128)(2,1)S(1)} %turn.1.own_ref, ...), custom_call_target="tpu_custom_call" | custom-call | tf_op jit(solution)/shard_map/gathered/pallas_call | solution.py:404
  105.7 6.7 %all-to-all-done.3.recv_ref = bf16[12,72,128]{2,1,0:T(8,128)(2,1)S(1)} async-done(((bf16[12,72,128]{2,1,0:T(8,128)(2,1)}), bf16[12,72,128]{2,1,0:T(8,128)(2,1)S(1)}, u32[]{:S(2)}, u32[]{:S(2)}) %all-to-all-start.3) | async-done | bytes 221216 | tf_op jit(solution)/shard_map/all_to_all | solution.py:392
  112.4 0.2 settle.1
  112.5 3.3 %collective-permute-start.8 = (f32[64,256]{1,0:T(8,128)S(1)}, f32[64,256]{1,0:T(8,128)S(1)}, u32[]{:S(2)}, u32[]{:S(2)}) collective-permute-start(f32[64,256]{1,0:T(8,128)S(1)} %get-tuple-element.28), channel_id=1, source_target_pairs={{0,0},{1,96},{2,192},{3,288},{4,384},{5,480},{6,576},{7,672},{8,1}... | collective-permute-start | bytes 196616 | tf_op jit(solution)/shard_map/ppermute | solution.py:430
  115.8 8.1 %all_to_all.25.gain_ref = f32[8,16,128]{2,1,0:T(8,128)S(1)} all-to-all(f32[8,16,128]{2,1,0:T(8,128)S(1)} %get-tuple-element.29), channel_id=1, replica_groups=mesh['z'=12,'y'=8,'x'=4,'c'=2] {'x','c'}, dimensions={0} | all-to-all | bytes 131072 | tf_op jit(solution)/shard_map/all_to_all | solution.py:431
  123.9 0.1 spread.1
  124.0 0.6 reshape.21
  124.7 6.0 %collective-permute-done.8 = f32[64,256]{1,0:T(8,128)S(1)} collective-permute-done((f32[64,256]{1,0:T(8,128)S(1)}, f32[64,256]{1,0:T(8,128)S(1)}, u32[]{:S(2)}, u32[]{:S(2)}) %collective-permute-start.8) | collective-permute-done | bytes 65568 | tf_op jit(solution)/shard_map/ppermute | solution.py:430
  130.7 0.6 slice.4
  (26 shorter events, 0.1 us)
Async XLA Ops:
  0.6 7.7 %copy-start.8 = (bf16[512,208]{0,1:T(8,128)(2,1)S(1)}, bf16[512,208]{0,1:T(8,128)(2,1)}, u32[]{:S(2)}) copy-start(bf16[512,208]{0,1:T(8,128)(2,1)} %param.14) | copy-start | bytes 638980
  0.6 16.8 %copy-start.10 = (f32[12800]{0:T(1024)S(1)}, f32[12800]{0:T(1024)}, u32[]{:S(2)}) copy-start(f32[12800]{0:T(1024)} %param.12) | copy-start | bytes 153604
  0.7 16.9 %copy-start.11 = (s32[1,8]{1,0:T(1,128)S(1)}, s32[1,8]{1,0:T(1,128)}, u32[]{:S(2)}) copy-start(s32[1,8]{1,0:T(1,128)} %param.10) | copy-start | bytes 100
  3.5 15.7 %all-to-all-start = ((bf16[8,416,128]{2,1,0:T(8,128)(2,1)}), bf16[8,416,128]{2,1,0:T(8,128)(2,1)S(1)}, u32[]{:S(2)}, u32[]{:S(2)}) async-start(bf16[8,416,128]{2,1,0:T(8,128)(2,1)} %cut.1), calls=%async_computation | async-start | bytes 1703936 | tf_op jit(solution)/shard_map/all_to_all | solution.py:332
  8.3 24.7 %copy-start.9 = (f32[3200]{0:T(1024)S(1)}, f32[3200]{0:T(1024)}, u32[]{:S(2)}) copy-start(f32[3200]{0:T(1024)} %param.13) | copy-start | bytes 38404
  8.3 19.6 %collective-permute-start.2 = (bf16[208,512]{1,0:T(8,128)(2,1)S(1)}, bf16[208,512]{1,0:T(8,128)(2,1)S(1)}, u32[]{:S(2)}, u32[]{:S(2)}) collective-permute-start(bf16[208,512]{1,0:T(8,128)(2,1)S(1)} %bitcast.25), channel_id=1, source_target_pairs={{0,4},{2,6},{4,0},{6,2},{1,5},{3,7},{5,1},{7,3},{8,12},{10,14},{12... | collective-permute-start | bytes 638984 | tf_op jit(solution)/shard_map/ppermute | solution.py:291
  10.4 18.6 %collective-permute-start.1 = (bf16[208,512]{1,0:T(8,128)(2,1)S(1)}, bf16[208,512]{1,0:T(8,128)(2,1)S(1)}, u32[]{:S(2)}, u32[]{:S(2)}) collective-permute-start(bf16[208,512]{1,0:T(8,128)(2,1)S(1)} %bitcast.26), channel_id=1, source_target_pairs={{0,6},{2,0},{4,2},{6,4},{1,7},{3,1},{5,3},{7,5},{8,14},{10,8},{12,... | collective-permute-start | bytes 638984 | tf_op jit(solution)/shard_map/ppermute | solution.py:291
  14.9 14.1 %collective-permute-start = (bf16[208,512]{1,0:T(8,128)(2,1)S(1)}, bf16[208,512]{1,0:T(8,128)(2,1)S(1)}, u32[]{:S(2)}, u32[]{:S(2)}) collective-permute-start(bf16[208,512]{1,0:T(8,128)(2,1)S(1)} %bitcast.27), channel_id=1, source_target_pairs={{0,2},{2,4},{4,6},{6,0},{1,3},{3,5},{5,7},{7,1},{8,10},{10,12},{12... | collective-permute-start | bytes 638984 | tf_op jit(solution)/shard_map/ppermute | solution.py:291
  21.1 9.7 %all-to-all-start.1 = ((f32[8,8,128]{2,1,0:T(8,128)}), f32[8,8,128]{2,1,0:T(8,128)S(1)}, u32[]{:S(2)}, u32[]{:S(2)}) async-start(f32[8,8,128]{2,1,0:T(8,128)} %sums.1), calls=%async_computation.1 | async-start | bytes 65536 | tf_op jit(solution)/shard_map/all_to_all | solution.py:359
  30.9 4.5 %collective-permute-start.3 = (bf16[4,208,512]{2,1,0:T(8,128)(2,1)}, bf16[4,208,512]{2,1,0:T(8,128)(2,1)S(1)}, u32[]{:S(2)}, u32[]{:S(2)}) collective-permute-start(bf16[4,208,512]{2,1,0:T(8,128)(2,1)} %pad_maximum_fusion.1), channel_id=1, source_target_pairs={{0,1},{1,0},{2,3},{3,2},{4,5},{5,4},{6,7},{7,6},{8,9},{9,8},{10,11... | collective-permute-start | bytes 2555912 | tf_op jit(solution)/shard_map/ppermute | solution.py:296
  38.1 43.9 %all-to-all-start.2 = ((bf16[8,688,128]{2,1,0:T(8,128)(2,1)}), bf16[8,688,128]{2,1,0:T(8,128)(2,1)S(1)}, u32[]{:S(2)}, u32[]{:S(2)}) async-start(bf16[8,688,128]{2,1,0:T(8,128)(2,1)} %terms.1), calls=%async_computation.2 | async-start | bytes 2818048 | tf_op jit(solution)/shard_map/all_to_all | solution.py:383
  45.4 16.1 %collective-permute-start.6 = (bf16[416,512]{1,0:T(8,128)(2,1)S(1)}, bf16[416,512]{1,0:T(8,128)(2,1)S(1)}, u32[]{:S(2)}, u32[]{:S(2)}) collective-permute-start(bf16[416,512]{1,0:T(8,128)(2,1)S(1)} %turn.1.own_ref), channel_id=1, source_target_pairs={{0,4},{2,6},{4,0},{6,2},{1,5},{3,7},{5,1},{7,3},{8,12},{10,14},{12... | collective-permute-start | bytes 1277960 | tf_op jit(solution)/shard_map/ppermute | solution.py:291
  49.8 19.9 %collective-permute-start.5 = (bf16[416,512]{1,0:T(8,128)(2,1)S(1)}, bf16[416,512]{1,0:T(8,128)(2,1)S(1)}, u32[]{:S(2)}, u32[]{:S(2)}) collective-permute-start(bf16[416,512]{1,0:T(8,128)(2,1)S(1)} %turn.1.own_ref), channel_id=1, source_target_pairs={{0,6},{2,0},{4,2},{6,4},{1,7},{3,1},{5,3},{7,5},{8,14},{10,8},{12,... | collective-permute-start | bytes 1277960 | tf_op jit(solution)/shard_map/ppermute | solution.py:291
  52.2 17.4 %collective-permute-start.4 = (bf16[416,512]{1,0:T(8,128)(2,1)S(1)}, bf16[416,512]{1,0:T(8,128)(2,1)S(1)}, u32[]{:S(2)}, u32[]{:S(2)}) collective-permute-start(bf16[416,512]{1,0:T(8,128)(2,1)S(1)} %turn.1.own_ref), channel_id=1, source_target_pairs={{0,2},{2,4},{4,6},{6,0},{1,3},{3,5},{5,7},{7,1},{8,10},{10,12},{12... | collective-permute-start | bytes 1277960 | tf_op jit(solution)/shard_map/ppermute | solution.py:291
  61.6 9.6 %copy-start = (bf16[416,512]{1,0:T(8,128)(2,1)}, bf16[416,512]{1,0:T(8,128)(2,1)S(1)}, u32[]{:S(2)}) copy-start(bf16[416,512]{1,0:T(8,128)(2,1)S(1)} %collective-permute-done.6.far_ref) | copy-start | bytes 1277956
  69.7 1.5 %copy-start.2 = (bf16[416,512]{1,0:T(8,128)(2,1)}, bf16[416,512]{1,0:T(8,128)(2,1)S(1)}, u32[]{:S(2)}) copy-start(bf16[416,512]{1,0:T(8,128)(2,1)S(1)} %collective-permute-done.5.after_ref) | copy-start | bytes 1277956
  69.7 1.5 %copy-start.4 = (bf16[416,512]{1,0:T(8,128)(2,1)}, bf16[416,512]{1,0:T(8,128)(2,1)S(1)}, u32[]{:S(2)}) copy-start(bf16[416,512]{1,0:T(8,128)(2,1)S(1)} %collective-permute-done.4.before_ref) | copy-start | bytes 1277956
  71.2 27.4 %collective-permute-start.7 = (bf16[4,416,512]{2,1,0:T(8,128)(2,1)}, bf16[4,416,512]{2,1,0:T(8,128)(2,1)S(1)}, u32[]{:S(2)}, u32[]{:S(2)}) collective-permute-start(bf16[4,416,512]{2,1,0:T(8,128)(2,1)} %pad_maximum_fusion), channel_id=1, source_target_pairs={{0,1},{1,0},{2,3},{3,2},{4,5},{5,4},{6,7},{7,6},{8,9},{9,8},{10,11... | collective-permute-start | bytes 5111816 | tf_op jit(solution)/shard_map/ppermute | solution.py:296
  82.4 0.7 copy-start.7
  83.0 29.3 %all-to-all-start.3 = ((bf16[12,72,128]{2,1,0:T(8,128)(2,1)}), bf16[12,72,128]{2,1,0:T(8,128)(2,1)S(1)}, u32[]{:S(2)}, u32[]{:S(2)}) async-start(bf16[12,72,128]{2,1,0:T(8,128)(2,1)} %copy-done.7), calls=%async_computation.3 | async-start | bytes 442368 | tf_op jit(solution)/shard_map/all_to_all | solution.py:392
  98.6 1.0 copy-start.1
  99.6 1.0 copy-start.3
  100.6 1.0 copy-start.5
  101.6 1.3 %copy-start.6 = (bf16[3200,208]{0,1:T(8,128)(2,1)S(1)}, bf16[3200,208]{0,1:T(8,128)(2,1)}, u32[]{:S(2)}) copy-start(bf16[3200,208]{0,1:T(8,128)(2,1)} %param.15) | copy-start | bytes 3993604
  112.5 18.2 %collective-permute-start.8 = (f32[64,256]{1,0:T(8,128)S(1)}, f32[64,256]{1,0:T(8,128)S(1)}, u32[]{:S(2)}, u32[]{:S(2)}) collective-permute-start(f32[64,256]{1,0:T(8,128)S(1)} %get-tuple-element.28), channel_id=1, source_target_pairs={{0,0},{1,96},{2,192},{3,288},{4,384},{5,480},{6,576},{7,672},{8,1}... | collective-permute-start | bytes 196616 | tf_op jit(solution)/shard_map/ppermute | solution.py:430

commit v9 on v8

--- a/solution.py
+++ b/solution.py
@@ -19,6 +19,7 @@
 REST = 384
 TILES, PR, SUB, VT = 8, 16, 4, 64
 VMEM = pltpu.CompilerParams(vmem_limit_bytes=48 * 1024 * 1024)
+ROOMY = pltpu.CompilerParams(vmem_limit_bytes=56 * 1024 * 1024)
 F32, BF16 = jnp.float32, jnp.bfloat16
 
 
@@ -81,41 +82,52 @@
     return pieces, rest
 
 
-def slot_values(tile, source_ref, live_ref, recv_ref):
+def wide(array):
+    return jnp.concatenate([array] * (WIDE // 128), axis=1)
+
+
+def row_stats(recv_ref):
+    marks = jnp.concatenate([recv_ref[t, REST : REST + PR, :] for t in range(TILES)], axis=0)
+    low = 64 + FEAT - 384
+    lane = lax.broadcasted_iota(jnp.int32, (128, 256), 0)
+    which = lax.broadcasted_iota(jnp.int32, (128, 256), 1) >> 7
+    pick = (lane >= low + 3 * which) & (lane < low + 3 * which + 3)
+    return jnp.dot(marks, pick.astype(F32).astype(BF16), preferred_element_type=F32)
+
+
+def slot_values(tile, source_ref, live_ref, recv_ref, stats):
     pieces, rest = unpack(recv_ref, source_ref[tile], 0)
     rest = jnp.where(lax.broadcasted_iota(jnp.int32, (VT, 128), 1) < FEAT - 384, rest, 0.0)
     grads = jnp.concatenate(pieces + [rest], axis=1)
     grads = jnp.where(live_ref[tile] > 0, grads, 0.0)
     pieces, rest = unpack(recv_ref, tile, 1)
     feats = jnp.concatenate(pieces + [rest], axis=1)
-    marks = rest[0:PR]
-    lane = lax.broadcasted_iota(jnp.int32, (PR, 128), 1) + 384
-    in_mean = (lane >= FEAT) & (lane < FEAT + 3)
-    in_std = (lane >= FEAT + 3) & (lane < FEAT + 6)
-    mean = jnp.sum(jnp.where(in_mean, marks, 0.0), axis=-1, keepdims=True)
-    inverse_std = jnp.sum(jnp.where(in_std, marks, 0.0), axis=-1, keepdims=True)
+    mean = wide(stats[tile * PR : (tile + 1) * PR, 0:128])
+    inverse_std = wide(stats[tile * PR : (tile + 1) * PR, 128:256])
     upstream = [grads[s * PR : (s + 1) * PR] for s in range(SUB)]
     normed = [(feats[s * PR : (s + 1) * PR] - mean) * inverse_std for s in range(SUB)]
     return upstream, normed, inverse_std
 
 
 def sums_kernel(source_ref, live_ref, recv_ref, gain_ref, out_ref):
-    lane = lax.broadcasted_iota(jnp.int32, (PR, 128), 1)
-    rows = []
+    stats = row_stats(recv_ref)
+    firsts, seconds = [], []
     for tile in range(TILES):
-        upstream, normed, _ = slot_values(tile, source_ref, live_ref, recv_ref)
+        upstream, normed, _ = slot_values(tile, source_ref, live_ref, recv_ref, stats)
         first = jnp.zeros((PR, WIDE), F32)
         second = jnp.zeros((PR, WIDE), F32)
         for s in range(SUB):
             scaled = upstream[s] * gain_ref[s : s + 1, :]
             first = first + scaled
             second = second + scaled * normed[s]
-        first = jnp.sum(first, axis=-1, keepdims=True)
-        second = jnp.sum(second, axis=-1, keepdims=True)
-        rows.append(jnp.where(lane == 0, first, jnp.where(lane == 1, second, 0.0)))
-    turned = jnp.concatenate(rows, axis=0).T[0:8, :]
-    for part in range(NMP):
-        out_ref[part] = turned
+        firsts.append(sum(first[:, q * 128 : q * 128 + 128] for q in range(4)))
+        seconds.append(sum(second[:, q * 128 : q * 128 + 128] for q in range(4)))
+    first = jnp.sum(jnp.concatenate(firsts, axis=0).T, axis=0, keepdims=True)
+    second = jnp.sum(jnp.concatenate(seconds, axis=0).T, axis=0, keepdims=True)
+    row = lax.broadcasted_iota(jnp.int32, (8, 128), 0)
+    both = jnp.where(row == 0, first, jnp.where(row == 1, second, 0.0))
+    for part in range(NMP):
+        out_ref[part] = both
 
 
 COLS, GROUP, GAIN = 208, 48, 16
@@ -132,8 +144,10 @@
     total = sums_ref[0]
     for part in range(1, NMP):
         total = total + sums_ref[part]
-    means = jnp.concatenate([total, jnp.zeros((120, 128), F32)], axis=0).T * (1.0 / PW)
-    lane = lax.broadcasted_iota(jnp.int32, (PR, 128), 1)
+    total = total * (1.0 / PW)
+    firsts = jnp.broadcast_to(total[0:1], (128, 128)).T
+    seconds = jnp.broadcast_to(total[1:2], (128, 128)).T
+    stats = row_stats(recv_ref)
     token = lax.broadcasted_iota(jnp.int32, (VT, VT), 0)
     place = lax.broadcasted_iota(jnp.int32, (VT, VT), 1)
     sub_of = ((token >> 3) & 1) * 2 + (token & 1)
@@ -141,10 +155,9 @@
     order = (place == sub_of * PR + row_of).astype(BF16)
     gains = [jnp.zeros((PR, WIDE), F32) for _ in range(SUB)]
     for tile in range(TILES):
-        upstream, normed, inverse_std = slot_values(tile, source_ref, live_ref, recv_ref)
-        own = means[tile * PR : (tile + 1) * PR]
-        first = jnp.sum(jnp.where(lane == 0, own, 0.0), axis=-1, keepdims=True)
-        second = jnp.sum(jnp.where(lane == 1, own, 0.0), axis=-1, keepdims=True)
+        upstream, normed, inverse_std = slot_values(tile, source_ref, live_ref, recv_ref, stats)
+        first = wide(firsts[tile * PR : (tile + 1) * PR])
+        second = wide(seconds[tile * PR : (tile + 1) * PR])
         branch = []
         for s in range(SUB):
             scaled = upstream[s] * gain_ref[s : s + 1, :]
@@ -245,7 +258,10 @@
         if low > start:
             pieces = pltpu.roll(pieces, low - start, 1)
         wide_ref[:, start : start + 640] += pieces
-    out_ref[...] = wide_ref[:, 0:VW]
+    for sub in range(SUB):
+        for tile in range(VW // 128):
+            row = sub * (VW // 128) + tile
+            out_ref[row : row + 1, :] = wide_ref[sub : sub + 1, tile * 128 : tile * 128 + 128]
 
 
 def gathered_kernel(
@@ -386,7 +402,7 @@
         out_shape=jax.ShapeDtypeStruct((NZ, THIRD, 128), BF16),
         in_specs=whole(1),
         out_specs=whole(1)[0],
-        compiler_params=VMEM,
+        compiler_params=ROOMY,
         name="fold",
     )(terms)
     terms = lax.all_to_all(terms, "z", 0, 0)
@@ -431,7 +447,7 @@
     gains = lax.all_to_all(gains, MP, 0, 0)
     gain_grad = pl.pallas_call(
         spread_kernel,
-        out_shape=jax.ShapeDtypeStruct((SUB, VW), F32),
+        out_shape=jax.ShapeDtypeStruct((PW // 128, 128), F32),
         in_specs=whole(1),
         out_specs=whole(1)[0],
         scratch_shapes=[pltpu.VMEM((SUB, 3456), F32)],

time: 132 us -> 134 us (1.015)
  local copies, waits for them, and re-layouts: 7.06 us -> 1.99 us
  waiting for transfers between devices: 39.9 us -> 44.1 us
  Pallas kernels: 12.5 us -> 15.6 us
    all_to_all x1, waiting for transfers between devices: 6.69 us -> 10.5 us  [body(): terms = lax.all_to_all(terms, 'z', 0, 0)]
    unnamed x24 -> x10, local copies, waits for them, and re-layouts: 5.04 us -> 1.33 us
    pallas_call x1, Pallas kernels: 0.37 us -> 2.41 us  [body(): pl.pallas_call(fold_kernel, out_shape=jax.ShapeDtypeStruct((NZ, THIRD, 12...]
  transfers between devices with their start and end apart: 13 -> 13, of which waited for: 9 -> 9; matrix products, arithmetic and copies ran while one was open for 3% -> 2% of each run, Pallas kernels for 5% -> 7%
where the time goes in v9:
time: 134 us; the launch traced here: 133 us
  starting transfers between devices  59 us (44%)
  waiting for transfers between devices  44.1 us (33%)
  Pallas kernels  15.6 us (12%)
  blocking collectives  8.3 us (6%)
  other arithmetic  2.91 us (2%)
  local copies, waits for them, and re-layouts  1.99 us (1%)
  between operations  1.5 us (1%)
    ppermute x6, starting transfers between devices, gather_x(): lax.ppermute(own, 'x', [(x, (x + step) % 4) for x in range(4)])  18.7 us
    ppermute x6, waiting for transfers between devices, gather_x(): lax.ppermute(own, 'x', [(x, (x + step) % 4) for x in range(4)])  15.5 us
    all_to_all x1, starting transfers between devices, body(): terms = lax.all_to_all(terms, 'z', 0, 0)  14.8 us
    all_to_all x1, waiting for transfers between devices, body(): terms = lax.all_to_all(terms, 'z', 0, 0)  10.5 us
    all_to_all x1, waiting for transfers between devices, body(): terms = lax.all_to_all(terms, 'y', 0, 0)  9.07 us
    all_to_all x1, blocking collectives, body(): gains = lax.all_to_all(gains, MP, 0, 0)  8.3 us
    all_to_all x1, starting transfers between devices, body(): terms = lax.all_to_all(terms, 'y', 0, 0)  7.1 us
    all_to_all x1, starting transfers between devices, body(): sums = lax.all_to_all(sums, MP, 0, 0)  6.73 us
  transfers between devices with their start and end apart: 13, of which 9 were waited for; matrix products, arithmetic and copies ran while one was open for 2% of the time, Pallas kernels for 7%

profile of v9, /device:TPU:68, one launch (start us, length us, event | category | flops | bytes accessed | tf_op | source)
XLA Modules:
  0.0 133.5 jit_solution(1132413934930344344)
XLA Ops:
  0.6 0.0 copy-start.1
  0.6 0.0 copy-start.3
  0.7 2.8 %cut.1 = bf16[8,416,128]{2,1,0:T(8,128)(2,1)} custom-call(bf16[16,12800]{1,0:T(8,128)(2,1)} %grad_hbm.1, bf16[16,12800]{1,0:T(8,128)(2,1)} %feat_hbm.1), custom_call_target="tpu_custom_call" | custom-call | tf_op jit(solution)/shard_map/cut/pallas_call | solution.py:333
  3.5 4.8 %all-to-all-start = ((bf16[8,416,128]{2,1,0:T(8,128)(2,1)}), bf16[8,416,128]{2,1,0:T(8,128)(2,1)S(1)}, u32[]{:S(2)}, u32[]{:S(2)}) async-start(bf16[8,416,128]{2,1,0:T(8,128)(2,1)} %cut.1), calls=%async_computation | async-start | bytes 1703936 | tf_op jit(solution)/shard_map/all_to_all | solution.py:348
  8.3 2.0 %collective-permute-start.2 = (bf16[208,512]{1,0:T(8,128)(2,1)S(1)}, bf16[208,512]{1,0:T(8,128)(2,1)S(1)}, u32[]{:S(2)}, u32[]{:S(2)}) collective-permute-start(bf16[208,512]{1,0:T(8,128)(2,1)S(1)} %bitcast.26), channel_id=1, source_target_pairs={{0,4},{2,6},{4,0},{6,2},{1,5},{3,7},{5,1},{7,3},{8,12},{10,14},{12... | collective-permute-start | bytes 638984 | tf_op jit(solution)/shard_map/ppermute | solution.py:307
  10.3 4.5 %collective-permute-start.1 = (bf16[208,512]{1,0:T(8,128)(2,1)S(1)}, bf16[208,512]{1,0:T(8,128)(2,1)S(1)}, u32[]{:S(2)}, u32[]{:S(2)}) collective-permute-start(bf16[208,512]{1,0:T(8,128)(2,1)S(1)} %bitcast.27), channel_id=1, source_target_pairs={{0,6},{2,0},{4,2},{6,4},{1,7},{3,1},{5,3},{7,5},{8,14},{10,8},{12,... | collective-permute-start | bytes 638984 | tf_op jit(solution)/shard_map/ppermute | solution.py:307
  14.9 1.9 %collective-permute-start = (bf16[208,512]{1,0:T(8,128)(2,1)S(1)}, bf16[208,512]{1,0:T(8,128)(2,1)S(1)}, u32[]{:S(2)}, u32[]{:S(2)}) collective-permute-start(bf16[208,512]{1,0:T(8,128)(2,1)S(1)} %bitcast.28), channel_id=1, source_target_pairs={{0,2},{2,4},{4,6},{6,0},{1,3},{3,5},{5,7},{7,1},{8,10},{10,12},{12... | collective-permute-start | bytes 638984 | tf_op jit(solution)/shard_map/ppermute | solution.py:307
  17.5 0.1 select_reduce_fusion.source_ref
  17.6 0.1 fusion.gain_ref
  17.7 1.5 %all-to-all-done.recv_ref = bf16[8,416,128]{2,1,0:T(8,128)(2,1)S(1)} async-done(((bf16[8,416,128]{2,1,0:T(8,128)(2,1)}), bf16[8,416,128]{2,1,0:T(8,128)(2,1)S(1)}, u32[]{:S(2)}, u32[]{:S(2)}) %all-to-all-start) | async-done | bytes 852000 | tf_op jit(solution)/shard_map/all_to_all | solution.py:348
  19.2 1.6 %sums.1 = f32[8,8,128]{2,1,0:T(8,128)} custom-call(s32[8]{0:T(128)S(1)} %select_reduce_fusion.source_ref, s32[8]{0:T(128)S(1)} %compare_convert_fusion.live_ref, bf16[8,416,128]{2,1,0:T(8,128)(2,1)S(1)} %all-to-all-done.recv_ref, f32[4,512]{1,0:T(4,128)S(1)} %fusion.gain_ref), custom_call_target="tpu_custom_call" | custom-call | tf_op jit(solution)/shard_map/sums/pallas_call | solution.py:367
  20.8 6.7 %all-to-all-start.1 = ((f32[8,8,128]{2,1,0:T(8,128)}), f32[8,8,128]{2,1,0:T(8,128)S(1)}, u32[]{:S(2)}, u32[]{:S(2)}) async-start(f32[8,8,128]{2,1,0:T(8,128)} %sums.1), calls=%async_computation.1 | async-start | bytes 65536 | tf_op jit(solution)/shard_map/all_to_all | solution.py:375
  27.5 0.0 collective-permute-done.2.far_ref
  27.5 1.4 %collective-permute-done.1.after_ref = bf16[208,512]{1,0:T(8,128)(2,1)S(1)} collective-permute-done((bf16[208,512]{1,0:T(8,128)(2,1)S(1)}, bf16[208,512]{1,0:T(8,128)(2,1)S(1)}, u32[]{:S(2)}, u32[]{:S(2)}) %collective-permute-start.1) | collective-permute-done | bytes 213024 | tf_op jit(solution)/shard_map/ppermute | solution.py:307
  28.9 0.0 collective-permute-done.before_ref
  29.0 1.0 pad_maximum_fusion.1
  30.0 0.6 all-to-all-done.1.sums_ref
  30.5 1.9 %collective-permute-start.3 = (bf16[4,208,512]{2,1,0:T(8,128)(2,1)}, bf16[4,208,512]{2,1,0:T(8,128)(2,1)S(1)}, u32[]{:S(2)}, u32[]{:S(2)}) collective-permute-start(bf16[4,208,512]{2,1,0:T(8,128)(2,1)} %pad_maximum_fusion.1), channel_id=1, source_target_pairs={{0,1},{1,0},{2,3},{3,2},{4,5},{5,4},{6,7},{7,6},{8,9},{9,8},{10,11... | collective-permute-start | bytes 2555912 | tf_op jit(solution)/shard_map/ppermute | solution.py:312
  32.5 0.1 broadcast_add_fusion
  32.6 0.1 pad_add_fusion.parts_ref
  32.6 0.1 fusion.1
  32.7 1.3 branch.1
  34.0 1.0 collective-permute-done.3.other_ref
  35.0 2.8 %terms.1 = bf16[8,688,128]{2,1,0:T(8,128)(2,1)} custom-call(s32[8]{0:T(128)S(1)} %pad_add_fusion.parts_ref, bf16[512,512]{1,0:T(8,128)(2,1)S(1)} %get-tuple-element.20.branch_ref, bf16[16,128]{1,0:T(8,128)(2,1)S(1)} %get-tuple-element.21.gain_ref, bf16[208,512]{1,0:T(8,128)(2,1)S(1)} %bitcast.30, bf16[208,512]{1,0:T(8,128)(2,1)S(1)} %collective-permute-done.before_ref, ...), custom_call_target="tpu_custom_call" | custom-call | tf_op jit(solution)/shard_map/terms/pallas_call | solution.py:390
  37.8 7.1 %all-to-all-start.2 = ((bf16[8,688,128]{2,1,0:T(8,128)(2,1)}), bf16[8,688,128]{2,1,0:T(8,128)(2,1)}, u32[]{:S(2)}, u32[]{:S(2)}) async-start(bf16[8,688,128]{2,1,0:T(8,128)(2,1)} %terms.1), calls=%async_computation.2 | async-start | bytes 2818048 | tf_op jit(solution)/shard_map/all_to_all | solution.py:399
  44.9 0.2 turn.1.own_ref
  45.1 4.3 %collective-permute-start.6 = (bf16[416,512]{1,0:T(8,128)(2,1)S(1)}, bf16[416,512]{1,0:T(8,128)(2,1)S(1)}, u32[]{:S(2)}, u32[]{:S(2)}) collective-permute-start(bf16[416,512]{1,0:T(8,128)(2,1)S(1)} %turn.1.own_ref), channel_id=1, source_target_pairs={{0,4},{2,6},{4,0},{6,2},{1,5},{3,7},{5,1},{7,3},{8,12},{10,14},{12... | collective-permute-start | bytes 1277960 | tf_op jit(solution)/shard_map/ppermute | solution.py:307
  49.4 2.5 %collective-permute-start.5 = (bf16[416,512]{1,0:T(8,128)(2,1)S(1)}, bf16[416,512]{1,0:T(8,128)(2,1)S(1)}, u32[]{:S(2)}, u32[]{:S(2)}) collective-permute-start(bf16[416,512]{1,0:T(8,128)(2,1)S(1)} %turn.1.own_ref), channel_id=1, source_target_pairs={{0,6},{2,0},{4,2},{6,4},{1,7},{3,1},{5,3},{7,5},{8,14},{10,8},{12,... | collective-permute-start | bytes 1277960 | tf_op jit(solution)/shard_map/ppermute | solution.py:307
  51.9 3.4 %collective-permute-start.4 = (bf16[416,512]{1,0:T(8,128)(2,1)S(1)}, bf16[416,512]{1,0:T(8,128)(2,1)S(1)}, u32[]{:S(2)}, u32[]{:S(2)}) collective-permute-start(bf16[416,512]{1,0:T(8,128)(2,1)S(1)} %turn.1.own_ref), channel_id=1, source_target_pairs={{0,2},{2,4},{4,6},{6,0},{1,3},{3,5},{5,7},{7,1},{8,10},{10,12},{12... | collective-permute-start | bytes 1277960 | tf_op jit(solution)/shard_map/ppermute | solution.py:307
  55.3 5.9 %collective-permute-done.6.far_ref = bf16[416,512]{1,0:T(8,128)(2,1)S(1)} collective-permute-done((bf16[416,512]{1,0:T(8,128)(2,1)S(1)}, bf16[416,512]{1,0:T(8,128)(2,1)S(1)}, u32[]{:S(2)}, u32[]{:S(2)}) %collective-permute-start.6) | collective-permute-done | bytes 426016 | tf_op jit(solution)/shard_map/ppermute | solution.py:307
  61.2 8.1 %collective-permute-done.5.after_ref = bf16[416,512]{1,0:T(8,128)(2,1)S(1)} collective-permute-done((bf16[416,512]{1,0:T(8,128)(2,1)S(1)}, bf16[416,512]{1,0:T(8,128)(2,1)S(1)}, u32[]{:S(2)}, u32[]{:S(2)}) %collective-permute-start.5) | collective-permute-done | bytes 426016 | tf_op jit(solution)/shard_map/ppermute | solution.py:307
  69.3 0.0 collective-permute-done.4.before_ref
  69.3 1.4 %pad_maximum_fusion = bf16[4,416,512]{2,1,0:T(8,128)(2,1)} fusion(bf16[1,416,512]{2,1,0:T(8,128)(2,1)S(1)} %bitcast.22, bf16[1,416,512]{2,1,0:T(8,128)(2,1)S(1)} %bitcast.23, bf16[1,416,512]{2,1,0:T(8,128)(2,1)S(1)} %bitcast.24, bf16[1,416,512]{2,1,0:T(8,128)(2,1)S(1)} %bitcast.21), kind=kLoop, calls=%fused_computation | loop fusion | flops 2555904 | bytes 3407872 | tf_op jit(solution)/shard_map/stack | solution.py:419
  70.7 1.9 %collective-permute-start.7 = (bf16[4,416,512]{2,1,0:T(8,128)(2,1)}, bf16[4,416,512]{2,1,0:T(8,128)(2,1)S(1)}, u32[]{:S(2)}, u32[]{:S(2)}) collective-permute-start(bf16[4,416,512]{2,1,0:T(8,128)(2,1)} %pad_maximum_fusion), channel_id=1, source_target_pairs={{0,1},{1,0},{2,3},{3,2},{4,5},{5,4},{6,7},{7,6},{8,9},{9,8},{10,11... | collective-permute-start | bytes 5111816 | tf_op jit(solution)/shard_map/ppermute | solution.py:312
  72.7 9.1 %all-to-all-done.2.recv_ref = bf16[8,688,128]{2,1,0:T(8,128)(2,1)} async-done(((bf16[8,688,128]{2,1,0:T(8,128)(2,1)}), bf16[8,688,128]{2,1,0:T(8,128)(2,1)}, u32[]{:S(2)}, u32[]{:S(2)}) %all-to-all-start.2) | async-done | bytes 1409056 | tf_op jit(solution)/shard_map/all_to_all | solution.py:399
  81.7 2.4 %fold.1 = bf16[12,72,128]{2,1,0:T(8,128)(2,1)} custom-call(bf16[8,688,128]{2,1,0:T(8,128)(2,1)} %all-to-all-done.2.recv_ref), custom_call_target="tpu_custom_call" | custom-call | tf_op jit(solution)/shard_map/fold/pallas_call | solution.py:400
  84.1 14.8 %all-to-all-start.3 = ((bf16[12,72,128]{2,1,0:T(8,128)(2,1)}), bf16[12,72,128]{2,1,0:T(8,128)(2,1)}, u32[]{:S(2)}, u32[]{:S(2)}) async-start(bf16[12,72,128]{2,1,0:T(8,128)(2,1)} %fold.1), calls=%async_computation.3 | async-start | bytes 442368 | tf_op jit(solution)/shard_map/all_to_all | solution.py:408
  99.0 0.0 collective-permute-done.7.other_ref
  99.0 0.0 copy-start
  99.0 1.3 copy-done
  100.3 2.7 %gathered.1 = (bf16[208,512]{1,0:T(8,128)(2,1)}, bf16[64,3200]{1,0:T(8,128)(2,1)}) custom-call(s32[1]{0:T(128)} %bitcast.12.tile_ref, s32[8]{0:T(128)S(1)} %pad_add_fusion.parts_ref, bf16[208,3200]{1,0:T(8,128)(2,1)S(1)} %bitcast.25, f32[1,3200]{1,0:T(1,128)S(1)} %broadcast_in_dim.44.scale_ref, bf16[416,512]{1,0:T(8,128)(2,1)S(1)} %turn.1.own_ref, ...), custom_call_target="tpu_custom_call" | custom-call | tf_op jit(solution)/shard_map/gathered/pallas_call | solution.py:420
  103.0 10.5 %all-to-all-done.3.recv_ref = bf16[12,72,128]{2,1,0:T(8,128)(2,1)} async-done(((bf16[12,72,128]{2,1,0:T(8,128)(2,1)}), bf16[12,72,128]{2,1,0:T(8,128)(2,1)}, u32[]{:S(2)}, u32[]{:S(2)}) %all-to-all-start.3) | async-done | bytes 221216 | tf_op jit(solution)/shard_map/all_to_all | solution.py:408
  113.6 1.1 settle.1
  114.7 3.1 %collective-permute-start.8 = (f32[64,256]{1,0:T(8,128)S(1)}, f32[64,256]{1,0:T(8,128)S(1)}, u32[]{:S(2)}, u32[]{:S(2)}) collective-permute-start(f32[64,256]{1,0:T(8,128)S(1)} %get-tuple-element.28), channel_id=1, source_target_pairs={{0,0},{1,96},{2,192},{3,288},{4,384},{5,480},{6,576},{7,672},{8,1}... | collective-permute-start | bytes 196616 | tf_op jit(solution)/shard_map/ppermute | solution.py:446
  117.8 8.3 %all_to_all.25.gain_ref = f32[8,16,128]{2,1,0:T(8,128)S(1)} all-to-all(f32[8,16,128]{2,1,0:T(8,128)S(1)} %get-tuple-element.29), channel_id=1, replica_groups=mesh['z'=12,'y'=8,'x'=4,'c'=2] {'x','c'}, dimensions={0} | all-to-all | bytes 131072 | tf_op jit(solution)/shard_map/all_to_all | solution.py:447
  126.0 0.8 spread.1
  126.8 6.0 %collective-permute-done.8 = f32[64,256]{1,0:T(8,128)S(1)} collective-permute-done((f32[64,256]{1,0:T(8,128)S(1)}, f32[64,256]{1,0:T(8,128)S(1)}, u32[]{:S(2)}, u32[]{:S(2)}) %collective-permute-start.8) | collective-permute-done | bytes 65568 | tf_op jit(solution)/shard_map/ppermute | solution.py:446
  132.8 0.6 slice.4
  (11 shorter events, 0.1 us)
Async XLA Ops:
  0.6 7.6 %copy-start.1 = (bf16[512,208]{0,1:T(8,128)(2,1)S(1)}, bf16[512,208]{0,1:T(8,128)(2,1)}, u32[]{:S(2)}) copy-start(bf16[512,208]{0,1:T(8,128)(2,1)} %param.14) | copy-start | bytes 638980
  0.6 16.8 %copy-start.3 = (f32[12800]{0:T(1024)S(1)}, f32[12800]{0:T(1024)}, u32[]{:S(2)}) copy-start(f32[12800]{0:T(1024)} %param.12) | copy-start | bytes 153604
  0.7 16.9 %copy-start.4 = (s32[1,8]{1,0:T(1,128)S(1)}, s32[1,8]{1,0:T(1,128)}, u32[]{:S(2)}) copy-start(s32[1,8]{1,0:T(1,128)} %param.10) | copy-start | bytes 100
  3.5 15.7 %all-to-all-start = ((bf16[8,416,128]{2,1,0:T(8,128)(2,1)}), bf16[8,416,128]{2,1,0:T(8,128)(2,1)S(1)}, u32[]{:S(2)}, u32[]{:S(2)}) async-start(bf16[8,416,128]{2,1,0:T(8,128)(2,1)} %cut.1), calls=%async_computation | async-start | bytes 1703936 | tf_op jit(solution)/shard_map/all_to_all | solution.py:348
  8.3 24.4 %copy-start.2 = (f32[3200]{0:T(1024)S(1)}, f32[3200]{0:T(1024)}, u32[]{:S(2)}) copy-start(f32[3200]{0:T(1024)} %param.13) | copy-start | bytes 38404
  8.3 19.2 %collective-permute-start.2 = (bf16[208,512]{1,0:T(8,128)(2,1)S(1)}, bf16[208,512]{1,0:T(8,128)(2,1)S(1)}, u32[]{:S(2)}, u32[]{:S(2)}) collective-permute-start(bf16[208,512]{1,0:T(8,128)(2,1)S(1)} %bitcast.26), channel_id=1, source_target_pairs={{0,4},{2,6},{4,0},{6,2},{1,5},{3,7},{5,1},{7,3},{8,12},{10,14},{12... | collective-permute-start | bytes 638984 | tf_op jit(solution)/shard_map/ppermute | solution.py:307
  10.3 18.6 %collective-permute-start.1 = (bf16[208,512]{1,0:T(8,128)(2,1)S(1)}, bf16[208,512]{1,0:T(8,128)(2,1)S(1)}, u32[]{:S(2)}, u32[]{:S(2)}) collective-permute-start(bf16[208,512]{1,0:T(8,128)(2,1)S(1)} %bitcast.27), channel_id=1, source_target_pairs={{0,6},{2,0},{4,2},{6,4},{1,7},{3,1},{5,3},{7,5},{8,14},{10,8},{12,... | collective-permute-start | bytes 638984 | tf_op jit(solution)/shard_map/ppermute | solution.py:307
  14.9 14.1 %collective-permute-start = (bf16[208,512]{1,0:T(8,128)(2,1)S(1)}, bf16[208,512]{1,0:T(8,128)(2,1)S(1)}, u32[]{:S(2)}, u32[]{:S(2)}) collective-permute-start(bf16[208,512]{1,0:T(8,128)(2,1)S(1)} %bitcast.28), channel_id=1, source_target_pairs={{0,2},{2,4},{4,6},{6,0},{1,3},{3,5},{5,7},{7,1},{8,10},{10,12},{12... | collective-permute-start | bytes 638984 | tf_op jit(solution)/shard_map/ppermute | solution.py:307
  20.8 9.7 %all-to-all-start.1 = ((f32[8,8,128]{2,1,0:T(8,128)}), f32[8,8,128]{2,1,0:T(8,128)S(1)}, u32[]{:S(2)}, u32[]{:S(2)}) async-start(f32[8,8,128]{2,1,0:T(8,128)} %sums.1), calls=%async_computation.1 | async-start | bytes 65536 | tf_op jit(solution)/shard_map/all_to_all | solution.py:375
  30.5 4.5 %collective-permute-start.3 = (bf16[4,208,512]{2,1,0:T(8,128)(2,1)}, bf16[4,208,512]{2,1,0:T(8,128)(2,1)S(1)}, u32[]{:S(2)}, u32[]{:S(2)}) collective-permute-start(bf16[4,208,512]{2,1,0:T(8,128)(2,1)} %pad_maximum_fusion.1), channel_id=1, source_target_pairs={{0,1},{1,0},{2,3},{3,2},{4,5},{5,4},{6,7},{7,6},{8,9},{9,8},{10,11... | collective-permute-start | bytes 2555912 | tf_op jit(solution)/shard_map/ppermute | solution.py:312
  37.8 44.0 %all-to-all-start.2 = ((bf16[8,688,128]{2,1,0:T(8,128)(2,1)}), bf16[8,688,128]{2,1,0:T(8,128)(2,1)}, u32[]{:S(2)}, u32[]{:S(2)}) async-start(bf16[8,688,128]{2,1,0:T(8,128)(2,1)} %terms.1), calls=%async_computation.2 | async-start | bytes 2818048 | tf_op jit(solution)/shard_map/all_to_all | solution.py:399
  45.1 16.1 %collective-permute-start.6 = (bf16[416,512]{1,0:T(8,128)(2,1)S(1)}, bf16[416,512]{1,0:T(8,128)(2,1)S(1)}, u32[]{:S(2)}, u32[]{:S(2)}) collective-permute-start(bf16[416,512]{1,0:T(8,128)(2,1)S(1)} %turn.1.own_ref), channel_id=1, source_target_pairs={{0,4},{2,6},{4,0},{6,2},{1,5},{3,7},{5,1},{7,3},{8,12},{10,14},{12... | collective-permute-start | bytes 1277960 | tf_op jit(solution)/shard_map/ppermute | solution.py:307
  49.4 19.9 %collective-permute-start.5 = (bf16[416,512]{1,0:T(8,128)(2,1)S(1)}, bf16[416,512]{1,0:T(8,128)(2,1)S(1)}, u32[]{:S(2)}, u32[]{:S(2)}) collective-permute-start(bf16[416,512]{1,0:T(8,128)(2,1)S(1)} %turn.1.own_ref), channel_id=1, source_target_pairs={{0,6},{2,0},{4,2},{6,4},{1,7},{3,1},{5,3},{7,5},{8,14},{10,8},{12,... | collective-permute-start | bytes 1277960 | tf_op jit(solution)/shard_map/ppermute | solution.py:307
  51.9 17.4 %collective-permute-start.4 = (bf16[416,512]{1,0:T(8,128)(2,1)S(1)}, bf16[416,512]{1,0:T(8,128)(2,1)S(1)}, u32[]{:S(2)}, u32[]{:S(2)}) collective-permute-start(bf16[416,512]{1,0:T(8,128)(2,1)S(1)} %turn.1.own_ref), channel_id=1, source_target_pairs={{0,2},{2,4},{4,6},{6,0},{1,3},{3,5},{5,7},{7,1},{8,10},{10,12},{12... | collective-permute-start | bytes 1277960 | tf_op jit(solution)/shard_map/ppermute | solution.py:307
  70.7 28.2 %collective-permute-start.7 = (bf16[4,416,512]{2,1,0:T(8,128)(2,1)}, bf16[4,416,512]{2,1,0:T(8,128)(2,1)S(1)}, u32[]{:S(2)}, u32[]{:S(2)}) collective-permute-start(bf16[4,416,512]{2,1,0:T(8,128)(2,1)} %pad_maximum_fusion), channel_id=1, source_target_pairs={{0,1},{1,0},{2,3},{3,2},{4,5},{5,4},{6,7},{7,6},{8,9},{9,8},{10,11... | collective-permute-start | bytes 5111816 | tf_op jit(solution)/shard_map/ppermute | solution.py:312
  84.1 29.4 %all-to-all-start.3 = ((bf16[12,72,128]{2,1,0:T(8,128)(2,1)}), bf16[12,72,128]{2,1,0:T(8,128)(2,1)}, u32[]{:S(2)}, u32[]{:S(2)}) async-start(bf16[12,72,128]{2,1,0:T(8,128)(2,1)} %fold.1), calls=%async_computation.3 | async-start | bytes 442368 | tf_op jit(solution)/shard_map/all_to_all | solution.py:408
  99.0 1.3 copy-start
  114.7 18.2 %collective-permute-start.8 = (f32[64,256]{1,0:T(8,128)S(1)}, f32[64,256]{1,0:T(8,128)S(1)}, u32[]{:S(2)}, u32[]{:S(2)}) collective-permute-start(f32[64,256]{1,0:T(8,128)S(1)} %get-tuple-element.28), channel_id=1, source_target_pairs={{0,0},{1,96},{2,192},{3,288},{4,384},{5,480},{6,576},{7,672},{8,1}... | collective-permute-start | bytes 196616 | tf_op jit(solution)/shard_map/ppermute | solution.py:446

commit v10 on v9

--- a/solution.py
+++ b/solution.py
@@ -19,7 +19,6 @@
 REST = 384
 TILES, PR, SUB, VT = 8, 16, 4, 64
 VMEM = pltpu.CompilerParams(vmem_limit_bytes=48 * 1024 * 1024)
-ROOMY = pltpu.CompilerParams(vmem_limit_bytes=56 * 1024 * 1024)
 F32, BF16 = jnp.float32, jnp.bfloat16
 
 
@@ -258,10 +257,7 @@
         if low > start:
             pieces = pltpu.roll(pieces, low - start, 1)
         wide_ref[:, start : start + 640] += pieces
-    for sub in range(SUB):
-        for tile in range(VW // 128):
-            row = sub * (VW // 128) + tile
-            out_ref[row : row + 1, :] = wide_ref[sub : sub + 1, tile * 128 : tile * 128 + 128]
+    out_ref[...] = wide_ref[:, 0:VW]
 
 
 def gathered_kernel(
@@ -402,7 +398,7 @@
         out_shape=jax.ShapeDtypeStruct((NZ, THIRD, 128), BF16),
         in_specs=whole(1),
         out_specs=whole(1)[0],
-        compiler_params=ROOMY,
+        compiler_params=VMEM,
         name="fold",
     )(terms)
     terms = lax.all_to_all(terms, "z", 0, 0)
@@ -447,7 +443,7 @@
     gains = lax.all_to_all(gains, MP, 0, 0)
     gain_grad = pl.pallas_call(
         spread_kernel,
-        out_shape=jax.ShapeDtypeStruct((PW // 128, 128), F32),
+        out_shape=jax.ShapeDtypeStruct((SUB, VW), F32),
         in_specs=whole(1),
         out_specs=whole(1)[0],
         scratch_shapes=[pltpu.VMEM((SUB, 3456), F32)],

time: 134 us -> 132 us (0.985)
  local copies, waits for them, and re-layouts: 1.99 us -> 7.06 us
  waiting for transfers between devices: 44.1 us -> 40.1 us
  Pallas kernels: 15.6 us -> 12 us
    all_to_all x1, waiting for transfers between devices: 10.5 us -> 6.69 us  [body(): terms = lax.all_to_all(terms, 'z', 0, 0)]
    unnamed x10 -> x24, local copies, waits for them, and re-layouts: 1.33 us -> 5.04 us
    pallas_call x1, Pallas kernels: 2.41 us -> 0.37 us  [body(): pl.pallas_call(fold_kernel, out_shape=jax.ShapeDtypeStruct((NZ, THIRD, 12...]
  transfers between devices with their start and end apart: 13 -> 13, of which waited for: 9 -> 9; matrix products, arithmetic and copies ran while one was open for 2% -> 3% of each run, Pallas kernels for 7% -> 5%
where the time goes in v10:
time: 132 us; the launch traced here: 131 us
  starting transfers between devices  59.2 us (45%)
  waiting for transfers between devices  40.1 us (30%)
  Pallas kernels  12 us (9%)
  blocking collectives  8.09 us (6%)
  local copies, waits for them, and re-layouts  7.06 us (5%)
  other arithmetic  2.96 us (2%)
  between operations  1.52 us (1%)
    ppermute x6, starting transfers between devices, gather_x(): lax.ppermute(own, 'x', [(x, (x + step) % 4) for x in range(4)])  18.7 us
    ppermute x6, waiting for transfers between devices, gather_x(): lax.ppermute(own, 'x', [(x, (x + step) % 4) for x in range(4)])  15.5 us
    all_to_all x1, starting transfers between devices, body(): terms = lax.all_to_all(terms, 'z', 0, 0)  14.7 us
    all_to_all x1, waiting for transfers between devices, body(): terms = lax.all_to_all(terms, 'y', 0, 0)  8.95 us
    all_to_all x1, blocking collectives, body(): gains = lax.all_to_all(gains, MP, 0, 0)  8.09 us
    all_to_all x1, starting transfers between devices, body(): terms = lax.all_to_all(terms, 'y', 0, 0)  7.1 us
    all_to_all x1, starting transfers between devices, body(): sums = lax.all_to_all(sums, MP, 0, 0)  6.73 us
    all_to_all x1, waiting for transfers between devices, body(): terms = lax.all_to_all(terms, 'z', 0, 0)  6.69 us
  transfers between devices with their start and end apart: 13, of which 9 were waited for; matrix products, arithmetic and copies ran while one was open for 3% of the time, Pallas kernels for 5%

profile of v10, /device:TPU:68, one launch (start us, length us, event | category | flops | bytes accessed | tf_op | source)
XLA Modules:
  0.0 130.9 jit_solution(454398797981086222)
XLA Ops:
  0.7 2.8 %cut.1 = bf16[8,416,128]{2,1,0:T(8,128)(2,1)} custom-call(bf16[16,12800]{1,0:T(8,128)(2,1)} %grad_hbm.1, bf16[16,12800]{1,0:T(8,128)(2,1)} %feat_hbm.1), custom_call_target="tpu_custom_call" | custom-call | tf_op jit(solution)/shard_map/cut/pallas_call | solution.py:329
  3.5 4.8 %all-to-all-start = ((bf16[8,416,128]{2,1,0:T(8,128)(2,1)}), bf16[8,416,128]{2,1,0:T(8,128)(2,1)S(1)}, u32[]{:S(2)}, u32[]{:S(2)}) async-start(bf16[8,416,128]{2,1,0:T(8,128)(2,1)} %cut.1), calls=%async_computation | async-start | bytes 1703936 | tf_op jit(solution)/shard_map/all_to_all | solution.py:344
  8.3 2.0 %collective-permute-start.2 = (bf16[208,512]{1,0:T(8,128)(2,1)S(1)}, bf16[208,512]{1,0:T(8,128)(2,1)S(1)}, u32[]{:S(2)}, u32[]{:S(2)}) collective-permute-start(bf16[208,512]{1,0:T(8,128)(2,1)S(1)} %bitcast.25), channel_id=1, source_target_pairs={{0,4},{2,6},{4,0},{6,2},{1,5},{3,7},{5,1},{7,3},{8,12},{10,14},{12... | collective-permute-start | bytes 638984 | tf_op jit(solution)/shard_map/ppermute | solution.py:303
  10.4 4.5 %collective-permute-start.1 = (bf16[208,512]{1,0:T(8,128)(2,1)S(1)}, bf16[208,512]{1,0:T(8,128)(2,1)S(1)}, u32[]{:S(2)}, u32[]{:S(2)}) collective-permute-start(bf16[208,512]{1,0:T(8,128)(2,1)S(1)} %bitcast.26), channel_id=1, source_target_pairs={{0,6},{2,0},{4,2},{6,4},{1,7},{3,1},{5,3},{7,5},{8,14},{10,8},{12,... | collective-permute-start | bytes 638984 | tf_op jit(solution)/shard_map/ppermute | solution.py:303
  14.9 1.9 %collective-permute-start = (bf16[208,512]{1,0:T(8,128)(2,1)S(1)}, bf16[208,512]{1,0:T(8,128)(2,1)S(1)}, u32[]{:S(2)}, u32[]{:S(2)}) collective-permute-start(bf16[208,512]{1,0:T(8,128)(2,1)S(1)} %bitcast.27), channel_id=1, source_target_pairs={{0,2},{2,4},{4,6},{6,0},{1,3},{3,5},{5,7},{7,1},{8,10},{10,12},{12... | collective-permute-start | bytes 638984 | tf_op jit(solution)/shard_map/ppermute | solution.py:303
  17.5 0.1 select_reduce_fusion.source_ref
  17.6 0.1 fusion.gain_ref
  17.7 1.5 %all-to-all-done.recv_ref = bf16[8,416,128]{2,1,0:T(8,128)(2,1)S(1)} async-done(((bf16[8,416,128]{2,1,0:T(8,128)(2,1)}), bf16[8,416,128]{2,1,0:T(8,128)(2,1)S(1)}, u32[]{:S(2)}, u32[]{:S(2)}) %all-to-all-start) | async-done | bytes 852000 | tf_op jit(solution)/shard_map/all_to_all | solution.py:344
  19.2 1.6 %sums.1 = f32[8,8,128]{2,1,0:T(8,128)} custom-call(s32[8]{0:T(128)S(1)} %select_reduce_fusion.source_ref, s32[8]{0:T(128)S(1)} %compare_convert_fusion.live_ref, bf16[8,416,128]{2,1,0:T(8,128)(2,1)S(1)} %all-to-all-done.recv_ref, f32[4,512]{1,0:T(4,128)S(1)} %fusion.gain_ref), custom_call_target="tpu_custom_call" | custom-call | tf_op jit(solution)/shard_map/sums/pallas_call | solution.py:363
  20.8 6.7 %all-to-all-start.1 = ((f32[8,8,128]{2,1,0:T(8,128)}), f32[8,8,128]{2,1,0:T(8,128)S(1)}, u32[]{:S(2)}, u32[]{:S(2)}) async-start(f32[8,8,128]{2,1,0:T(8,128)} %sums.1), calls=%async_computation.1 | async-start | bytes 65536 | tf_op jit(solution)/shard_map/all_to_all | solution.py:371
  27.5 1.4 %collective-permute-done.1.after_ref = bf16[208,512]{1,0:T(8,128)(2,1)S(1)} collective-permute-done((bf16[208,512]{1,0:T(8,128)(2,1)S(1)}, bf16[208,512]{1,0:T(8,128)(2,1)S(1)}, u32[]{:S(2)}, u32[]{:S(2)}) %collective-permute-start.1) | collective-permute-done | bytes 213024 | tf_op jit(solution)/shard_map/ppermute | solution.py:303
  29.0 1.0 pad_maximum_fusion.1
  30.0 0.5 all-to-all-done.1.sums_ref
  30.6 1.9 %collective-permute-start.3 = (bf16[4,208,512]{2,1,0:T(8,128)(2,1)}, bf16[4,208,512]{2,1,0:T(8,128)(2,1)S(1)}, u32[]{:S(2)}, u32[]{:S(2)}) collective-permute-start(bf16[4,208,512]{2,1,0:T(8,128)(2,1)} %pad_maximum_fusion.1), channel_id=1, source_target_pairs={{0,1},{1,0},{2,3},{3,2},{4,5},{5,4},{6,7},{7,6},{8,9},{9,8},{10,11... | collective-permute-start | bytes 2555912 | tf_op jit(solution)/shard_map/ppermute | solution.py:308
  32.5 0.1 broadcast_add_fusion
  32.6 0.1 pad_add_fusion.parts_ref
  32.7 0.1 fusion.1
  32.7 1.3 branch.1
  34.1 1.0 collective-permute-done.3.other_ref
  35.0 2.8 %terms.1 = bf16[8,688,128]{2,1,0:T(8,128)(2,1)} custom-call(s32[8]{0:T(128)S(1)} %pad_add_fusion.parts_ref, bf16[512,512]{1,0:T(8,128)(2,1)S(1)} %get-tuple-element.20.branch_ref, bf16[16,128]{1,0:T(8,128)(2,1)S(1)} %get-tuple-element.21.gain_ref, bf16[208,512]{1,0:T(8,128)(2,1)S(1)} %bitcast.29, bf16[208,512]{1,0:T(8,128)(2,1)S(1)} %collective-permute-done.before_ref, ...), custom_call_target="tpu_custom_call" | custom-call | tf_op jit(solution)/shard_map/terms/pallas_call | solution.py:386
  37.8 7.1 %all-to-all-start.2 = ((bf16[8,688,128]{2,1,0:T(8,128)(2,1)}), bf16[8,688,128]{2,1,0:T(8,128)(2,1)S(1)}, u32[]{:S(2)}, u32[]{:S(2)}) async-start(bf16[8,688,128]{2,1,0:T(8,128)(2,1)} %terms.1), calls=%async_computation.2 | async-start | bytes 2818048 | tf_op jit(solution)/shard_map/all_to_all | solution.py:395
  44.9 0.2 turn.1.own_ref
  45.1 4.3 %collective-permute-start.6 = (bf16[416,512]{1,0:T(8,128)(2,1)S(1)}, bf16[416,512]{1,0:T(8,128)(2,1)S(1)}, u32[]{:S(2)}, u32[]{:S(2)}) collective-permute-start(bf16[416,512]{1,0:T(8,128)(2,1)S(1)} %turn.1.own_ref), channel_id=1, source_target_pairs={{0,4},{2,6},{4,0},{6,2},{1,5},{3,7},{5,1},{7,3},{8,12},{10,14},{12... | collective-permute-start | bytes 1277960 | tf_op jit(solution)/shard_map/ppermute | solution.py:303
  49.4 2.5 %collective-permute-start.5 = (bf16[416,512]{1,0:T(8,128)(2,1)S(1)}, bf16[416,512]{1,0:T(8,128)(2,1)S(1)}, u32[]{:S(2)}, u32[]{:S(2)}) collective-permute-start(bf16[416,512]{1,0:T(8,128)(2,1)S(1)} %turn.1.own_ref), channel_id=1, source_target_pairs={{0,6},{2,0},{4,2},{6,4},{1,7},{3,1},{5,3},{7,5},{8,14},{10,8},{12,... | collective-permute-start | bytes 1277960 | tf_op jit(solution)/shard_map/ppermute | solution.py:303
  51.9 3.4 %collective-permute-start.4 = (bf16[416,512]{1,0:T(8,128)(2,1)S(1)}, bf16[416,512]{1,0:T(8,128)(2,1)S(1)}, u32[]{:S(2)}, u32[]{:S(2)}) collective-permute-start(bf16[416,512]{1,0:T(8,128)(2,1)S(1)} %turn.1.own_ref), channel_id=1, source_target_pairs={{0,2},{2,4},{4,6},{6,0},{1,3},{3,5},{5,7},{7,1},{8,10},{10,12},{12... | collective-permute-start | bytes 1277960 | tf_op jit(solution)/shard_map/ppermute | solution.py:303
  55.3 5.9 %collective-permute-done.6.far_ref = bf16[416,512]{1,0:T(8,128)(2,1)S(1)} collective-permute-done((bf16[416,512]{1,0:T(8,128)(2,1)S(1)}, bf16[416,512]{1,0:T(8,128)(2,1)S(1)}, u32[]{:S(2)}, u32[]{:S(2)}) %collective-permute-start.6) | collective-permute-done | bytes 426016 | tf_op jit(solution)/shard_map/ppermute | solution.py:303
  61.2 8.1 %collective-permute-done.5.after_ref = bf16[416,512]{1,0:T(8,128)(2,1)S(1)} collective-permute-done((bf16[416,512]{1,0:T(8,128)(2,1)S(1)}, bf16[416,512]{1,0:T(8,128)(2,1)S(1)}, u32[]{:S(2)}, u32[]{:S(2)}) %collective-permute-start.5) | collective-permute-done | bytes 426016 | tf_op jit(solution)/shard_map/ppermute | solution.py:303
  69.3 0.0 collective-permute-done.4.before_ref
  69.3 1.5 %pad_maximum_fusion = bf16[4,416,512]{2,1,0:T(8,128)(2,1)} fusion(bf16[1,416,512]{2,1,0:T(8,128)(2,1)S(1)} %bitcast.21, bf16[1,416,512]{2,1,0:T(8,128)(2,1)S(1)} %bitcast.22, bf16[1,416,512]{2,1,0:T(8,128)(2,1)S(1)} %bitcast.23, bf16[1,416,512]{2,1,0:T(8,128)(2,1)S(1)} %bitcast.20), kind=kLoop, calls=%fused_computation | loop fusion | flops 2555904 | bytes 3407872 | tf_op jit(solution)/shard_map/stack | solution.py:415
  70.8 1.9 %collective-permute-start.7 = (bf16[4,416,512]{2,1,0:T(8,128)(2,1)}, bf16[4,416,512]{2,1,0:T(8,128)(2,1)S(1)}, u32[]{:S(2)}, u32[]{:S(2)}) collective-permute-start(bf16[4,416,512]{2,1,0:T(8,128)(2,1)} %pad_maximum_fusion), channel_id=1, source_target_pairs={{0,1},{1,0},{2,3},{3,2},{4,5},{5,4},{6,7},{7,6},{8,9},{9,8},{10,11... | collective-permute-start | bytes 5111816 | tf_op jit(solution)/shard_map/ppermute | solution.py:308
  72.7 9.0 %all-to-all-done.2.recv_ref = bf16[8,688,128]{2,1,0:T(8,128)(2,1)S(1)} async-done(((bf16[8,688,128]{2,1,0:T(8,128)(2,1)}), bf16[8,688,128]{2,1,0:T(8,128)(2,1)S(1)}, u32[]{:S(2)}, u32[]{:S(2)}) %all-to-all-start.2) | async-done | bytes 1409056 | tf_op jit(solution)/shard_map/all_to_all | solution.py:395
  81.7 0.4 fold.1
  82.1 0.7 copy-done.7
  82.7 14.7 %all-to-all-start.3 = ((bf16[12,72,128]{2,1,0:T(8,128)(2,1)}), bf16[12,72,128]{2,1,0:T(8,128)(2,1)S(1)}, u32[]{:S(2)}, u32[]{:S(2)}) async-start(bf16[12,72,128]{2,1,0:T(8,128)(2,1)} %copy-done.7), calls=%async_computation.3 | async-start | bytes 442368 | tf_op jit(solution)/shard_map/all_to_all | solution.py:404
  97.5 0.7 broadcast_in_dim.44.scale_ref
  98.2 1.0 copy-done.1
  99.2 1.0 copy-done.3
  100.2 1.0 copy-done.5
  101.2 1.3 %copy-done.6 = bf16[3200,208]{0,1:T(8,128)(2,1)S(1)} copy-done((bf16[3200,208]{0,1:T(8,128)(2,1)S(1)}, bf16[3200,208]{0,1:T(8,128)(2,1)}, u32[]{:S(2)}) %copy-start.6) | copy-done | bytes 1331224
  102.6 2.7 %gathered.1 = (bf16[208,512]{1,0:T(8,128)(2,1)}, bf16[64,3200]{1,0:T(8,128)(2,1)}) custom-call(s32[1]{0:T(128)} %bitcast.12.tile_ref, s32[8]{0:T(128)S(1)} %pad_add_fusion.parts_ref, bf16[208,3200]{1,0:T(8,128)(2,1)S(1)} %bitcast.24, f32[1,3200]{1,0:T(1,128)S(1)} %broadcast_in_dim.44.scale_ref, bf16[416,512]{1,0:T(8,128)(2,1)S(1)} %turn.1.own_ref, ...), custom_call_target="tpu_custom_call" | custom-call | tf_op jit(solution)/shard_map/gathered/pallas_call | solution.py:416
  105.3 6.7 %all-to-all-done.3.recv_ref = bf16[12,72,128]{2,1,0:T(8,128)(2,1)S(1)} async-done(((bf16[12,72,128]{2,1,0:T(8,128)(2,1)}), bf16[12,72,128]{2,1,0:T(8,128)(2,1)S(1)}, u32[]{:S(2)}, u32[]{:S(2)}) %all-to-all-start.3) | async-done | bytes 221216 | tf_op jit(solution)/shard_map/all_to_all | solution.py:404
  112.0 0.2 settle.1
  112.1 3.3 %collective-permute-start.8 = (f32[64,256]{1,0:T(8,128)S(1)}, f32[64,256]{1,0:T(8,128)S(1)}, u32[]{:S(2)}, u32[]{:S(2)}) collective-permute-start(f32[64,256]{1,0:T(8,128)S(1)} %get-tuple-element.28), channel_id=1, source_target_pairs={{0,0},{1,96},{2,192},{3,288},{4,384},{5,480},{6,576},{7,672},{8,1}... | collective-permute-start | bytes 196616 | tf_op jit(solution)/shard_map/ppermute | solution.py:442
  115.5 8.1 %all_to_all.25.gain_ref = f32[8,16,128]{2,1,0:T(8,128)S(1)} all-to-all(f32[8,16,128]{2,1,0:T(8,128)S(1)} %get-tuple-element.29), channel_id=1, replica_groups=mesh['z'=12,'y'=8,'x'=4,'c'=2] {'x','c'}, dimensions={0} | all-to-all | bytes 131072 | tf_op jit(solution)/shard_map/all_to_all | solution.py:443
  123.6 0.1 spread.1
  123.7 0.6 reshape.21
  124.3 6.0 %collective-permute-done.8 = f32[64,256]{1,0:T(8,128)S(1)} collective-permute-done((f32[64,256]{1,0:T(8,128)S(1)}, f32[64,256]{1,0:T(8,128)S(1)}, u32[]{:S(2)}, u32[]{:S(2)}) %collective-permute-start.8) | collective-permute-done | bytes 65568 | tf_op jit(solution)/shard_map/ppermute | solution.py:442
  130.3 0.6 slice.4
  (26 shorter events, 0.1 us)
Async XLA Ops:
  0.6 7.7 %copy-start.8 = (bf16[512,208]{0,1:T(8,128)(2,1)S(1)}, bf16[512,208]{0,1:T(8,128)(2,1)}, u32[]{:S(2)}) copy-start(bf16[512,208]{0,1:T(8,128)(2,1)} %param.14) | copy-start | bytes 638980
  0.6 16.8 %copy-start.10 = (f32[12800]{0:T(1024)S(1)}, f32[12800]{0:T(1024)}, u32[]{:S(2)}) copy-start(f32[12800]{0:T(1024)} %param.12) | copy-start | bytes 153604
  0.7 16.9 %copy-start.11 = (s32[1,8]{1,0:T(1,128)S(1)}, s32[1,8]{1,0:T(1,128)}, u32[]{:S(2)}) copy-start(s32[1,8]{1,0:T(1,128)} %param.10) | copy-start | bytes 100
  3.5 15.7 %all-to-all-start = ((bf16[8,416,128]{2,1,0:T(8,128)(2,1)}), bf16[8,416,128]{2,1,0:T(8,128)(2,1)S(1)}, u32[]{:S(2)}, u32[]{:S(2)}) async-start(bf16[8,416,128]{2,1,0:T(8,128)(2,1)} %cut.1), calls=%async_computation | async-start | bytes 1703936 | tf_op jit(solution)/shard_map/all_to_all | solution.py:344
  8.3 24.4 %copy-start.9 = (f32[3200]{0:T(1024)S(1)}, f32[3200]{0:T(1024)}, u32[]{:S(2)}) copy-start(f32[3200]{0:T(1024)} %param.13) | copy-start | bytes 38404
  8.3 19.2 %collective-permute-start.2 = (bf16[208,512]{1,0:T(8,128)(2,1)S(1)}, bf16[208,512]{1,0:T(8,128)(2,1)S(1)}, u32[]{:S(2)}, u32[]{:S(2)}) collective-permute-start(bf16[208,512]{1,0:T(8,128)(2,1)S(1)} %bitcast.25), channel_id=1, source_target_pairs={{0,4},{2,6},{4,0},{6,2},{1,5},{3,7},{5,1},{7,3},{8,12},{10,14},{12... | collective-permute-start | bytes 638984 | tf_op jit(solution)/shard_map/ppermute | solution.py:303
  10.4 18.6 %collective-permute-start.1 = (bf16[208,512]{1,0:T(8,128)(2,1)S(1)}, bf16[208,512]{1,0:T(8,128)(2,1)S(1)}, u32[]{:S(2)}, u32[]{:S(2)}) collective-permute-start(bf16[208,512]{1,0:T(8,128)(2,1)S(1)} %bitcast.26), channel_id=1, source_target_pairs={{0,6},{2,0},{4,2},{6,4},{1,7},{3,1},{5,3},{7,5},{8,14},{10,8},{12,... | collective-permute-start | bytes 638984 | tf_op jit(solution)/shard_map/ppermute | solution.py:303
  14.9 14.1 %collective-permute-start = (bf16[208,512]{1,0:T(8,128)(2,1)S(1)}, bf16[208,512]{1,0:T(8,128)(2,1)S(1)}, u32[]{:S(2)}, u32[]{:S(2)}) collective-permute-start(bf16[208,512]{1,0:T(8,128)(2,1)S(1)} %bitcast.27), channel_id=1, source_target_pairs={{0,2},{2,4},{4,6},{6,0},{1,3},{3,5},{5,7},{7,1},{8,10},{10,12},{12... | collective-permute-start | bytes 638984 | tf_op jit(solution)/shard_map/ppermute | solution.py:303
  20.8 9.7 %all-to-all-start.1 = ((f32[8,8,128]{2,1,0:T(8,128)}), f32[8,8,128]{2,1,0:T(8,128)S(1)}, u32[]{:S(2)}, u32[]{:S(2)}) async-start(f32[8,8,128]{2,1,0:T(8,128)} %sums.1), calls=%async_computation.1 | async-start | bytes 65536 | tf_op jit(solution)/shard_map/all_to_all | solution.py:371
  30.6 4.5 %collective-permute-start.3 = (bf16[4,208,512]{2,1,0:T(8,128)(2,1)}, bf16[4,208,512]{2,1,0:T(8,128)(2,1)S(1)}, u32[]{:S(2)}, u32[]{:S(2)}) collective-permute-start(bf16[4,208,512]{2,1,0:T(8,128)(2,1)} %pad_maximum_fusion.1), channel_id=1, source_target_pairs={{0,1},{1,0},{2,3},{3,2},{4,5},{5,4},{6,7},{7,6},{8,9},{9,8},{10,11... | collective-permute-start | bytes 2555912 | tf_op jit(solution)/shard_map/ppermute | solution.py:308
  37.8 43.9 %all-to-all-start.2 = ((bf16[8,688,128]{2,1,0:T(8,128)(2,1)}), bf16[8,688,128]{2,1,0:T(8,128)(2,1)S(1)}, u32[]{:S(2)}, u32[]{:S(2)}) async-start(bf16[8,688,128]{2,1,0:T(8,128)(2,1)} %terms.1), calls=%async_computation.2 | async-start | bytes 2818048 | tf_op jit(solution)/shard_map/all_to_all | solution.py:395
  45.1 16.1 %collective-permute-start.6 = (bf16[416,512]{1,0:T(8,128)(2,1)S(1)}, bf16[416,512]{1,0:T(8,128)(2,1)S(1)}, u32[]{:S(2)}, u32[]{:S(2)}) collective-permute-start(bf16[416,512]{1,0:T(8,128)(2,1)S(1)} %turn.1.own_ref), channel_id=1, source_target_pairs={{0,4},{2,6},{4,0},{6,2},{1,5},{3,7},{5,1},{7,3},{8,12},{10,14},{12... | collective-permute-start | bytes 1277960 | tf_op jit(solution)/shard_map/ppermute | solution.py:303
  49.4 19.9 %collective-permute-start.5 = (bf16[416,512]{1,0:T(8,128)(2,1)S(1)}, bf16[416,512]{1,0:T(8,128)(2,1)S(1)}, u32[]{:S(2)}, u32[]{:S(2)}) collective-permute-start(bf16[416,512]{1,0:T(8,128)(2,1)S(1)} %turn.1.own_ref), channel_id=1, source_target_pairs={{0,6},{2,0},{4,2},{6,4},{1,7},{3,1},{5,3},{7,5},{8,14},{10,8},{12,... | collective-permute-start | bytes 1277960 | tf_op jit(solution)/shard_map/ppermute | solution.py:303
  51.9 17.4 %collective-permute-start.4 = (bf16[416,512]{1,0:T(8,128)(2,1)S(1)}, bf16[416,512]{1,0:T(8,128)(2,1)S(1)}, u32[]{:S(2)}, u32[]{:S(2)}) collective-permute-start(bf16[416,512]{1,0:T(8,128)(2,1)S(1)} %turn.1.own_ref), channel_id=1, source_target_pairs={{0,2},{2,4},{4,6},{6,0},{1,3},{3,5},{5,7},{7,1},{8,10},{10,12},{12... | collective-permute-start | bytes 1277960 | tf_op jit(solution)/shard_map/ppermute | solution.py:303
  61.2 9.6 %copy-start = (bf16[416,512]{1,0:T(8,128)(2,1)}, bf16[416,512]{1,0:T(8,128)(2,1)S(1)}, u32[]{:S(2)}) copy-start(bf16[416,512]{1,0:T(8,128)(2,1)S(1)} %collective-permute-done.6.far_ref) | copy-start | bytes 1277956
  69.3 1.5 %copy-start.2 = (bf16[416,512]{1,0:T(8,128)(2,1)}, bf16[416,512]{1,0:T(8,128)(2,1)S(1)}, u32[]{:S(2)}) copy-start(bf16[416,512]{1,0:T(8,128)(2,1)S(1)} %collective-permute-done.5.after_ref) | copy-start | bytes 1277956
  69.3 1.5 %copy-start.4 = (bf16[416,512]{1,0:T(8,128)(2,1)}, bf16[416,512]{1,0:T(8,128)(2,1)S(1)}, u32[]{:S(2)}) copy-start(bf16[416,512]{1,0:T(8,128)(2,1)S(1)} %collective-permute-done.4.before_ref) | copy-start | bytes 1277956
  70.8 27.4 %collective-permute-start.7 = (bf16[4,416,512]{2,1,0:T(8,128)(2,1)}, bf16[4,416,512]{2,1,0:T(8,128)(2,1)S(1)}, u32[]{:S(2)}, u32[]{:S(2)}) collective-permute-start(bf16[4,416,512]{2,1,0:T(8,128)(2,1)} %pad_maximum_fusion), channel_id=1, source_target_pairs={{0,1},{1,0},{2,3},{3,2},{4,5},{5,4},{6,7},{7,6},{8,9},{9,8},{10,11... | collective-permute-start | bytes 5111816 | tf_op jit(solution)/shard_map/ppermute | solution.py:308
  82.1 0.7 copy-start.7
  82.7 29.2 %all-to-all-start.3 = ((bf16[12,72,128]{2,1,0:T(8,128)(2,1)}), bf16[12,72,128]{2,1,0:T(8,128)(2,1)S(1)}, u32[]{:S(2)}, u32[]{:S(2)}) async-start(bf16[12,72,128]{2,1,0:T(8,128)(2,1)} %copy-done.7), calls=%async_computation.3 | async-start | bytes 442368 | tf_op jit(solution)/shard_map/all_to_all | solution.py:404
  98.2 1.0 copy-start.1
  99.2 1.0 copy-start.3
  100.2 1.0 copy-start.5
  101.2 1.3 %copy-start.6 = (bf16[3200,208]{0,1:T(8,128)(2,1)S(1)}, bf16[3200,208]{0,1:T(8,128)(2,1)}, u32[]{:S(2)}) copy-start(bf16[3200,208]{0,1:T(8,128)(2,1)} %param.15) | copy-start | bytes 3993604
  112.1 18.2 %collective-permute-start.8 = (f32[64,256]{1,0:T(8,128)S(1)}, f32[64,256]{1,0:T(8,128)S(1)}, u32[]{:S(2)}, u32[]{:S(2)}) collective-permute-start(f32[64,256]{1,0:T(8,128)S(1)} %get-tuple-element.28), channel_id=1, source_target_pairs={{0,0},{1,96},{2,192},{3,288},{4,384},{5,480},{6,576},{7,672},{8,1}... | collective-permute-start | bytes 196616 | tf_op jit(solution)/shard_map/ppermute | solution.py:442

commit v11 on v9

--- a/solution.py
+++ b/solution.py
@@ -19,7 +19,6 @@
 REST = 384
 TILES, PR, SUB, VT = 8, 16, 4, 64
 VMEM = pltpu.CompilerParams(vmem_limit_bytes=48 * 1024 * 1024)
-ROOMY = pltpu.CompilerParams(vmem_limit_bytes=56 * 1024 * 1024)
 F32, BF16 = jnp.float32, jnp.bfloat16
 
 
@@ -247,7 +246,8 @@
         gain_ref[part] = gain
 
 
-def spread_kernel(gain_ref, out_ref, wide_ref):
+def spread_kernel(gain_ref, part_ref, out_ref, block_ref, wide_ref):
+    block_ref[...] = part_ref[0:BLOCK, 0 : block_ref.shape[1]]
     wide_ref[...] = jnp.zeros_like(wide_ref)
     for part in range(NMP):
         gain = gain_ref[part]
@@ -402,7 +402,7 @@
         out_shape=jax.ShapeDtypeStruct((NZ, THIRD, 128), BF16),
         in_specs=whole(1),
         out_specs=whole(1)[0],
-        compiler_params=ROOMY,
+        compiler_params=VMEM,
         name="fold",
     )(terms)
     terms = lax.all_to_all(terms, "z", 0, 0)
@@ -443,17 +443,20 @@
         name="settle",
     )(terms)
 
-    proj_grad = lax.ppermute(part, DP + MP, last_places())[:BLOCK, :cols]
+    part = lax.ppermute(part, DP + MP, last_places())
     gains = lax.all_to_all(gains, MP, 0, 0)
-    gain_grad = pl.pallas_call(
+    gain_grad, proj_grad = pl.pallas_call(
         spread_kernel,
-        out_shape=jax.ShapeDtypeStruct((PW // 128, 128), F32),
-        in_specs=whole(1),
-        out_specs=whole(1)[0],
+        out_shape=(
+            jax.ShapeDtypeStruct((PW // 128, 128), F32),
+            jax.ShapeDtypeStruct((BLOCK, cols), F32),
+        ),
+        in_specs=whole(2),
+        out_specs=tuple(whole(2)),
         scratch_shapes=[pltpu.VMEM((SUB, 3456), F32)],
         compiler_params=VMEM,
         name="spread",
-    )(gains)
+    )(gains, part)
     return (residual_grad, attn_grad.T, proj_grad, gain_grad.reshape(-1))
 
 

time: 134 us -> 132 us (0.985)
  local copies, waits for them, and re-layouts: 1.99 us -> 5.79 us
  waiting for transfers between devices: 44.1 us -> 40.9 us
  Pallas kernels: 15.6 us -> 12.7 us
    all_to_all x1, waiting for transfers between devices: 10.5 us -> 6.69 us  [body(): terms = lax.all_to_all(terms, 'z', 0, 0)]
    unnamed x10 -> x24, local copies, waits for them, and re-layouts: 1.33 us -> 5.04 us
    pallas_call x1, Pallas kernels: 2.41 us -> 0.37 us  [body(): pl.pallas_call(fold_kernel, out_shape=jax.ShapeDtypeStruct((NZ, THIRD, 12...]
  transfers between devices with their start and end apart: 13 -> 13, of which waited for: 9 -> 9; matrix products, arithmetic and copies ran while one was open for 2% -> 3% of each run, Pallas kernels for 7% -> 5%
where the time goes in v11:
time: 132 us; the launch traced here: 131 us
  starting transfers between devices  59.2 us (45%)
  waiting for transfers between devices  40.9 us (31%)
  Pallas kernels  12.7 us (10%)
  blocking collectives  8.08 us (6%)
  local copies, waits for them, and re-layouts  5.79 us (4%)
  other arithmetic  2.95 us (2%)
  between operations  1.52 us (1%)
    ppermute x6, starting transfers between devices, gather_x(): lax.ppermute(own, 'x', [(x, (x + step) % 4) for x in range(4)])  18.7 us
    ppermute x6, waiting for transfers between devices, gather_x(): lax.ppermute(own, 'x', [(x, (x + step) % 4) for x in range(4)])  15.4 us
    all_to_all x1, starting transfers between devices, body(): terms = lax.all_to_all(terms, 'z', 0, 0)  14.8 us
    all_to_all x1, waiting for transfers between devices, body(): terms = lax.all_to_all(terms, 'y', 0, 0)  8.97 us
    all_to_all x1, blocking collectives, body(): gains = lax.all_to_all(gains, MP, 0, 0)  8.08 us
    all_to_all x1, starting transfers between devices, body(): terms = lax.all_to_all(terms, 'y', 0, 0)  7.09 us
    ppermute x1, waiting for transfers between devices, body(): part = lax.ppermute(part, DP + MP, last_places())  6.79 us
    all_to_all x1, starting transfers between devices, body(): sums = lax.all_to_all(sums, MP, 0, 0)  6.73 us
  transfers between devices with their start and end apart: 13, of which 9 were waited for; matrix products, arithmetic and copies ran while one was open for 3% of the time, Pallas kernels for 5%

profile of v11, /device:TPU:68, one launch (start us, length us, event | category | flops | bytes accessed | tf_op | source)
XLA Modules:
  0.0 131.1 jit_solution(6920021237721851225)
XLA Ops:
  0.7 2.8 %cut.1 = bf16[8,416,128]{2,1,0:T(8,128)(2,1)} custom-call(bf16[16,12800]{1,0:T(8,128)(2,1)} %grad_hbm.1, bf16[16,12800]{1,0:T(8,128)(2,1)} %feat_hbm.1), custom_call_target="tpu_custom_call" | custom-call | tf_op jit(solution)/shard_map/cut/pallas_call | solution.py:333
  3.5 4.8 %all-to-all-start = ((bf16[8,416,128]{2,1,0:T(8,128)(2,1)}), bf16[8,416,128]{2,1,0:T(8,128)(2,1)S(1)}, u32[]{:S(2)}, u32[]{:S(2)}) async-start(bf16[8,416,128]{2,1,0:T(8,128)(2,1)} %cut.1), calls=%async_computation | async-start | bytes 1703936 | tf_op jit(solution)/shard_map/all_to_all | solution.py:348
  8.3 2.0 %collective-permute-start.2 = (bf16[208,512]{1,0:T(8,128)(2,1)S(1)}, bf16[208,512]{1,0:T(8,128)(2,1)S(1)}, u32[]{:S(2)}, u32[]{:S(2)}) collective-permute-start(bf16[208,512]{1,0:T(8,128)(2,1)S(1)} %bitcast.26), channel_id=1, source_target_pairs={{0,4},{2,6},{4,0},{6,2},{1,5},{3,7},{5,1},{7,3},{8,12},{10,14},{12... | collective-permute-start | bytes 638984 | tf_op jit(solution)/shard_map/ppermute | solution.py:307
  10.3 4.5 %collective-permute-start.1 = (bf16[208,512]{1,0:T(8,128)(2,1)S(1)}, bf16[208,512]{1,0:T(8,128)(2,1)S(1)}, u32[]{:S(2)}, u32[]{:S(2)}) collective-permute-start(bf16[208,512]{1,0:T(8,128)(2,1)S(1)} %bitcast.27), channel_id=1, source_target_pairs={{0,6},{2,0},{4,2},{6,4},{1,7},{3,1},{5,3},{7,5},{8,14},{10,8},{12,... | collective-permute-start | bytes 638984 | tf_op jit(solution)/shard_map/ppermute | solution.py:307
  14.9 1.9 %collective-permute-start = (bf16[208,512]{1,0:T(8,128)(2,1)S(1)}, bf16[208,512]{1,0:T(8,128)(2,1)S(1)}, u32[]{:S(2)}, u32[]{:S(2)}) collective-permute-start(bf16[208,512]{1,0:T(8,128)(2,1)S(1)} %bitcast.28), channel_id=1, source_target_pairs={{0,2},{2,4},{4,6},{6,0},{1,3},{3,5},{5,7},{7,1},{8,10},{10,12},{12... | collective-permute-start | bytes 638984 | tf_op jit(solution)/shard_map/ppermute | solution.py:307
  17.5 0.1 select_reduce_fusion.source_ref
  17.6 0.1 fusion.gain_ref
  17.7 1.5 %all-to-all-done.recv_ref = bf16[8,416,128]{2,1,0:T(8,128)(2,1)S(1)} async-done(((bf16[8,416,128]{2,1,0:T(8,128)(2,1)}), bf16[8,416,128]{2,1,0:T(8,128)(2,1)S(1)}, u32[]{:S(2)}, u32[]{:S(2)}) %all-to-all-start) | async-done | bytes 852000 | tf_op jit(solution)/shard_map/all_to_all | solution.py:348
  19.2 1.6 %sums.1 = f32[8,8,128]{2,1,0:T(8,128)} custom-call(s32[8]{0:T(128)S(1)} %select_reduce_fusion.source_ref, s32[8]{0:T(128)S(1)} %compare_convert_fusion.live_ref, bf16[8,416,128]{2,1,0:T(8,128)(2,1)S(1)} %all-to-all-done.recv_ref, f32[4,512]{1,0:T(4,128)S(1)} %fusion.gain_ref), custom_call_target="tpu_custom_call" | custom-call | tf_op jit(solution)/shard_map/sums/pallas_call | solution.py:367
  20.8 6.7 %all-to-all-start.1 = ((f32[8,8,128]{2,1,0:T(8,128)}), f32[8,8,128]{2,1,0:T(8,128)S(1)}, u32[]{:S(2)}, u32[]{:S(2)}) async-start(f32[8,8,128]{2,1,0:T(8,128)} %sums.1), calls=%async_computation.1 | async-start | bytes 65536 | tf_op jit(solution)/shard_map/all_to_all | solution.py:375
  27.5 0.0 collective-permute-done.2.far_ref
  27.5 1.4 %collective-permute-done.1.after_ref = bf16[208,512]{1,0:T(8,128)(2,1)S(1)} collective-permute-done((bf16[208,512]{1,0:T(8,128)(2,1)S(1)}, bf16[208,512]{1,0:T(8,128)(2,1)S(1)}, u32[]{:S(2)}, u32[]{:S(2)}) %collective-permute-start.1) | collective-permute-done | bytes 213024 | tf_op jit(solution)/shard_map/ppermute | solution.py:307
  29.0 0.0 collective-permute-done.before_ref
  29.0 1.0 pad_maximum_fusion.1
  30.0 0.6 all-to-all-done.1.sums_ref
  30.5 1.9 %collective-permute-start.3 = (bf16[4,208,512]{2,1,0:T(8,128)(2,1)}, bf16[4,208,512]{2,1,0:T(8,128)(2,1)S(1)}, u32[]{:S(2)}, u32[]{:S(2)}) collective-permute-start(bf16[4,208,512]{2,1,0:T(8,128)(2,1)} %pad_maximum_fusion.1), channel_id=1, source_target_pairs={{0,1},{1,0},{2,3},{3,2},{4,5},{5,4},{6,7},{7,6},{8,9},{9,8},{10,11... | collective-permute-start | bytes 2555912 | tf_op jit(solution)/shard_map/ppermute | solution.py:312
  32.5 0.1 broadcast_add_fusion
  32.6 0.1 pad_add_fusion.parts_ref
  32.7 0.1 fusion.1
  32.7 1.3 branch.1
  34.1 1.0 collective-permute-done.3.other_ref
  35.0 2.8 %terms.1 = bf16[8,688,128]{2,1,0:T(8,128)(2,1)} custom-call(s32[8]{0:T(128)S(1)} %pad_add_fusion.parts_ref, bf16[512,512]{1,0:T(8,128)(2,1)S(1)} %get-tuple-element.22.branch_ref, bf16[16,128]{1,0:T(8,128)(2,1)S(1)} %get-tuple-element.23.gain_ref, bf16[208,512]{1,0:T(8,128)(2,1)S(1)} %bitcast.30, bf16[208,512]{1,0:T(8,128)(2,1)S(1)} %collective-permute-done.before_ref, ...), custom_call_target="tpu_custom_call" | custom-call | tf_op jit(solution)/shard_map/terms/pallas_call | solution.py:390
  37.8 7.1 %all-to-all-start.2 = ((bf16[8,688,128]{2,1,0:T(8,128)(2,1)}), bf16[8,688,128]{2,1,0:T(8,128)(2,1)S(1)}, u32[]{:S(2)}, u32[]{:S(2)}) async-start(bf16[8,688,128]{2,1,0:T(8,128)(2,1)} %terms.1), calls=%async_computation.2 | async-start | bytes 2818048 | tf_op jit(solution)/shard_map/all_to_all | solution.py:399
  44.9 0.2 turn.1.own_ref
  45.1 4.4 %collective-permute-start.6 = (bf16[416,512]{1,0:T(8,128)(2,1)S(1)}, bf16[416,512]{1,0:T(8,128)(2,1)S(1)}, u32[]{:S(2)}, u32[]{:S(2)}) collective-permute-start(bf16[416,512]{1,0:T(8,128)(2,1)S(1)} %turn.1.own_ref), channel_id=1, source_target_pairs={{0,4},{2,6},{4,0},{6,2},{1,5},{3,7},{5,1},{7,3},{8,12},{10,14},{12... | collective-permute-start | bytes 1277960 | tf_op jit(solution)/shard_map/ppermute | solution.py:307
  49.4 2.5 %collective-permute-start.5 = (bf16[416,512]{1,0:T(8,128)(2,1)S(1)}, bf16[416,512]{1,0:T(8,128)(2,1)S(1)}, u32[]{:S(2)}, u32[]{:S(2)}) collective-permute-start(bf16[416,512]{1,0:T(8,128)(2,1)S(1)} %turn.1.own_ref), channel_id=1, source_target_pairs={{0,6},{2,0},{4,2},{6,4},{1,7},{3,1},{5,3},{7,5},{8,14},{10,8},{12,... | collective-permute-start | bytes 1277960 | tf_op jit(solution)/shard_map/ppermute | solution.py:307
  51.9 3.4 %collective-permute-start.4 = (bf16[416,512]{1,0:T(8,128)(2,1)S(1)}, bf16[416,512]{1,0:T(8,128)(2,1)S(1)}, u32[]{:S(2)}, u32[]{:S(2)}) collective-permute-start(bf16[416,512]{1,0:T(8,128)(2,1)S(1)} %turn.1.own_ref), channel_id=1, source_target_pairs={{0,2},{2,4},{4,6},{6,0},{1,3},{3,5},{5,7},{7,1},{8,10},{10,12},{12... | collective-permute-start | bytes 1277960 | tf_op jit(solution)/shard_map/ppermute | solution.py:307
  55.3 5.9 %collective-permute-done.6.far_ref = bf16[416,512]{1,0:T(8,128)(2,1)S(1)} collective-permute-done((bf16[416,512]{1,0:T(8,128)(2,1)S(1)}, bf16[416,512]{1,0:T(8,128)(2,1)S(1)}, u32[]{:S(2)}, u32[]{:S(2)}) %collective-permute-start.6) | collective-permute-done | bytes 426016 | tf_op jit(solution)/shard_map/ppermute | solution.py:307
  61.2 8.1 %collective-permute-done.5.after_ref = bf16[416,512]{1,0:T(8,128)(2,1)S(1)} collective-permute-done((bf16[416,512]{1,0:T(8,128)(2,1)S(1)}, bf16[416,512]{1,0:T(8,128)(2,1)S(1)}, u32[]{:S(2)}, u32[]{:S(2)}) %collective-permute-start.5) | collective-permute-done | bytes 426016 | tf_op jit(solution)/shard_map/ppermute | solution.py:307
  69.3 0.0 collective-permute-done.4.before_ref
  69.3 1.5 %pad_maximum_fusion = bf16[4,416,512]{2,1,0:T(8,128)(2,1)} fusion(bf16[1,416,512]{2,1,0:T(8,128)(2,1)S(1)} %bitcast.22, bf16[1,416,512]{2,1,0:T(8,128)(2,1)S(1)} %bitcast.23, bf16[1,416,512]{2,1,0:T(8,128)(2,1)S(1)} %bitcast.24, bf16[1,416,512]{2,1,0:T(8,128)(2,1)S(1)} %bitcast.21), kind=kLoop, calls=%fused_computation | loop fusion | flops 2555904 | bytes 3407872 | tf_op jit(solution)/shard_map/stack | solution.py:419
  70.8 1.9 %collective-permute-start.7 = (bf16[4,416,512]{2,1,0:T(8,128)(2,1)}, bf16[4,416,512]{2,1,0:T(8,128)(2,1)S(1)}, u32[]{:S(2)}, u32[]{:S(2)}) collective-permute-start(bf16[4,416,512]{2,1,0:T(8,128)(2,1)} %pad_maximum_fusion), channel_id=1, source_target_pairs={{0,1},{1,0},{2,3},{3,2},{4,5},{5,4},{6,7},{7,6},{8,9},{9,8},{10,11... | collective-permute-start | bytes 5111816 | tf_op jit(solution)/shard_map/ppermute | solution.py:312
  72.7 9.0 %all-to-all-done.2.recv_ref = bf16[8,688,128]{2,1,0:T(8,128)(2,1)S(1)} async-done(((bf16[8,688,128]{2,1,0:T(8,128)(2,1)}), bf16[8,688,128]{2,1,0:T(8,128)(2,1)S(1)}, u32[]{:S(2)}, u32[]{:S(2)}) %all-to-all-start.2) | async-done | bytes 1409056 | tf_op jit(solution)/shard_map/all_to_all | solution.py:399
  81.7 0.4 fold.1
  82.1 0.7 copy-done.7
  82.7 14.8 %all-to-all-start.3 = ((bf16[12,72,128]{2,1,0:T(8,128)(2,1)}), bf16[12,72,128]{2,1,0:T(8,128)(2,1)S(1)}, u32[]{:S(2)}, u32[]{:S(2)}) async-start(bf16[12,72,128]{2,1,0:T(8,128)(2,1)} %copy-done.7), calls=%async_computation.3 | async-start | bytes 442368 | tf_op jit(solution)/shard_map/all_to_all | solution.py:408
  97.5 0.7 broadcast_in_dim.44.scale_ref
  98.3 1.0 copy-done.1
  99.3 1.0 copy-done.3
  100.3 1.0 copy-done.5
  101.3 1.3 %copy-done.6 = bf16[3200,208]{0,1:T(8,128)(2,1)S(1)} copy-done((bf16[3200,208]{0,1:T(8,128)(2,1)S(1)}, bf16[3200,208]{0,1:T(8,128)(2,1)}, u32[]{:S(2)}) %copy-start.6) | copy-done | bytes 1331224
  102.6 2.7 %gathered.1 = (bf16[208,512]{1,0:T(8,128)(2,1)}, bf16[64,3200]{1,0:T(8,128)(2,1)}) custom-call(s32[1]{0:T(128)} %bitcast.12.tile_ref, s32[8]{0:T(128)S(1)} %pad_add_fusion.parts_ref, bf16[208,3200]{1,0:T(8,128)(2,1)S(1)} %bitcast.25, f32[1,3200]{1,0:T(1,128)S(1)} %broadcast_in_dim.44.scale_ref, bf16[416,512]{1,0:T(8,128)(2,1)S(1)} %turn.1.own_ref, ...), custom_call_target="tpu_custom_call" | custom-call | tf_op jit(solution)/shard_map/gathered/pallas_call | solution.py:420
  105.3 6.7 %all-to-all-done.3.recv_ref = bf16[12,72,128]{2,1,0:T(8,128)(2,1)S(1)} async-done(((bf16[12,72,128]{2,1,0:T(8,128)(2,1)}), bf16[12,72,128]{2,1,0:T(8,128)(2,1)S(1)}, u32[]{:S(2)}, u32[]{:S(2)}) %all-to-all-start.3) | async-done | bytes 221216 | tf_op jit(solution)/shard_map/all_to_all | solution.py:408
  112.0 0.2 settle.1
  112.2 3.3 %collective-permute-start.8 = (f32[64,256]{1,0:T(8,128)S(1)}, f32[64,256]{1,0:T(8,128)S(1)}, u32[]{:S(2)}, u32[]{:S(2)}) collective-permute-start(f32[64,256]{1,0:T(8,128)S(1)} %get-tuple-element.31), channel_id=1, source_target_pairs={{0,0},{1,96},{2,192},{3,288},{4,384},{5,480},{6,576},{7,672},{8,1}... | collective-permute-start | bytes 196616 | tf_op jit(solution)/shard_map/ppermute | solution.py:446
  115.5 8.1 %all_to_all.25.gain_ref = f32[8,16,128]{2,1,0:T(8,128)S(1)} all-to-all(f32[8,16,128]{2,1,0:T(8,128)S(1)} %get-tuple-element.30), channel_id=1, replica_groups=mesh['z'=12,'y'=8,'x'=4,'c'=2] {'x','c'}, dimensions={0} | all-to-all | bytes 131072 | tf_op jit(solution)/shard_map/all_to_all | solution.py:447
  123.6 6.8 %collective-permute-done.8.part_ref = f32[64,256]{1,0:T(8,128)S(1)} collective-permute-done((f32[64,256]{1,0:T(8,128)S(1)}, f32[64,256]{1,0:T(8,128)S(1)}, u32[]{:S(2)}, u32[]{:S(2)}) %collective-permute-start.8) | collective-permute-done | bytes 65568 | tf_op jit(solution)/shard_map/ppermute | solution.py:446
  130.4 0.8 spread.1
  (24 shorter events, 0.1 us)
Async XLA Ops:
  0.6 7.7 %copy-start.8 = (bf16[512,208]{0,1:T(8,128)(2,1)S(1)}, bf16[512,208]{0,1:T(8,128)(2,1)}, u32[]{:S(2)}) copy-start(bf16[512,208]{0,1:T(8,128)(2,1)} %param.14) | copy-start | bytes 638980
  0.6 16.8 %copy-start.10 = (f32[12800]{0:T(1024)S(1)}, f32[12800]{0:T(1024)}, u32[]{:S(2)}) copy-start(f32[12800]{0:T(1024)} %param.12) | copy-start | bytes 153604
  0.7 16.9 %copy-start.11 = (s32[1,8]{1,0:T(1,128)S(1)}, s32[1,8]{1,0:T(1,128)}, u32[]{:S(2)}) copy-start(s32[1,8]{1,0:T(1,128)} %param.10) | copy-start | bytes 100
  3.5 15.7 %all-to-all-start = ((bf16[8,416,128]{2,1,0:T(8,128)(2,1)}), bf16[8,416,128]{2,1,0:T(8,128)(2,1)S(1)}, u32[]{:S(2)}, u32[]{:S(2)}) async-start(bf16[8,416,128]{2,1,0:T(8,128)(2,1)} %cut.1), calls=%async_computation | async-start | bytes 1703936 | tf_op jit(solution)/shard_map/all_to_all | solution.py:348
  8.3 24.4 %copy-start.9 = (f32[3200]{0:T(1024)S(1)}, f32[3200]{0:T(1024)}, u32[]{:S(2)}) copy-start(f32[3200]{0:T(1024)} %param.13) | copy-start | bytes 38404
  8.3 19.2 %collective-permute-start.2 = (bf16[208,512]{1,0:T(8,128)(2,1)S(1)}, bf16[208,512]{1,0:T(8,128)(2,1)S(1)}, u32[]{:S(2)}, u32[]{:S(2)}) collective-permute-start(bf16[208,512]{1,0:T(8,128)(2,1)S(1)} %bitcast.26), channel_id=1, source_target_pairs={{0,4},{2,6},{4,0},{6,2},{1,5},{3,7},{5,1},{7,3},{8,12},{10,14},{12... | collective-permute-start | bytes 638984 | tf_op jit(solution)/shard_map/ppermute | solution.py:307
  10.3 18.6 %collective-permute-start.1 = (bf16[208,512]{1,0:T(8,128)(2,1)S(1)}, bf16[208,512]{1,0:T(8,128)(2,1)S(1)}, u32[]{:S(2)}, u32[]{:S(2)}) collective-permute-start(bf16[208,512]{1,0:T(8,128)(2,1)S(1)} %bitcast.27), channel_id=1, source_target_pairs={{0,6},{2,0},{4,2},{6,4},{1,7},{3,1},{5,3},{7,5},{8,14},{10,8},{12,... | collective-permute-start | bytes 638984 | tf_op jit(solution)/shard_map/ppermute | solution.py:307
  14.9 14.1 %collective-permute-start = (bf16[208,512]{1,0:T(8,128)(2,1)S(1)}, bf16[208,512]{1,0:T(8,128)(2,1)S(1)}, u32[]{:S(2)}, u32[]{:S(2)}) collective-permute-start(bf16[208,512]{1,0:T(8,128)(2,1)S(1)} %bitcast.28), channel_id=1, source_target_pairs={{0,2},{2,4},{4,6},{6,0},{1,3},{3,5},{5,7},{7,1},{8,10},{10,12},{12... | collective-permute-start | bytes 638984 | tf_op jit(solution)/shard_map/ppermute | solution.py:307
  20.8 9.7 %all-to-all-start.1 = ((f32[8,8,128]{2,1,0:T(8,128)}), f32[8,8,128]{2,1,0:T(8,128)S(1)}, u32[]{:S(2)}, u32[]{:S(2)}) async-start(f32[8,8,128]{2,1,0:T(8,128)} %sums.1), calls=%async_computation.1 | async-start | bytes 65536 | tf_op jit(solution)/shard_map/all_to_all | solution.py:375
  30.5 4.5 %collective-permute-start.3 = (bf16[4,208,512]{2,1,0:T(8,128)(2,1)}, bf16[4,208,512]{2,1,0:T(8,128)(2,1)S(1)}, u32[]{:S(2)}, u32[]{:S(2)}) collective-permute-start(bf16[4,208,512]{2,1,0:T(8,128)(2,1)} %pad_maximum_fusion.1), channel_id=1, source_target_pairs={{0,1},{1,0},{2,3},{3,2},{4,5},{5,4},{6,7},{7,6},{8,9},{9,8},{10,11... | collective-permute-start | bytes 2555912 | tf_op jit(solution)/shard_map/ppermute | solution.py:312
  37.8 43.9 %all-to-all-start.2 = ((bf16[8,688,128]{2,1,0:T(8,128)(2,1)}), bf16[8,688,128]{2,1,0:T(8,128)(2,1)S(1)}, u32[]{:S(2)}, u32[]{:S(2)}) async-start(bf16[8,688,128]{2,1,0:T(8,128)(2,1)} %terms.1), calls=%async_computation.2 | async-start | bytes 2818048 | tf_op jit(solution)/shard_map/all_to_all | solution.py:399
  45.1 16.1 %collective-permute-start.6 = (bf16[416,512]{1,0:T(8,128)(2,1)S(1)}, bf16[416,512]{1,0:T(8,128)(2,1)S(1)}, u32[]{:S(2)}, u32[]{:S(2)}) collective-permute-start(bf16[416,512]{1,0:T(8,128)(2,1)S(1)} %turn.1.own_ref), channel_id=1, source_target_pairs={{0,4},{2,6},{4,0},{6,2},{1,5},{3,7},{5,1},{7,3},{8,12},{10,14},{12... | collective-permute-start | bytes 1277960 | tf_op jit(solution)/shard_map/ppermute | solution.py:307
  49.4 19.9 %collective-permute-start.5 = (bf16[416,512]{1,0:T(8,128)(2,1)S(1)}, bf16[416,512]{1,0:T(8,128)(2,1)S(1)}, u32[]{:S(2)}, u32[]{:S(2)}) collective-permute-start(bf16[416,512]{1,0:T(8,128)(2,1)S(1)} %turn.1.own_ref), channel_id=1, source_target_pairs={{0,6},{2,0},{4,2},{6,4},{1,7},{3,1},{5,3},{7,5},{8,14},{10,8},{12,... | collective-permute-start | bytes 1277960 | tf_op jit(solution)/shard_map/ppermute | solution.py:307
  51.9 17.4 %collective-permute-start.4 = (bf16[416,512]{1,0:T(8,128)(2,1)S(1)}, bf16[416,512]{1,0:T(8,128)(2,1)S(1)}, u32[]{:S(2)}, u32[]{:S(2)}) collective-permute-start(bf16[416,512]{1,0:T(8,128)(2,1)S(1)} %turn.1.own_ref), channel_id=1, source_target_pairs={{0,2},{2,4},{4,6},{6,0},{1,3},{3,5},{5,7},{7,1},{8,10},{10,12},{12... | collective-permute-start | bytes 1277960 | tf_op jit(solution)/shard_map/ppermute | solution.py:307
  61.2 9.6 %copy-start = (bf16[416,512]{1,0:T(8,128)(2,1)}, bf16[416,512]{1,0:T(8,128)(2,1)S(1)}, u32[]{:S(2)}) copy-start(bf16[416,512]{1,0:T(8,128)(2,1)S(1)} %collective-permute-done.6.far_ref) | copy-start | bytes 1277956
  69.3 1.5 %copy-start.2 = (bf16[416,512]{1,0:T(8,128)(2,1)}, bf16[416,512]{1,0:T(8,128)(2,1)S(1)}, u32[]{:S(2)}) copy-start(bf16[416,512]{1,0:T(8,128)(2,1)S(1)} %collective-permute-done.5.after_ref) | copy-start | bytes 1277956
  69.3 1.5 %copy-start.4 = (bf16[416,512]{1,0:T(8,128)(2,1)}, bf16[416,512]{1,0:T(8,128)(2,1)S(1)}, u32[]{:S(2)}) copy-start(bf16[416,512]{1,0:T(8,128)(2,1)S(1)} %collective-permute-done.4.before_ref) | copy-start | bytes 1277956
  70.8 27.5 %collective-permute-start.7 = (bf16[4,416,512]{2,1,0:T(8,128)(2,1)}, bf16[4,416,512]{2,1,0:T(8,128)(2,1)S(1)}, u32[]{:S(2)}, u32[]{:S(2)}) collective-permute-start(bf16[4,416,512]{2,1,0:T(8,128)(2,1)} %pad_maximum_fusion), channel_id=1, source_target_pairs={{0,1},{1,0},{2,3},{3,2},{4,5},{5,4},{6,7},{7,6},{8,9},{9,8},{10,11... | collective-permute-start | bytes 5111816 | tf_op jit(solution)/shard_map/ppermute | solution.py:312
  82.1 0.7 copy-start.7
  82.7 29.3 %all-to-all-start.3 = ((bf16[12,72,128]{2,1,0:T(8,128)(2,1)}), bf16[12,72,128]{2,1,0:T(8,128)(2,1)S(1)}, u32[]{:S(2)}, u32[]{:S(2)}) async-start(bf16[12,72,128]{2,1,0:T(8,128)(2,1)} %copy-done.7), calls=%async_computation.3 | async-start | bytes 442368 | tf_op jit(solution)/shard_map/all_to_all | solution.py:408
  98.3 1.0 copy-start.1
  99.3 1.0 copy-start.3
  100.3 1.0 copy-start.5
  101.3 1.3 %copy-start.6 = (bf16[3200,208]{0,1:T(8,128)(2,1)S(1)}, bf16[3200,208]{0,1:T(8,128)(2,1)}, u32[]{:S(2)}) copy-start(bf16[3200,208]{0,1:T(8,128)(2,1)} %param.15) | copy-start | bytes 3993604
  112.2 18.2 %collective-permute-start.8 = (f32[64,256]{1,0:T(8,128)S(1)}, f32[64,256]{1,0:T(8,128)S(1)}, u32[]{:S(2)}, u32[]{:S(2)}) collective-permute-start(f32[64,256]{1,0:T(8,128)S(1)} %get-tuple-element.31), channel_id=1, source_target_pairs={{0,0},{1,96},{2,192},{3,288},{4,384},{5,480},{6,576},{7,672},{8,1}... | collective-permute-start | bytes 196616 | tf_op jit(solution)/shard_map/ppermute | solution.py:446
